TPU v7x, 128 devices: a whole 4x4x4 slice. The times are simulated.
128 devices in a mesh: dp: 32 (over x_lo, z, y), tensor: 4 (over x_hi, core).
Axes of the slice: x: 4 (x_hi: 2, x_lo: 2; x = x_hi * 2 + x_lo), y: 4, z: 4, core: 2. Of those that a mesh axis runs over, the one named last changes fastest.
Arguments:
- layer_input: bfloat16 [16384, 2048], P(('dp', 'tensor')), may hold values from -6 to 6
- teacher_out: bfloat16 [16384, 2048], P(('dp', 'tensor')), may hold values from -6 to 6
- lengths: int32 [32, 2], replicated, may hold values from 64 to 448, as said below
- norm1_gain: bfloat16 [2048], P('dp'), may hold values from 0.5 to 1.5
- query_weight: bfloat16 [2048, 1024], P('dp', 'tensor'), may hold values from -0.125 to 0.125
- key_weight: bfloat16 [2048, 1024], P('dp', 'tensor'), may hold values from -0.125 to 0.125
- value_weight: bfloat16 [2048, 2048], P('dp', 'tensor'), may hold values from -0.125 to 0.125
- output_gate: bfloat16 [2048, 2048], P('dp', 'tensor'), may hold values from -0.125 to 0.125
- beta_weight: bfloat16 [2048, 8], P('dp', 'tensor'), may hold values from -0.125 to 0.125
- decay_weight: bfloat16 [2048, 8], P('dp', 'tensor'), may hold values from -0.125 to 0.125
- decay_log: float32 [8], P('tensor'), may hold values from 0 to 2.7
- step_bias: float32 [8], P('tensor'), may hold values from -6 to -1
- query_taps: bfloat16 [4, 1024], P(None, 'tensor'), may hold values from -3 to 3
- key_taps: bfloat16 [4, 1024], P(None, 'tensor'), may hold values from -3 to 3
- value_taps: bfloat16 [4, 2048], P(None, 'tensor'), may hold values from -3 to 3
- mixer_gain: bfloat16 [256], replicated, may hold values from 0.5 to 1.5
- out_weight: bfloat16 [2048, 2048], P('dp', 'tensor'), may hold values from -0.125 to 0.125
- norm2_gain: bfloat16 [2048], P('dp'), may hold values from 0.5 to 1.5
- gate_weight: bfloat16 [2048, 5632], P('dp', 'tensor'), may hold values from -0.125 to 0.125
- up_weight: bfloat16 [2048, 5632], P('dp', 'tensor'), may hold values from -0.125 to 0.125
- down_weight: bfloat16 [2048, 5632], P('dp', 'tensor'), may hold values from -0.078125 to 0.078125
Outputs:
- layer_out: float32 [16384, 2048], P(('dp', 'tensor'))
- grad_input: float32 [16384, 2048], P(('dp', 'tensor'))
- grad_norm1_gain: float32 [2048], P('dp')
- grad_query_weight: float32 [2048, 1024], P('dp', 'tensor')
- grad_key_weight: float32 [2048, 1024], P('dp', 'tensor')
- grad_value_weight: float32 [2048, 2048], P('dp', 'tensor')
- grad_output_gate: float32 [2048, 2048], P('dp', 'tensor')
- grad_beta_weight: float32 [2048, 8], P('dp', 'tensor')
- grad_decay_weight: float32 [2048, 8], P('dp', 'tensor')
- grad_decay_log: float32 [8], P('tensor')
- grad_step_bias: float32 [8], P('tensor')
- grad_query_taps: float32 [4, 1024], P(None, 'tensor')
- grad_key_taps: float32 [4, 1024], P(None, 'tensor')
- grad_value_taps: float32 [4, 2048], P(None, 'tensor')
- grad_mixer_gain: float32 [256], replicated
- grad_out_weight: float32 [2048, 2048], P('dp', 'tensor')
- grad_norm2_gain: float32 [2048], P('dp')
- grad_gate_weight: float32 [2048, 5632], P('dp', 'tensor')
- grad_up_weight: float32 [2048, 5632], P('dp', 'tensor')
- grad_down_weight: float32 [2048, 5632], P('dp', 'tensor')
Inputs may be any that keep to these rules, and one draw needn't show every extreme that they name: Each group's lengths sum to at most 512; one of its two sequences, in a place drawn from the seed, starts within the group's first 128 positions and ends within its last 128.
All inputs are finite; a program needn't handle non-finite values.
Results may differ from a plain program's by a relative error of at most 0.025.
Values may be sent and summed in bfloat16 or wider, within the bound.
No kernel may reach another device: no remote copies, remote signals or barrier semaphores. Data moves between devices by JAX's collectives and lax.ppermute only.
A program may use at most 192 MiB of HBM per device.

v0:
```python
from functools import partial

import jax
import jax.numpy as jnp
from jax import lax
from jax.sharding import PartitionSpec as P

H = 8
DK = 128
DV = 256
CONV = 4
SPAN = 64


EPSILON = 1e-06
MIXER_FLOOR = 0.001
HIGHEST = lax.Precision.HIGHEST


def causal_conv(values, kernel_taps, seg_ids):
    taps_count = kernel_taps.shape[0]
    columns = values.shape[1]
    summed = values * kernel_taps[taps_count - 1][None, :]
    for offset in range(1, taps_count):
        moved = jnp.concatenate(
            [jnp.zeros((offset, columns), values.dtype), values[:-offset]], axis=0
        )
        earlier = jnp.concatenate([jnp.full((offset,), -1, jnp.int32), seg_ids[:-offset]], axis=0)
        matches = (earlier == seg_ids).astype(values.dtype)
        summed = summed + kernel_taps[taps_count - 1 - offset][None, :] * moved * matches[:, None]
    return jax.nn.silu(summed)


def unit_rows(values):
    return values * lax.rsqrt(jnp.sum(values * values, axis=-1, keepdims=True) + EPSILON)


def gated_norm(mixed_rows, gain, gate_rows):
    scaled = mixed_rows * lax.rsqrt(
        jnp.mean(mixed_rows * mixed_rows, axis=-1, keepdims=True) + MIXER_FLOOR
    )
    return scaled * gain * jax.nn.silu(gate_rows)


def block_step(state_now, inputs):
    query_block, key_block, value_block, beta_block, decay_block, seg_block, seg_prior = inputs
    length = seg_block.shape[0]
    row_index = lax.broadcasted_iota(jnp.int32, (length, length), 0)
    col_index = lax.broadcasted_iota(jnp.int32, (length, length), 1)
    causal = (seg_block[:, None] == seg_block[None, :]) & (col_index <= row_index)
    strict = causal & (col_index < row_index)
    cumulative = jnp.cumsum(decay_block, axis=-1)
    spread = jnp.where(causal[None], cumulative[:, :, None] - cumulative[:, None, :], 0.0)
    ratio = jnp.exp(spread) * causal[None].astype(jnp.float32)
    carry_in = (seg_block == seg_prior).astype(jnp.float32)
    growth = jnp.exp(cumulative) * carry_in[None, :]
    key_inner = jnp.einsum("hik,hjk->hij", key_block, key_block, precision=HIGHEST)
    lower_part = jnp.where(strict[None], beta_block[:, :, None] * ratio * key_inner, 0.0)
    recalled = jnp.einsum("hik,hvk->hiv", key_block, state_now, precision=HIGHEST)
    target_rows = beta_block[:, :, None] * (value_block - growth[:, :, None] * recalled)
    system = lower_part + jnp.eye(length, dtype=jnp.float32)[None]
    written = jax.scipy.linalg.solve_triangular(system, target_rows, lower=True, unit_diagonal=True)
    scores = jnp.einsum("hik,hjk->hij", query_block, key_block, precision=HIGHEST) * ratio
    outputs = growth[:, :, None] * jnp.einsum(
        "hik,hvk->hiv", query_block, state_now, precision=HIGHEST
    )
    outputs = outputs + jnp.einsum("hij,hjv->hiv", scores, written, precision=HIGHEST)
    fading = ratio[:, length - 1, :]
    new_state = growth[:, length - 1][:, None, None] * state_now
    new_state = new_state + jnp.einsum(
        "hjv,hjk->hvk", fading[:, :, None] * written, key_block, precision=HIGHEST
    )
    return (new_state, outputs)


def mixer_core(
    seg_ids,
    seg_before,
    query_raw,
    key_raw,
    value_raw,
    gate_raw,
    beta_raw,
    decay_raw,
    conv_query,
    conv_key,
    conv_value,
    decay_log,
    step_bias,
    mixer_gain,
):
    row_count = query_raw.shape[0]
    heads_here = decay_log.shape[0]
    blocks = row_count // SPAN
    queries = unit_rows(
        causal_conv(query_raw, conv_query, seg_ids).reshape(row_count, heads_here, DK)
    ) * DK ** (-0.5)
    keys_unit = unit_rows(
        causal_conv(key_raw, conv_key, seg_ids).reshape(row_count, heads_here, DK)
    )
    values = causal_conv(value_raw, conv_value, seg_ids).reshape(row_count, heads_here, DV)
    beta_rates = jax.nn.sigmoid(beta_raw)
    decays = -jnp.exp(decay_log)[None, :] * jax.nn.softplus(decay_raw + step_bias[None, :])

    def heads_first(member_array):
        return jnp.swapaxes(member_array.reshape((blocks, SPAN) + member_array.shape[1:]), 1, 2)

    seg_blocks = seg_ids.reshape(blocks, SPAN)
    initial = jnp.zeros((heads_here, DV, DK), jnp.float32)
    ignored, outputs = lax.scan(
        jax.checkpoint(block_step),
        initial,
        (
            heads_first(queries),
            heads_first(keys_unit),
            heads_first(values),
            heads_first(beta_rates),
            heads_first(decays),
            seg_blocks,
            seg_before,
        ),
    )
    mixed_rows = jnp.swapaxes(outputs, 1, 2).reshape(row_count, heads_here, DV)
    gated_rows = gated_norm(mixed_rows, mixer_gain, gate_raw.reshape(row_count, heads_here, DV))
    return gated_rows.reshape(row_count, heads_here * DV)


def shards(
    layer_input,
    teacher_out,
    lengths,
    norm1_gain,
    query_weight,
    key_weight,
    value_weight,
    output_gate,
    beta_weight,
    decay_weight,
    decay_log,
    step_bias,
    query_taps,
    key_taps,
    value_taps,
    mixer_gain,
    out_weight,
    norm2_gain,
    gate_weight,
    up_weight,
    down_weight,
):
    tok_rows = layer_input.shape[0]
    group_rows = tok_rows * lax.axis_size("tensor")
    all_rows = group_rows * lax.axis_size("dp")
    group_index = lax.axis_index("dp")
    tensor_index = lax.axis_index("tensor")
    heads_here = decay_log.shape[0]
    own_lengths = lax.dynamic_index_in_dim(lengths, group_index, 0, keepdims=False)
    boundary = jnp.cumsum(own_lengths)
    positions = jnp.arange(group_rows, dtype=jnp.int32)
    seg_ids = jnp.sum((positions[:, None] >= boundary[None, :]).astype(jnp.int32), axis=1)
    seg_before = jnp.concatenate([jnp.full((1,), -1, jnp.int32), seg_ids[SPAN - 1 : -1 : SPAN]])
    own_rows = tensor_index * tok_rows + jnp.arange(tok_rows, dtype=jnp.int32)
    validity = (own_rows < boundary[-1]).astype(jnp.float32)[:, None]
    loss_scale = jnp.float32(all_rows) / jnp.sum(lengths).astype(jnp.float32)
    gain_one, query_full, key_full, value_full, outgate_full, beta_full, decay_full, outw_full = (
        lax.all_gather(norm1_gain, "dp", axis=0, tiled=True),
        lax.all_gather(query_weight, "dp", axis=0, tiled=True),
        lax.all_gather(key_weight, "dp", axis=0, tiled=True),
        lax.all_gather(value_weight, "dp", axis=0, tiled=True),
        lax.all_gather(output_gate, "dp", axis=0, tiled=True),
        lax.all_gather(beta_weight, "dp", axis=0, tiled=True),
        lax.all_gather(decay_weight, "dp", axis=0, tiled=True),
        lax.all_gather(out_weight, "dp", axis=0, tiled=True),
    )
    input_float = layer_input.astype(jnp.float32)
    scale_one = lax.rsqrt(jnp.mean(input_float * input_float, axis=-1, keepdims=True) + EPSILON)
    gain_first = gain_one.astype(jnp.float32)
    normed_own = (input_float * scale_one * gain_first).astype(jnp.bfloat16)
    normed_one = lax.all_gather(normed_own, "tensor", axis=0, tiled=True)
    small_full = jnp.concatenate([beta_full, decay_full], axis=1)
    query_raw = jnp.dot(normed_one, query_full, preferred_element_type=jnp.float32)
    key_raw = jnp.dot(normed_one, key_full, preferred_element_type=jnp.float32)
    value_raw = jnp.dot(normed_one, value_full, preferred_element_type=jnp.float32)
    gate_raw = jnp.dot(normed_one, outgate_full, preferred_element_type=jnp.float32)
    small_raw = jnp.dot(normed_one, small_full, preferred_element_type=jnp.float32)
    beta_raw = small_raw[:, :heads_here]
    decay_raw = small_raw[:, heads_here:]
    taps_query = query_taps.astype(jnp.float32)
    taps_key = key_taps.astype(jnp.float32)
    taps_value = value_taps.astype(jnp.float32)
    gain_mixer = mixer_gain.astype(jnp.float32)
    core = partial(mixer_core, seg_ids, seg_before)
    gated_rows, pullback = jax.vjp(
        core,
        query_raw,
        key_raw,
        value_raw,
        gate_raw,
        beta_raw,
        decay_raw,
        taps_query,
        taps_key,
        taps_value,
        decay_log,
        step_bias,
        gain_mixer,
    )
    gated_low = gated_rows.astype(jnp.bfloat16)
    branch_terms = jnp.einsum("gv,dv->gd", gated_low, outw_full, preferred_element_type=jnp.float32)
    branch_one = lax.psum_scatter(
        branch_terms.astype(jnp.bfloat16), "tensor", scatter_dimension=0, tiled=True
    ).astype(jnp.float32)
    hidden = input_float + branch_one
    gain_two, gate_full, up_full, down_full = (
        lax.all_gather(norm2_gain, "dp", axis=0, tiled=True),
        lax.all_gather(gate_weight, "dp", axis=0, tiled=True),
        lax.all_gather(up_weight, "dp", axis=0, tiled=True),
        lax.all_gather(down_weight, "dp", axis=0, tiled=True),
    )
    gain_second = gain_two.astype(jnp.float32)
    scale_two = lax.rsqrt(jnp.mean(hidden * hidden, axis=-1, keepdims=True) + EPSILON)
    normed_two_own = (hidden * scale_two * gain_second).astype(jnp.bfloat16)
    normed_two = lax.all_gather(normed_two_own, "tensor", axis=0, tiled=True)
    gate_in = jnp.dot(normed_two, gate_full, preferred_element_type=jnp.float32)
    up_in = jnp.dot(normed_two, up_full, preferred_element_type=jnp.float32)
    sigma = jax.nn.sigmoid(gate_in)
    act_low = (gate_in * sigma * up_in).astype(jnp.bfloat16)
    ffn_terms = jnp.einsum("gf,df->gd", act_low, down_full, preferred_element_type=jnp.float32)
    branch_two = lax.psum_scatter(
        ffn_terms.astype(jnp.bfloat16), "tensor", scatter_dimension=0, tiled=True
    ).astype(jnp.float32)
    layer_out = hidden + branch_two
    grad_layer = loss_scale * validity * (layer_out - teacher_out.astype(jnp.float32))
    grad_branch_two = lax.all_gather(grad_layer.astype(jnp.bfloat16), "tensor", axis=0, tiled=True)
    grad_down = jnp.einsum(
        "gd,gf->df", grad_branch_two, act_low, preferred_element_type=jnp.float32
    )
    grad_act = jnp.dot(grad_branch_two, down_full, preferred_element_type=jnp.float32)
    grad_gate_in = (grad_act * up_in * sigma * (1.0 + gate_in * (1.0 - sigma))).astype(jnp.bfloat16)
    grad_up_in = (grad_act * gate_in * sigma).astype(jnp.bfloat16)
    grad_gate = jnp.einsum(
        "gd,gf->df", normed_two, grad_gate_in, preferred_element_type=jnp.float32
    )
    grad_up = jnp.einsum("gd,gf->df", normed_two, grad_up_in, preferred_element_type=jnp.float32)
    normed_terms = jnp.einsum(
        "gf,df->gd", grad_gate_in, gate_full, preferred_element_type=jnp.float32
    )
    normed_terms = normed_terms + jnp.einsum(
        "gf,df->gd", grad_up_in, up_full, preferred_element_type=jnp.float32
    )
    grad_normed_two = lax.psum_scatter(
        normed_terms.astype(jnp.bfloat16), "tensor", scatter_dimension=0, tiled=True
    ).astype(jnp.float32)
    ffn_grads = (
        lax.psum_scatter(
            grad_gate.astype(jnp.bfloat16), "dp", scatter_dimension=0, tiled=True
        ).astype(jnp.float32),
        lax.psum_scatter(
            grad_up.astype(jnp.bfloat16), "dp", scatter_dimension=0, tiled=True
        ).astype(jnp.float32),
        lax.psum_scatter(
            grad_down.astype(jnp.bfloat16), "dp", scatter_dimension=0, tiled=True
        ).astype(jnp.float32),
    )
    weighted_two = gain_second * grad_normed_two
    grad_gain_two = jnp.sum(grad_normed_two * hidden * scale_two, axis=0)
    grad_hidden = (
        grad_layer
        + scale_two * weighted_two
        - hidden
        * (scale_two * scale_two * scale_two)
        * jnp.mean(weighted_two * hidden, axis=-1, keepdims=True)
    )
    grad_branch_one = lax.all_gather(grad_hidden.astype(jnp.bfloat16), "tensor", axis=0, tiled=True)
    grad_outw = jnp.einsum(
        "gd,gv->dv", grad_branch_one, gated_low, preferred_element_type=jnp.float32
    )
    grad_gated = jnp.dot(grad_branch_one, outw_full, preferred_element_type=jnp.float32)
    (
        grad_query_raw,
        grad_key_raw,
        grad_value_raw,
        grad_gate_raw,
        grad_beta_raw,
        grad_decay_raw,
        grad_qtaps,
        grad_ktaps,
        grad_vtaps,
        grad_dlog,
        grad_bias,
        grad_mgain,
    ) = pullback(grad_gated)
    query_low = grad_query_raw.astype(jnp.bfloat16)
    key_low = grad_key_raw.astype(jnp.bfloat16)
    value_low = grad_value_raw.astype(jnp.bfloat16)
    outgate_low = grad_gate_raw.astype(jnp.bfloat16)
    small_low = jnp.concatenate([grad_beta_raw, grad_decay_raw], axis=1).astype(jnp.bfloat16)
    grad_query_w = jnp.einsum(
        "gd,gk->dk", normed_one, query_low, preferred_element_type=jnp.float32
    )
    grad_key_w = jnp.einsum("gd,gk->dk", normed_one, key_low, preferred_element_type=jnp.float32)
    grad_value_w = jnp.einsum(
        "gd,gk->dk", normed_one, value_low, preferred_element_type=jnp.float32
    )
    grad_outgate_w = jnp.einsum(
        "gd,gk->dk", normed_one, outgate_low, preferred_element_type=jnp.float32
    )
    grad_small_w = jnp.einsum(
        "gd,gk->dk", normed_one, small_low, preferred_element_type=jnp.float32
    )
    first_terms = jnp.einsum("gk,dk->gd", query_low, query_full, preferred_element_type=jnp.float32)
    first_terms = first_terms + jnp.einsum(
        "gk,dk->gd", key_low, key_full, preferred_element_type=jnp.float32
    )
    first_terms = first_terms + jnp.einsum(
        "gk,dk->gd", value_low, value_full, preferred_element_type=jnp.float32
    )
    first_terms = first_terms + jnp.einsum(
        "gk,dk->gd", outgate_low, outgate_full, preferred_element_type=jnp.float32
    )
    first_terms = first_terms + jnp.einsum(
        "gk,dk->gd", small_low, small_full, preferred_element_type=jnp.float32
    )
    grad_normed_one = lax.psum_scatter(
        first_terms.astype(jnp.bfloat16), "tensor", scatter_dimension=0, tiled=True
    ).astype(jnp.float32)
    weighted_one = gain_first * grad_normed_one
    grad_gain_one = jnp.sum(grad_normed_one * input_float * scale_one, axis=0)
    grad_input = (
        grad_hidden
        + scale_one * weighted_one
        - input_float
        * (scale_one * scale_one * scale_one)
        * jnp.mean(weighted_one * input_float, axis=-1, keepdims=True)
    )
    attn_grads = (
        lax.psum_scatter(
            grad_query_w.astype(jnp.bfloat16), "dp", scatter_dimension=0, tiled=True
        ).astype(jnp.float32),
        lax.psum_scatter(
            grad_key_w.astype(jnp.bfloat16), "dp", scatter_dimension=0, tiled=True
        ).astype(jnp.float32),
        lax.psum_scatter(
            grad_value_w.astype(jnp.bfloat16), "dp", scatter_dimension=0, tiled=True
        ).astype(jnp.float32),
        lax.psum_scatter(
            grad_outgate_w.astype(jnp.bfloat16), "dp", scatter_dimension=0, tiled=True
        ).astype(jnp.float32),
        lax.psum_scatter(
            grad_small_w.astype(jnp.bfloat16), "dp", scatter_dimension=0, tiled=True
        ).astype(jnp.float32),
        lax.psum_scatter(
            grad_outw.astype(jnp.bfloat16), "dp", scatter_dimension=0, tiled=True
        ).astype(jnp.float32),
    )
    zero_index = jnp.zeros((), jnp.int32)
    head_start = tensor_index * heads_here
    qk_width = query_taps.shape[1]
    v_width = value_taps.shape[1]
    dlog_full = lax.dynamic_update_slice(jnp.zeros((H,), jnp.float32), grad_dlog, (head_start,))
    bias_full = lax.dynamic_update_slice(jnp.zeros((H,), jnp.float32), grad_bias, (head_start,))
    qtaps_full = lax.dynamic_update_slice(
        jnp.zeros((CONV, H * DK), jnp.float32), grad_qtaps, (zero_index, tensor_index * qk_width)
    )
    ktaps_full = lax.dynamic_update_slice(
        jnp.zeros((CONV, H * DK), jnp.float32), grad_ktaps, (zero_index, tensor_index * qk_width)
    )
    vtaps_full = lax.dynamic_update_slice(
        jnp.zeros((CONV, H * DV), jnp.float32), grad_vtaps, (zero_index, tensor_index * v_width)
    )
    summed = lax.psum(
        (
            grad_gain_one,
            grad_gain_two,
            dlog_full,
            bias_full,
            qtaps_full,
            ktaps_full,
            vtaps_full,
            grad_mgain,
        ),
        ("dp", "tensor"),
    )
    rows_dp = norm1_gain.shape[0]
    grad_norm1 = lax.dynamic_slice_in_dim(summed[0], group_index * rows_dp, rows_dp)
    grad_norm2 = lax.dynamic_slice_in_dim(summed[1], group_index * rows_dp, rows_dp)
    grad_decay_log = lax.dynamic_slice_in_dim(summed[2], head_start, heads_here)
    grad_step_bias = lax.dynamic_slice_in_dim(summed[3], head_start, heads_here)
    grad_query_taps = lax.dynamic_slice_in_dim(summed[4], tensor_index * qk_width, qk_width, axis=1)
    grad_key_taps = lax.dynamic_slice_in_dim(summed[5], tensor_index * qk_width, qk_width, axis=1)
    grad_value_taps = lax.dynamic_slice_in_dim(summed[6], tensor_index * v_width, v_width, axis=1)
    small_sum = attn_grads[4]
    return (
        layer_out,
        grad_input,
        grad_norm1,
        attn_grads[0],
        attn_grads[1],
        attn_grads[2],
        attn_grads[3],
        small_sum[:, :heads_here],
        small_sum[:, heads_here:],
        grad_decay_log,
        grad_step_bias,
        grad_query_taps,
        grad_key_taps,
        grad_value_taps,
        summed[7],
        attn_grads[5],
        grad_norm2,
        ffn_grads[0],
        ffn_grads[1],
        ffn_grads[2],
    )


def solution(mesh):
    in_specs = (
        P(("dp", "tensor"), None),
        P(("dp", "tensor"), None),
        P(),
        P("dp"),
        P("dp", "tensor"),
        P("dp", "tensor"),
        P("dp", "tensor"),
        P("dp", "tensor"),
        P("dp", "tensor"),
        P("dp", "tensor"),
        P("tensor"),
        P("tensor"),
        P(None, "tensor"),
        P(None, "tensor"),
        P(None, "tensor"),
        P(),
        P("dp", "tensor"),
        P("dp"),
        P("dp", "tensor"),
        P("dp", "tensor"),
        P("dp", "tensor"),
    )
    out_specs = (
        P(("dp", "tensor"), None),
        P(("dp", "tensor"), None),
        P("dp"),
        P("dp", "tensor"),
        P("dp", "tensor"),
        P("dp", "tensor"),
        P("dp", "tensor"),
        P("dp", "tensor"),
        P("dp", "tensor"),
        P("tensor"),
        P("tensor"),
        P(None, "tensor"),
        P(None, "tensor"),
        P(None, "tensor"),
        P(),
        P("dp", "tensor"),
        P("dp"),
        P("dp", "tensor"),
        P("dp", "tensor"),
        P("dp", "tensor"),
    )
    return jax.shard_map(shards, mesh=mesh, in_specs=in_specs, out_specs=out_specs, check_vma=False)
```

profile of v0, /device:TPU:0, one launch (start us, length us, event | category | flops | bytes accessed | tf_op | source)
XLA Modules:
  0.0 3638.4 jit_solution(457464479483530772)
XLA Ops:
  10.9 85.4 %all-reduce.37 = (bf16[2048]{0:T(1024)(128)(2,1)S(1)}, bf16[2048]{0:T(1024)(128)(2,1)S(1)}) all-reduce(bf16[2048]{0:T(1024)(128)(2,1)S(1)} %dynamic-update-slice, bf16[2048]{0:T(1024)(128)(2,1)S(1)} %dynamic-update-slice.1), channel_id=1, replica_groups=mesh['dp'=32,'tensor'=4] {'dp'}, use_global_device_ids=true, to_apply=%add.34 | all-reduce | flops 4096 | bytes 16384
  104.8 74.9 %all-gather.1 = bf16[32,64,2]{1,2,0:T(2,128)(2,1)S(1)} all-gather(bf16[1,64,2]{1,2,0:T(2,128)(2,1)S(1)} %bitcast.526), channel_id=1, replica_groups=mesh['dp'=32,'tensor'=4] {'dp'}, dimensions={0}, use_global_device_ids=true | all-gather | bytes 8448 | tf_op jit(solution)/shard_map/all_gather | solution.py:172
  179.7 76.8 %all-gather = bf16[32,64,2]{1,2,0:T(2,128)(2,1)S(1)} all-gather(bf16[1,64,2]{1,2,0:T(2,128)(2,1)S(1)} %bitcast.527), channel_id=1, replica_groups=mesh['dp'=32,'tensor'=4] {'dp'}, dimensions={0}, use_global_device_ids=true | all-gather | bytes 8448 | tf_op jit(solution)/shard_map/all_gather | solution.py:171
  260.7 14.5 all-gather.21.cloned.1.call-done
  277.8 150.3 %all-gather.17.cloned.1.call-done = bf16[2048,256]{1,0:T(8,128)(2,1)} async-done(((bf16[64,256]{1,0:T(8,128)(2,1)}), bf16[2048,256]{1,0:T(8,128)(2,1)}) %all-gather.17.cloned.1.call-update) | async-done | bytes 1048592 | tf_op jit(solution)/shard_map/all_gather | solution.py:168
  441.5 141.8 %all-gather.19.cloned.1.call-done = bf16[2048,512]{1,0:T(8,128)(2,1)} async-done(((bf16[64,512]{1,0:T(8,128)(2,1)}), bf16[2048,512]{1,0:T(8,128)(2,1)}) %all-gather.19.cloned.1.call-update) | async-done | bytes 2097168 | tf_op jit(solution)/shard_map/all_gather | solution.py:169
  595.1 168.4 %while.42 = (s32[]{:T(128)}, f32[2,256,128]{2,1,0:T(8,128)S(1)}, f32[8,2,64,256]{3,2,1,0:T(8,128)}, f32[8,2,256,128]{3,2,1,0:T(8,128)}, f32[8,2,64]{2,1,0:T(2,12...) while((s32[]{:T(128)}, f32[2,256,128]{2,1,0:T(8,128)S(1)}, ...), condition=%wide.region_7.9_spmd.clone, body=%wide.region_5.8_spmd.clone.sunk | while | flops 227266752 | bytes 3575005 | solution.py:110
  774.0 121.1 %all-gather.25.cloned.1.call-done = bf16[2048,512]{1,0:T(8,128)(2,1)} async-done(((bf16[64,512]{1,0:T(8,128)(2,1)}), bf16[2048,512]{1,0:T(8,128)(2,1)}) %all-gather.25.cloned.1.call-update) | async-done | bytes 2097168 | tf_op jit(solution)/shard_map/all_gather | solution.py:173
  900.1 37.5 %reduce-scatter.16.cloned.1.call-done = bf16[128,2048]{1,0:T(8,128)(2,1)} async-done(((bf16[512,2048]{1,0:T(8,128)(2,1)}), bf16[128,2048]{1,0:T(8,128)(2,1)}) %reduce-scatter.16.cloned.1.call-update) | async-done | bytes 524304 | tf_op jit(solution)/shard_map/reduce_scatter | solution.py:210
  942.3 158.3 %all-gather.29.cloned.1.call-done = bf16[2048,1408]{1,0:T(8,128)(2,1)} async-done(((bf16[64,1408]{1,0:T(8,128)(2,1)}), bf16[2048,1408]{1,0:T(8,128)(2,1)}) %all-gather.29.cloned.1.call-update) | async-done | bytes 5767184 | tf_op jit(solution)/shard_map/all_gather | solution.py:216
  1100.6 29.7 all-gather.27.cloned.1.call-done
  1138.5 154.6 %all-gather.31.cloned.1.call-done = bf16[2048,1408]{1,0:T(8,128)(2,1)} async-done(((bf16[64,1408]{1,0:T(8,128)(2,1)}), bf16[2048,1408]{1,0:T(8,128)(2,1)}) %all-gather.31.cloned.1.call-update) | async-done | bytes 5767184 | tf_op jit(solution)/shard_map/all_gather | solution.py:217
  1302.7 154.6 %all-gather.33.cloned.1.call-done = bf16[2048,1408]{1,0:T(8,128)(2,1)} async-done(((bf16[64,1408]{1,0:T(8,128)(2,1)}), bf16[2048,1408]{1,0:T(8,128)(2,1)}) %all-gather.33.cloned.1.call-update) | async-done | bytes 5767184 | tf_op jit(solution)/shard_map/all_gather | solution.py:218
  1467.8 36.5 %reduce-scatter.18.cloned.1.call-done = bf16[128,2048]{1,0:T(8,128)(2,1)} async-done(((bf16[512,2048]{1,0:T(8,128)(2,1)}), bf16[128,2048]{1,0:T(8,128)(2,1)}) %reduce-scatter.18.cloned.1.call-update) | async-done | bytes 524304 | tf_op jit(solution)/shard_map/reduce_scatter | solution.py:229
  1507.5 25.8 all-gather.35.cloned.1.call-done
  1556.2 37.9 %reduce-scatter.20.cloned.1.call-done = bf16[128,2048]{1,0:T(8,128)(2,1)} async-done(((bf16[512,2048]{1,0:T(8,128)(2,1)}), bf16[128,2048]{1,0:T(8,128)(2,1)}) %reduce-scatter.20.cloned.1.call-update) | async-done | bytes 524304 | tf_op jit(solution)/shard_map/reduce_scatter | solution.py:251
  1606.2 19.1 all-gather.37.cloned.1.call-done
  1642.4 292.3 %while.43 = (s32[]{:T(128)}, f32[2,256,128]{2,1,0:T(8,128)}, f32[8,2,64,128]{3,2,1,0:T(8,128)}, f32[8,2,64,128]{3,2,1,0:T(8,128)}, f32[8,2,64,256]{3,2,1,0:T(8,1...) while((s32[]{:T(128)}, f32[2,256,128]{2,1,0:T(8,128)}, ...), condition=%wide.region_27.29_spmd.clone, body=%wide.region_16.28_spmd.clone.sunk | while | flops 612094144 | bytes 13472583 | solution.py:110
  1654.1 11.2 custom-call.26
  1690.7 11.2 custom-call.26
  1727.3 11.2 custom-call.26
  2023.4 95.5 %reduce-scatter.40.cloned.1.call-done = bf16[64,4]{1,0:T(8,128)(2,1)} async-done(((bf16[2048,4]{1,0:T(8,128)(2,1)}), bf16[64,4]{1,0:T(8,128)(2,1)}) %reduce-scatter.40.cloned.1.call-update) | async-done | bytes 528
  2120.3 158.6 %reduce-scatter.24.cloned.1.call-done = bf16[64,256]{1,0:T(8,128)(2,1)} async-done(((bf16[2048,256]{1,0:T(8,128)(2,1)}), bf16[64,256]{1,0:T(8,128)(2,1)}) %reduce-scatter.24.cloned.1.call-update) | async-done | bytes 32784 | tf_op jit(solution)/shard_map/reduce_scatter | solution.py:337
  2280.2 158.1 %reduce-scatter.26.cloned.1.call-done = bf16[64,256]{1,0:T(8,128)(2,1)} async-done(((bf16[2048,256]{1,0:T(8,128)(2,1)}), bf16[64,256]{1,0:T(8,128)(2,1)}) %reduce-scatter.26.cloned.1.call-update) | async-done | bytes 32784 | tf_op jit(solution)/shard_map/reduce_scatter | solution.py:340
  2439.8 35.9 reduce-scatter.22.cloned.1.call-done
  2480.0 160.9 %reduce-scatter.28.cloned.1.call-done = bf16[64,512]{1,0:T(8,128)(2,1)} async-done(((bf16[2048,512]{1,0:T(8,128)(2,1)}), bf16[64,512]{1,0:T(8,128)(2,1)}) %reduce-scatter.28.cloned.1.call-update) | async-done | bytes 65552 | tf_op jit(solution)/shard_map/reduce_scatter | solution.py:343
  2642.4 160.5 %reduce-scatter.30.cloned.1.call-done = bf16[64,512]{1,0:T(8,128)(2,1)} async-done(((bf16[2048,512]{1,0:T(8,128)(2,1)}), bf16[64,512]{1,0:T(8,128)(2,1)}) %reduce-scatter.30.cloned.1.call-update) | async-done | bytes 65552 | tf_op jit(solution)/shard_map/reduce_scatter | solution.py:346
  2804.5 160.9 %reduce-scatter.32.cloned.1.call-done = bf16[64,512]{1,0:T(8,128)(2,1)} async-done(((bf16[2048,512]{1,0:T(8,128)(2,1)}), bf16[64,512]{1,0:T(8,128)(2,1)}) %reduce-scatter.32.cloned.1.call-update) | async-done | bytes 65552 | tf_op jit(solution)/shard_map/reduce_scatter | solution.py:352
  2966.8 170.2 %reduce-scatter.34.cloned.1.call-done = bf16[64,1408]{1,0:T(8,128)(2,1)} async-done(((bf16[2048,1408]{1,0:T(8,128)(2,1)}), bf16[64,1408]{1,0:T(8,128)(2,1)}) %reduce-scatter.34.cloned.1.call-update) | async-done | bytes 180240 | tf_op jit(solution)/shard_map/reduce_scatter | solution.py:255
  3138.7 169.4 %reduce-scatter.36.cloned.1.call-done = bf16[64,1408]{1,0:T(8,128)(2,1)} async-done(((bf16[2048,1408]{1,0:T(8,128)(2,1)}), bf16[64,1408]{1,0:T(8,128)(2,1)}) %reduce-scatter.36.cloned.1.call-update) | async-done | bytes 180240 | tf_op jit(solution)/shard_map/reduce_scatter | solution.py:258
  3309.8 169.8 %reduce-scatter.38.cloned.1.call-done = bf16[64,1408]{1,0:T(8,128)(2,1)} async-done(((bf16[2048,1408]{1,0:T(8,128)(2,1)}), bf16[64,1408]{1,0:T(8,128)(2,1)}) %reduce-scatter.38.cloned.1.call-update) | async-done | bytes 180240 | tf_op jit(solution)/shard_map/reduce_scatter | solution.py:261
  3481.3 140.2 %all-reduce.40.cloned.1.call-done = (f32[2048]{0:T(1024)}, f32[8]{0:T(128)}, f32[8]{0:T(128)}, f32[4,1024]{1,0:T(4,128)}, f32[4,1024]{1,0:T(4,128)}, /*index=5*/f32[4,2048]{1,0:T(4,128)}, f32[256]{0:T(256)}, f32[2048]{0:T(1024)}) async-done(((f32[2048]{0:T(1024)}, f32[8]{0:T(128)}, f32[8]{0:T(128)}, f32[4,1024]{1,0:T(4,128)}, f32[4,1024]{1,0:T(4,128)}, /*index=5*/f32[4,2048]{1,0:T(4,128)}, f32[256]{0:T(256)}, ...) | async-done | bytes 83024 | tf_op jit(solution)/shard_map/psum | solution.py:371
  (1126 shorter events, 685.9 us)
Async XLA Ops:
  7.3 250.3 %all-gather.15.cloned.1.call-start = ((), (), s32[]{:S(2)}) async-start(), calls=%async_computation.13 | async-start | bytes 2621440 | tf_op jit(solution)/shard_map/all_gather | solution.py:179
  100.1 175.0 %all-gather.21.cloned.1.call-start = ((), (), s32[]{:S(2)}) async-start(), calls=%async_computation.16 | async-start | bytes 1081344 | tf_op jit(solution)/shard_map/all_gather | solution.py:167
  100.9 327.2 %all-gather.17.cloned.1.call-start = ((), (), s32[]{:S(2)}) async-start(), calls=%async_computation.14 | async-start | bytes 1081344 | tf_op jit(solution)/shard_map/all_gather | solution.py:168
  101.6 481.6 %all-gather.19.cloned.1.call-start = ((), (), s32[]{:S(2)}) async-start(), calls=%async_computation.15 | async-start | bytes 2162688 | tf_op jit(solution)/shard_map/all_gather | solution.py:169
  102.2 666.6 %all-gather.23.cloned.1.call-start = ((), (), s32[]{:S(2)}) async-start(), calls=%async_computation.17 | async-start | bytes 2162688 | tf_op jit(solution)/shard_map/all_gather | solution.py:170
  102.8 792.2 %all-gather.25.cloned.1.call-start = ((), (), s32[]{:S(2)}) async-start(), calls=%async_computation.18 | async-start | bytes 2162688 | tf_op jit(solution)/shard_map/all_gather | solution.py:173
  103.4 834.2 %reduce-scatter.16.cloned.1.call-start = ((), (), s32[]{:S(2)}) async-start(), calls=%async_computation.19 | async-start | bytes 2621440 | tf_op jit(solution)/shard_map/reduce_scatter | solution.py:210
  899.2 201.3 %all-gather.29.cloned.1.call-start = ((), (), s32[]{:S(2)}) async-start(), calls=%async_computation.21 | async-start | bytes 5947392 | tf_op jit(solution)/shard_map/all_gather | solution.py:216
  900.0 230.2 %all-gather.27.cloned.1.call-start = ((), (), s32[]{:S(2)}) async-start(), calls=%async_computation.20 | async-start | bytes 2621440 | tf_op jit(solution)/shard_map/all_gather | solution.py:223
  940.9 352.2 %all-gather.31.cloned.1.call-start = ((), (), s32[]{:S(2)}) async-start(), calls=%async_computation.22 | async-start | bytes 5947392 | tf_op jit(solution)/shard_map/all_gather | solution.py:217
  941.5 515.8 %all-gather.33.cloned.1.call-start = ((), (), s32[]{:S(2)}) async-start(), calls=%async_computation.23 | async-start | bytes 5947392 | tf_op jit(solution)/shard_map/all_gather | solution.py:218
  942.2 562.1 %reduce-scatter.18.cloned.1.call-start = ((), (), s32[]{:S(2)}) async-start(), calls=%async_computation.24 | async-start | bytes 2621440 | tf_op jit(solution)/shard_map/reduce_scatter | solution.py:229
  1465.2 68.1 %all-gather.35.cloned.1.call-start = ((), (), s32[]{:S(2)}) async-start(), calls=%async_computation.25 | async-start | bytes 2621440 | tf_op jit(solution)/shard_map/all_gather | solution.py:234
  1507.1 87.0 %reduce-scatter.20.cloned.1.call-start = ((), (), s32[]{:S(2)}) async-start(), calls=%async_computation.26 | async-start | bytes 2621440 | tf_op jit(solution)/shard_map/reduce_scatter | solution.py:251
  1556.1 69.2 %all-gather.37.cloned.1.call-start = ((), (), s32[]{:S(2)}) async-start(), calls=%async_computation.27 | async-start | bytes 2621440 | tf_op jit(solution)/shard_map/all_gather | solution.py:274
  1599.1 519.8 %reduce-scatter.40.cloned.1.call-start = ((), (), s32[]{:S(2)}) async-start(), calls=%async_computation.37 | async-start | bytes 540672
  1959.2 319.7 %reduce-scatter.24.cloned.1.call-start = ((), (), s32[]{:S(2)}) async-start(), calls=%async_computation.29 | async-start | bytes 1081344 | tf_op jit(solution)/shard_map/reduce_scatter | solution.py:337
  1965.6 472.8 %reduce-scatter.26.cloned.1.call-start = ((), (), s32[]{:S(2)}) async-start(), calls=%async_computation.30 | async-start | bytes 1081344 | tf_op jit(solution)/shard_map/reduce_scatter | solution.py:340
  1975.7 499.9 %reduce-scatter.22.cloned.1.call-start = ((), (), s32[]{:S(2)}) async-start(), calls=%async_computation.28 | async-start | bytes 2621440 | tf_op jit(solution)/shard_map/reduce_scatter | solution.py:324
  1986.4 654.6 %reduce-scatter.28.cloned.1.call-start = ((), (), s32[]{:S(2)}) async-start(), calls=%async_computation.31 | async-start | bytes 2162688 | tf_op jit(solution)/shard_map/reduce_scatter | solution.py:343
  1990.6 812.4 %reduce-scatter.30.cloned.1.call-start = ((), (), s32[]{:S(2)}) async-start(), calls=%async_computation.32 | async-start | bytes 2162688 | tf_op jit(solution)/shard_map/reduce_scatter | solution.py:346
  1994.2 971.1 %reduce-scatter.32.cloned.1.call-start = ((), (), s32[]{:S(2)}) async-start(), calls=%async_computation.33 | async-start | bytes 2162688 | tf_op jit(solution)/shard_map/reduce_scatter | solution.py:352
  1999.5 1137.5 %reduce-scatter.34.cloned.1.call-start = ((), (), s32[]{:S(2)}) async-start(), calls=%async_computation.34 | async-start | bytes 5947392 | tf_op jit(solution)/shard_map/reduce_scatter | solution.py:255
  2007.7 1300.3 %reduce-scatter.36.cloned.1.call-start = ((), (), s32[]{:S(2)}) async-start(), calls=%async_computation.35 | async-start | bytes 5947392 | tf_op jit(solution)/shard_map/reduce_scatter | solution.py:258
  2014.4 1465.2 %reduce-scatter.38.cloned.1.call-start = ((), (), s32[]{:S(2)}) async-start(), calls=%async_computation.36 | async-start | bytes 5947392 | tf_op jit(solution)/shard_map/reduce_scatter | solution.py:261
  2022.6 455.1 %copy-start.100 = (f32[128]{0:T(128)S(1)}, f32[128]{0:T(128)}, u32[]{:S(2)}) copy-start(f32[128]{0:T(128)} %get-tuple-element.900) | copy-start | bytes 1540
  2022.6 455.0 %copy-start.25 = (f32[128,2048]{1,0:T(8,128)S(1)}, f32[128,2048]{1,0:T(8,128)}, u32[]{:S(2)}) copy-start(f32[128,2048]{1,0:T(8,128)} %get-tuple-element.820) | copy-start | bytes 3145732
  2022.7 1598.9 %all-reduce.40.cloned.1.call-start = ((), (), s32[]{:S(2)}) async-start(), calls=%async_computation.38 | async-start | bytes 167936 | tf_op jit(solution)/shard_map/psum | solution.py:371
  2023.0 454.6 %copy-start.102 = (f32[8]{0:T(128)}, f32[8]{0:T(128)S(1)}, u32[]{:S(2)}) copy-start(f32[8]{0:T(128)S(1)} %dynamic_update_slice.77) | copy-start | bytes 100
  2023.0 454.6 %copy-start.45 = (f32[4,1024]{1,0:T(4,128)}, f32[4,1024]{1,0:T(4,128)S(1)}, u32[]{:S(2)}) copy-start(f32[4,1024]{1,0:T(4,128)S(1)} %add_dynamic-update-slice_fusion.2) | copy-start | bytes 49156
  2023.0 454.6 %copy-start.46 = (f32[4,1024]{1,0:T(4,128)}, f32[4,1024]{1,0:T(4,128)S(1)}, u32[]{:S(2)}) copy-start(f32[4,1024]{1,0:T(4,128)S(1)} %add_dynamic-update-slice_fusion.1) | copy-start | bytes 49156
  2023.1 454.5 %copy-start.40 = (f32[4,2048]{1,0:T(4,128)}, f32[4,2048]{1,0:T(4,128)S(1)}, u32[]{:S(2)}) copy-start(f32[4,2048]{1,0:T(4,128)S(1)} %add_dynamic-update-slice_fusion) | copy-start | bytes 98308
  (171 other events, 7833.1 us)
Sparse Core Ops, SparseCore 0:
  100.3 22.7 all-gather.14
  124.7 150.4 all-gather.20
  276.8 151.2 all-gather.16
  429.6 153.5 all-gather.18
  584.7 154.2 all-gather.22
  740.5 154.4 all-gather.24
  899.4 38.1 reduce-scatter.15
  939.3 161.2 all-gather.28
  1102.9 27.2 all-gather.26
  1131.8 161.2 all-gather.30
  1294.8 162.4 all-gather.32
  1465.3 38.9 reduce-scatter.17
  1507.2 26.0 all-gather.34
  1556.3 37.7 reduce-scatter.19
  1599.2 26.0 all-gather.36
  1959.3 159.5 reduce-scatter.39
  2121.1 157.6 reduce-scatter.23
  2281.2 157.1 reduce-scatter.25
  2441.0 34.5 reduce-scatter.21
  2478.0 162.9 reduce-scatter.27
  2643.3 159.6 reduce-scatter.29
  2805.4 159.8 reduce-scatter.31
  2967.7 169.2 reduce-scatter.33
  3139.3 168.7 reduce-scatter.35
  3310.5 169.0 reduce-scatter.37
  3486.5 134.9 all-reduce.39
where the time goes:
time: 3650 us; the launch traced here: 3640 us
  waiting for transfers between devices  2670 us (73%)
  other arithmetic  286 us (8%)
  matrix products  274 us (8%)
  blocking collectives  237 us (6%)
  local copies, waits for them, and re-layouts  152 us (4%)
    another operation x64, other arithmetic, block_step(): jax.scipy.linalg.solve_triangular(system, target_rows, lower=True, unit_d...  175 us
    reduce_scatter x1, waiting for transfers between devices, shards(): lax.psum_scatter(grad_gate.astype(jnp.bfloat16), 'dp', scatter_dimension=...  170 us
    reduce_scatter x1, waiting for transfers between devices, shards(): lax.psum_scatter(grad_down.astype(jnp.bfloat16), 'dp', scatter_dimension=...  170 us
    reduce_scatter x1, waiting for transfers between devices, shards(): lax.psum_scatter(grad_up.astype(jnp.bfloat16), 'dp', scatter_dimension=0,...  169 us
    reduce_scatter x1, waiting for transfers between devices, shards(): lax.psum_scatter(grad_value_w.astype(jnp.bfloat16), 'dp', scatter_dimensi...  161 us
    reduce_scatter x1, waiting for transfers between devices, shards(): lax.psum_scatter(grad_outw.astype(jnp.bfloat16), 'dp', scatter_dimension=...  161 us
    reduce_scatter x1, waiting for transfers between devices, shards(): lax.psum_scatter(grad_outgate_w.astype(jnp.bfloat16), 'dp', scatter_dimen...  161 us
    reduce_scatter x1, waiting for transfers between devices, shards(): lax.psum_scatter(grad_query_w.astype(jnp.bfloat16), 'dp', scatter_dimensi...  159 us
  transfers between devices with their start and end apart: 26, of which 24 were waited for; matrix products, arithmetic and copies ran while one was open for 9% of the time, Pallas kernels for 0%

commit v1 on v0

v1 whole, which is shorter than its diff:
```python
from functools import partial

import jax
import jax.numpy as jnp
from jax import lax
from jax.sharding import Mesh, PartitionSpec as P

H = 8
DK = 128
DV = 256
CONV = 4
SPAN = 64


EPSILON = 1e-06
MIXER_FLOOR = 0.001
HIGHEST = lax.Precision.HIGHEST


def causal_conv(values, kernel_taps, seg_ids):
    taps_count = kernel_taps.shape[0]
    columns = values.shape[1]
    summed = values * kernel_taps[taps_count - 1][None, :]
    for offset in range(1, taps_count):
        moved = jnp.concatenate(
            [jnp.zeros((offset, columns), values.dtype), values[:-offset]], axis=0
        )
        earlier = jnp.concatenate([jnp.full((offset,), -1, jnp.int32), seg_ids[:-offset]], axis=0)
        matches = (earlier == seg_ids).astype(values.dtype)
        summed = summed + kernel_taps[taps_count - 1 - offset][None, :] * moved * matches[:, None]
    return jax.nn.silu(summed)


def unit_rows(values):
    return values * lax.rsqrt(jnp.sum(values * values, axis=-1, keepdims=True) + EPSILON)


def gated_norm(mixed_rows, gain, gate_rows):
    scaled = mixed_rows * lax.rsqrt(
        jnp.mean(mixed_rows * mixed_rows, axis=-1, keepdims=True) + MIXER_FLOOR
    )
    return scaled * gain * jax.nn.silu(gate_rows)


def block_step(state_now, inputs):
    query_block, key_block, value_block, beta_block, decay_block, seg_block, seg_prior = inputs
    length = seg_block.shape[0]
    row_index = lax.broadcasted_iota(jnp.int32, (length, length), 0)
    col_index = lax.broadcasted_iota(jnp.int32, (length, length), 1)
    causal = (seg_block[:, None] == seg_block[None, :]) & (col_index <= row_index)
    strict = causal & (col_index < row_index)
    cumulative = jnp.cumsum(decay_block, axis=-1)
    spread = jnp.where(causal[None], cumulative[:, :, None] - cumulative[:, None, :], 0.0)
    ratio = jnp.exp(spread) * causal[None].astype(jnp.float32)
    carry_in = (seg_block == seg_prior).astype(jnp.float32)
    growth = jnp.exp(cumulative) * carry_in[None, :]
    key_inner = jnp.einsum("hik,hjk->hij", key_block, key_block, precision=HIGHEST)
    lower_part = jnp.where(strict[None], beta_block[:, :, None] * ratio * key_inner, 0.0)
    recalled = jnp.einsum("hik,hvk->hiv", key_block, state_now, precision=HIGHEST)
    target_rows = beta_block[:, :, None] * (value_block - growth[:, :, None] * recalled)
    system = lower_part + jnp.eye(length, dtype=jnp.float32)[None]
    written = jax.scipy.linalg.solve_triangular(system, target_rows, lower=True, unit_diagonal=True)
    scores = jnp.einsum("hik,hjk->hij", query_block, key_block, precision=HIGHEST) * ratio
    outputs = growth[:, :, None] * jnp.einsum(
        "hik,hvk->hiv", query_block, state_now, precision=HIGHEST
    )
    outputs = outputs + jnp.einsum("hij,hjv->hiv", scores, written, precision=HIGHEST)
    fading = ratio[:, length - 1, :]
    new_state = growth[:, length - 1][:, None, None] * state_now
    new_state = new_state + jnp.einsum(
        "hjv,hjk->hvk", fading[:, :, None] * written, key_block, precision=HIGHEST
    )
    return (new_state, outputs)


def mixer_core(
    seg_ids,
    seg_before,
    query_raw,
    key_raw,
    value_raw,
    gate_raw,
    beta_raw,
    decay_raw,
    conv_query,
    conv_key,
    conv_value,
    decay_log,
    step_bias,
    mixer_gain,
):
    row_count = query_raw.shape[0]
    heads_here = decay_log.shape[0]
    blocks = row_count // SPAN
    queries = unit_rows(
        causal_conv(query_raw, conv_query, seg_ids).reshape(row_count, heads_here, DK)
    ) * DK ** (-0.5)
    keys_unit = unit_rows(
        causal_conv(key_raw, conv_key, seg_ids).reshape(row_count, heads_here, DK)
    )
    values = causal_conv(value_raw, conv_value, seg_ids).reshape(row_count, heads_here, DV)
    beta_rates = jax.nn.sigmoid(beta_raw)
    decays = -jnp.exp(decay_log)[None, :] * jax.nn.softplus(decay_raw + step_bias[None, :])

    def heads_first(member_array):
        return jnp.swapaxes(member_array.reshape((blocks, SPAN) + member_array.shape[1:]), 1, 2)

    seg_blocks = seg_ids.reshape(blocks, SPAN)
    initial = jnp.zeros((heads_here, DV, DK), jnp.float32)
    ignored, outputs = lax.scan(
        jax.checkpoint(block_step),
        initial,
        (
            heads_first(queries),
            heads_first(keys_unit),
            heads_first(values),
            heads_first(beta_rates),
            heads_first(decays),
            seg_blocks,
            seg_before,
        ),
    )
    mixed_rows = jnp.swapaxes(outputs, 1, 2).reshape(row_count, heads_here, DV)
    gated_rows = gated_norm(mixed_rows, mixer_gain, gate_raw.reshape(row_count, heads_here, DV))
    return gated_rows.reshape(row_count, heads_here * DV)


SWAP = [(0, 1), (1, 0)]
PLANE = ("z", "y")
SMALL = 128


def trade(values, axis):
    return lax.ppermute(values, axis, SWAP)


def paired(own, other, index, axis):
    first = jnp.where(index == 0, own, other)
    second = jnp.where(index == 0, other, own)
    return jnp.stack([first, second], axis=axis)


def gather_tokens(own):
    rows, columns = own.shape
    pair = paired(own, trade(own, "xh"), lax.axis_index("xh"), 0)
    full = paired(pair, trade(pair, "c"), lax.axis_index("c"), 1)
    return full.reshape(4 * rows, columns)


def scatter_tokens(terms):
    rows = terms.shape[0] // 4
    columns = terms.shape[1]
    core = lax.axis_index("c")
    half = lax.axis_index("xh")
    parts = terms.reshape(2, 2, rows, columns)
    kept = lax.dynamic_index_in_dim(parts, core, 1, keepdims=False)
    sent = lax.dynamic_index_in_dim(parts, 1 - core, 1, keepdims=False).astype(jnp.bfloat16)
    summed = kept + trade(sent, "c").astype(jnp.float32)
    kept = lax.dynamic_index_in_dim(summed, half, 0, keepdims=False)
    sent = lax.dynamic_index_in_dim(summed, 1 - half, 0, keepdims=False).astype(jnp.bfloat16)
    return kept + trade(sent, "xh").astype(jnp.float32)


def gather_weights(block):
    both = jnp.stack([block, trade(block, "xl")], axis=0)
    full = lax.all_gather(both, PLANE, axis=0, tiled=False)
    return full.reshape(-1, block.shape[1])


def scatter_grads(grads):
    columns = grads.shape[1]
    both = lax.psum_scatter(grads, PLANE, scatter_dimension=0, tiled=True)
    both = both.reshape(2, -1, columns)
    return both[0].astype(jnp.float32) + trade(both[1], "xl").astype(jnp.float32)


def features_in(rows):
    count = rows.shape[0]
    halves = rows.reshape(count, 2, -1)
    flip = lax.axis_index("xl") == 1
    first = jnp.where(flip, halves[:, 1], halves[:, 0]).reshape(count, 16, 64)
    second = jnp.where(flip, halves[:, 0], halves[:, 1]).reshape(count, 16, 64)
    return jnp.concatenate([first, second], axis=2).reshape(count, -1)


def features_out(rows):
    count = rows.shape[0]
    blocks = rows.reshape(count, 16, 2, 64)
    flip = lax.axis_index("xl") == 1
    first = blocks[:, :, 0].reshape(count, -1)
    second = blocks[:, :, 1].reshape(count, -1)
    low = jnp.where(flip, second, first)
    high = jnp.where(flip, first, second)
    return jnp.concatenate([low, high], axis=1)


def sum_over(values, axes):
    for axis in axes:
        size = lax.axis_size(axis)
        step = 1
        while step < size:
            values = values + lax.ppermute(values, axis, [(i, i ^ step) for i in range(size)])
            step *= 2
    return values


def product(left, right):
    return jnp.dot(left, right, preferred_element_type=jnp.float32)


def product_t(left, right):
    return jnp.einsum("gf,df->gd", left, right, preferred_element_type=jnp.float32)


def t_product(left, right):
    return jnp.einsum(
        "gd,gf->df", left, right, preferred_element_type=jnp.float32
    ).astype(jnp.bfloat16)


def shards(
    layer_input,
    teacher_out,
    lengths,
    norm1_gain,
    query_weight,
    key_weight,
    value_weight,
    output_gate,
    beta_weight,
    decay_weight,
    decay_log,
    step_bias,
    query_taps,
    key_taps,
    value_taps,
    mixer_gain,
    out_weight,
    norm2_gain,
    gate_weight,
    up_weight,
    down_weight,
):
    tok_rows = layer_input.shape[0]
    group_rows = 4 * tok_rows
    all_rows = 32 * group_rows
    rows_dp = norm1_gain.shape[0]
    group_index = lax.axis_index("xl") * 16 + lax.axis_index("z") * 4 + lax.axis_index("y")
    tensor_index = lax.axis_index("xh") * 2 + lax.axis_index("c")
    heads_here = decay_log.shape[0]
    own_lengths = lax.dynamic_index_in_dim(lengths, group_index, 0, keepdims=False)
    boundary = jnp.cumsum(own_lengths)
    positions = jnp.arange(group_rows, dtype=jnp.int32)
    seg_ids = jnp.sum((positions[:, None] >= boundary[None, :]).astype(jnp.int32), axis=1)
    seg_before = jnp.concatenate([jnp.full((1,), -1, jnp.int32), seg_ids[SPAN - 1 : -1 : SPAN]])
    own_rows = tensor_index * tok_rows + jnp.arange(tok_rows, dtype=jnp.int32)
    validity = (own_rows < boundary[-1]).astype(jnp.float32)[:, None]
    loss_scale = jnp.float32(all_rows) / jnp.sum(lengths).astype(jnp.float32)

    filler = jnp.zeros((rows_dp, SMALL - 2 * heads_here - 2), jnp.bfloat16)
    mixer_block = jnp.concatenate(
        [
            query_weight,
            key_weight,
            value_weight,
            output_gate,
            beta_weight,
            decay_weight,
            norm1_gain[:, None],
            norm2_gain[:, None],
            filler,
            out_weight,
        ],
        axis=1,
    )
    ffn_block = jnp.concatenate([gate_weight, up_weight, down_weight], axis=1)
    mixer_full = gather_weights(mixer_block)
    ffn_full = gather_weights(ffn_block)
    input_own = features_in(layer_input)
    teacher_own = features_in(teacher_out).astype(jnp.float32)
    input_all = gather_tokens(input_own)

    qk_width = query_taps.shape[1]
    v_width = value_taps.shape[1]
    f_width = gate_weight.shape[1]
    proj_width = 2 * qk_width + 2 * v_width
    proj_full = mixer_full[:, : proj_width + SMALL]
    outw_full = mixer_full[:, proj_width + SMALL :]
    gains = mixer_full[:, proj_width : proj_width + SMALL].T.astype(jnp.float32)
    gain_first = gains[2 * heads_here][None, :]
    gain_second = gains[2 * heads_here + 1][None, :]
    gate_up_full = ffn_full[:, : 2 * f_width]
    down_full = ffn_full[:, 2 * f_width :]

    input_float = input_own.astype(jnp.float32)
    scale_one = lax.rsqrt(jnp.mean(input_float * input_float, axis=-1, keepdims=True) + EPSILON)
    every = input_all.astype(jnp.float32)
    scale_all = lax.rsqrt(jnp.mean(every * every, axis=-1, keepdims=True) + EPSILON)
    normed_one = (every * scale_all * gain_first).astype(jnp.bfloat16)

    raw = product(normed_one, proj_full)
    query_raw = raw[:, :qk_width]
    key_raw = raw[:, qk_width : 2 * qk_width]
    value_raw = raw[:, 2 * qk_width : 2 * qk_width + v_width]
    gate_raw = raw[:, 2 * qk_width + v_width : proj_width]
    beta_raw = raw[:, proj_width : proj_width + heads_here]
    decay_raw = raw[:, proj_width + heads_here : proj_width + 2 * heads_here]
    core = partial(mixer_core, seg_ids, seg_before)
    gated_rows, pullback = jax.vjp(
        core,
        query_raw,
        key_raw,
        value_raw,
        gate_raw,
        beta_raw,
        decay_raw,
        query_taps.astype(jnp.float32),
        key_taps.astype(jnp.float32),
        value_taps.astype(jnp.float32),
        decay_log,
        step_bias,
        mixer_gain.astype(jnp.float32),
    )
    gated_low = gated_rows.astype(jnp.bfloat16)
    hidden = input_float + scatter_tokens(product_t(gated_low, outw_full))
    scale_two = lax.rsqrt(jnp.mean(hidden * hidden, axis=-1, keepdims=True) + EPSILON)
    normed_two = gather_tokens((hidden * scale_two * gain_second).astype(jnp.bfloat16))
    gate_up = product(normed_two, gate_up_full)
    gate_in = gate_up[:, :f_width]
    up_in = gate_up[:, f_width:]
    sigma = jax.nn.sigmoid(gate_in)
    act_low = (gate_in * sigma * up_in).astype(jnp.bfloat16)
    layer_out = hidden + scatter_tokens(product_t(act_low, down_full))
    grad_layer = loss_scale * validity * (layer_out - teacher_own)
    grad_branch_two = gather_tokens(grad_layer.astype(jnp.bfloat16))
    grad_act = product(grad_branch_two, down_full)
    grad_gate_in = (grad_act * up_in * sigma * (1.0 + gate_in * (1.0 - sigma))).astype(jnp.bfloat16)
    grad_up_in = (grad_act * gate_in * sigma).astype(jnp.bfloat16)
    grad_gate_up = jnp.concatenate([grad_gate_in, grad_up_in], axis=1)
    grad_normed_two = scatter_tokens(product_t(grad_gate_up, gate_up_full))
    down_sum = scatter_grads(t_product(grad_branch_two, act_low))
    gate_up_sum = scatter_grads(t_product(normed_two, grad_gate_up))

    weighted_two = gain_second * grad_normed_two
    grad_gain_two = jnp.sum(grad_normed_two * hidden * scale_two, axis=0)
    grad_hidden = (
        grad_layer
        + scale_two * weighted_two
        - hidden
        * (scale_two * scale_two * scale_two)
        * jnp.mean(weighted_two * hidden, axis=-1, keepdims=True)
    )
    grad_branch_one = gather_tokens(grad_hidden.astype(jnp.bfloat16))
    outw_grad = t_product(grad_branch_one, gated_low)
    grad_gated = product(grad_branch_one, outw_full)
    (
        grad_query_raw,
        grad_key_raw,
        grad_value_raw,
        grad_gate_raw,
        grad_beta_raw,
        grad_decay_raw,
        grad_qtaps,
        grad_ktaps,
        grad_vtaps,
        grad_dlog,
        grad_bias,
        grad_mgain,
    ) = pullback(grad_gated)
    raw_low = jnp.concatenate(
        [
            grad_query_raw,
            grad_key_raw,
            grad_value_raw,
            grad_gate_raw,
            grad_beta_raw,
            grad_decay_raw,
            jnp.zeros((group_rows, SMALL - 2 * heads_here), jnp.float32),
        ],
        axis=1,
    ).astype(jnp.bfloat16)
    proj_grad = t_product(normed_one, raw_low)
    grad_normed_one = scatter_tokens(product_t(raw_low, proj_full))
    weighted_one = gain_first * grad_normed_one
    grad_gain_one = jnp.sum(grad_normed_one * input_float * scale_one, axis=0)
    grad_input = (
        grad_hidden
        + scale_one * weighted_one
        - input_float
        * (scale_one * scale_one * scale_one)
        * jnp.mean(weighted_one * input_float, axis=-1, keepdims=True)
    )
    mixer_sum = scatter_grads(jnp.concatenate([proj_grad, outw_grad], axis=1))

    taps = jnp.concatenate([grad_qtaps, grad_ktaps, grad_vtaps], axis=1)
    gain_pair = features_out(jnp.stack([grad_gain_one, grad_gain_two]))
    n_taps = taps.size
    n_all = 2 * gain_pair.shape[1] + grad_mgain.shape[0]
    flat = jnp.concatenate(
        [gain_pair.reshape(-1), grad_mgain, taps.reshape(-1), grad_dlog, grad_bias]
    )
    flat = jnp.pad(flat, (0, -flat.shape[0] % 1024)).reshape(-1, 128)
    flat = sum_over(flat, ("xl", "z", "y"))
    shared_rows = n_all // 128
    shared = sum_over(flat[:shared_rows], ("xh", "c")).reshape(-1)
    flat = flat.reshape(-1)
    taps_sum = flat[n_all : n_all + n_taps].reshape(CONV, -1)
    heads_at = n_all + n_taps
    features = gain_pair.shape[1]
    norm1_grad = lax.dynamic_slice_in_dim(shared, group_index * rows_dp, rows_dp)
    norm2_grad = lax.dynamic_slice_in_dim(shared, features + group_index * rows_dp, rows_dp)
    small_at = proj_width
    out_at = proj_width + SMALL
    return (
        features_out(layer_out),
        features_out(grad_input),
        norm1_grad,
        mixer_sum[:, :qk_width],
        mixer_sum[:, qk_width : 2 * qk_width],
        mixer_sum[:, 2 * qk_width : 2 * qk_width + v_width],
        mixer_sum[:, 2 * qk_width + v_width : proj_width],
        mixer_sum[:, small_at : small_at + heads_here],
        mixer_sum[:, small_at + heads_here : small_at + 2 * heads_here],
        flat[heads_at : heads_at + heads_here],
        flat[heads_at + heads_here : heads_at + 2 * heads_here],
        taps_sum[:, :qk_width],
        taps_sum[:, qk_width : 2 * qk_width],
        taps_sum[:, 2 * qk_width :],
        shared[2 * features :],
        mixer_sum[:, out_at:],
        norm2_grad,
        gate_up_sum[:, :f_width],
        gate_up_sum[:, f_width:],
        down_sum,
    )


def solution(mesh):
    fine = Mesh(mesh.devices.reshape(2, 4, 4, 2, 2), ("xl", "z", "y", "xh", "c"))
    dp = ("xl", "z", "y")
    tensor = ("xh", "c")
    tokens = P(dp + tensor, None)
    weight = P(dp, tensor)
    gain = P(dp)
    heads = P(tensor)
    taps = P(None, tensor)
    in_specs = (
        (tokens, tokens, P(), gain)
        + (weight,) * 6
        + (heads, heads, taps, taps, taps, P(), weight, gain)
        + (weight,) * 3
    )
    out_specs = (
        (tokens, tokens, gain)
        + (weight,) * 6
        + (heads, heads, taps, taps, taps, P(), weight, gain)
        + (weight,) * 3
    )
    return jax.shard_map(shards, mesh=fine, in_specs=in_specs, out_specs=out_specs, check_vma=False)
```

time: 3650 us -> 951 us (0.26)
  waiting for transfers between devices: 2670 us -> 266 us
  blocking collectives: 237 us -> 0 us
  matrix products: 274 us -> 187 us
  starting transfers between devices: 1.92 us -> 43.9 us
    reduce_scatter x12 -> x2, waiting for transfers between devices: 1460 us -> 84.4 us  [scatter_grads(): both = lax.psum_scatter(grads, PLANE, scatter_dimension=0, tiled=True)]
    all_gather x12 -> x2, waiting for transfers between devices: 970 us -> 40.3 us  [gather_weights(): full = lax.all_gather(both, PLANE, axis=0, tiled=False)]
    all_gather x2 -> x0, blocking collectives: 152 us -> none  [the longest x1 76.8 us: shards(): lax.all_gather(beta_weight, 'dp', axis=0, tiled=True)]
    psum x1 -> x0, waiting for transfers between devices: 140 us -> none  [shards(): lax.psum((grad_gain_one, grad_gain_two, dlog_full, bias_full, qtaps_full,...]
    ppermute x0 -> x28, waiting for transfers between devices: none -> 138 us  [the longest x21 128 us: trade(): return lax.ppermute(values, axis, SWAP)]
    unnamed x27 -> x6, waiting for transfers between devices: 101 us -> 3.57 us
    unnamed x1 -> x0, blocking collectives: 85.4 us -> none
    dot_general x27 -> x12, matrix products: 116 us -> 73.1 us  [the longest x4 25.4 us: product_t(): jnp.einsum('gf,df->gd', left, right, preferred_element_type=jnp.float32)]
  transfers between devices with their start and end apart: 26 -> 33, of which waited for: 24 -> 26; matrix products, arithmetic and copies ran while one was open for 9% -> 57% of each run, Pallas kernels for 0% -> 0%
where the time goes in v1:
time: 951 us; the launch traced here: 945 us
  waiting for transfers between devices  266 us (28%)
  other arithmetic  260 us (27%)
  matrix products  187 us (20%)
  local copies, waits for them, and re-layouts  168 us (18%)
  starting transfers between devices  43.9 us (5%)
  between operations  16.8 us (2%)
    another operation x64, other arithmetic, block_step(): jax.scipy.linalg.solve_triangular(system, target_rows, lower=True, unit_d...  159 us
    ppermute x21, waiting for transfers between devices, trade(): return lax.ppermute(values, axis, SWAP)  128 us
    reduce_scatter x2, waiting for transfers between devices, scatter_grads(): both = lax.psum_scatter(grads, PLANE, scatter_dimension=0, tiled=True)  84.4 us
    unnamed x272, local copies, waits for them, and re-layouts  55.1 us
    all_gather x2, waiting for transfers between devices, gather_weights(): full = lax.all_gather(both, PLANE, axis=0, tiled=False)  40.3 us
    ppermute x21, starting transfers between devices, trade(): return lax.ppermute(values, axis, SWAP)  32.2 us
    dot_general x4, matrix products, product_t(): jnp.einsum('gf,df->gd', left, right, preferred_element_type=jnp.float32)  25.4 us
    dot_general x4, matrix products, product(): return jnp.dot(left, right, preferred_element_type=jnp.float32)  24.1 us
  transfers between devices with their start and end apart: 33, of which 26 were waited for; matrix products, arithmetic and copies ran while one was open for 57% of the time, Pallas kernels for 0%

profile of v1, /device:TPU:0, one launch (start us, length us, event | category | flops | bytes accessed | tf_op | source)
XLA Modules:
  0.0 944.6 jit_solution(1620330921566634629)
XLA Ops:
  27.9 11.6 %collective-permute-done = bf16[128,2048]{1,0:T(8,128)(2,1)S(1)} collective-permute-done((bf16[128,2048]{1,0:T(8,128)(2,1)S(1)}, bf16[128,2048]{1,0:T(8,128)(2,1)S(1)}, u32[]{:S(2)}, u32[]{:S(2)}) %collective-permute-start) | collective-permute-done | bytes 524320 | tf_op jit(solution)/shard_map/ppermute | solution.py:134
  40.1 9.4 collective-permute-done.7
  56.4 40.3 %all-gather.5.cloned.1.call-done = bf16[32,64,2176]{2,1,0:T(8,128)(2,1)} async-done(((bf16[2,64,2176]{2,1,0:T(8,128)(2,1)}), bf16[32,64,2176]{2,1,0:T(8,128)(2,1)}) %all-gather.5.cloned.1.call-update) | async-done | bytes 8912912 | tf_op jit(solution)/shard_map/all_gather | solution.py:166
  138.9 141.6 %while.42 = (s32[]{:T(128)}, f32[2,256,128]{2,1,0:T(8,128)S(1)}, f32[8,2,64,256]{3,2,1,0:T(8,128)S(1)}, f32[8,2,256,128]{3,2,1,0:T(8,128)}, f32[8,2,64]{2,1,0:T(...) while((s32[]{:T(128)}, f32[2,256,128]{2,1,0:T(8,128)S(1)}, ...), condition=%wide.region_7.9_spmd.clone, body=%wide.region_5.8_spmd.clone.sunk | while | flops 227266752 | bytes 3607773 | solution.py:110
  144.1 9.8 %custom-call.29 = f32[2,1,64,64]{2,3,1,0:T(8,128)S(1)} custom-call(f32[2,1,64,64]{3,2,1,0:T(8,128)S(1)} %fusion.376), custom_call_target="InvertDiagBlocksLowerTriangular" | custom-call | tf_op jit(solution)/shard_map/jvp()/while/body/eval_jaxpr/jit(_solve_triangular)/vmap()/triangular_solve/custom-call.1 | solution.py:62
  161.8 9.8 %custom-call.29 = f32[2,1,64,64]{2,3,1,0:T(8,128)S(1)} custom-call(f32[2,1,64,64]{3,2,1,0:T(8,128)S(1)} %fusion.376), custom_call_target="InvertDiagBlocksLowerTriangular" | custom-call | tf_op jit(solution)/shard_map/jvp()/while/body/eval_jaxpr/jit(_solve_triangular)/vmap()/triangular_solve/custom-call.1 | solution.py:62
  179.5 9.8 %custom-call.29 = f32[2,1,64,64]{2,3,1,0:T(8,128)S(1)} custom-call(f32[2,1,64,64]{3,2,1,0:T(8,128)S(1)} %fusion.376), custom_call_target="InvertDiagBlocksLowerTriangular" | custom-call | tf_op jit(solution)/shard_map/jvp()/while/body/eval_jaxpr/jit(_solve_triangular)/vmap()/triangular_solve/custom-call.1 | solution.py:62
  197.2 9.8 %custom-call.29 = f32[2,1,64,64]{2,3,1,0:T(8,128)S(1)} custom-call(f32[2,1,64,64]{3,2,1,0:T(8,128)S(1)} %fusion.376), custom_call_target="InvertDiagBlocksLowerTriangular" | custom-call | tf_op jit(solution)/shard_map/jvp()/while/body/eval_jaxpr/jit(_solve_triangular)/vmap()/triangular_solve/custom-call.1 | solution.py:62
  214.9 9.8 %custom-call.29 = f32[2,1,64,64]{2,3,1,0:T(8,128)S(1)} custom-call(f32[2,1,64,64]{3,2,1,0:T(8,128)S(1)} %fusion.376), custom_call_target="InvertDiagBlocksLowerTriangular" | custom-call | tf_op jit(solution)/shard_map/jvp()/while/body/eval_jaxpr/jit(_solve_triangular)/vmap()/triangular_solve/custom-call.1 | solution.py:62
  232.6 9.8 %custom-call.29 = f32[2,1,64,64]{2,3,1,0:T(8,128)S(1)} custom-call(f32[2,1,64,64]{3,2,1,0:T(8,128)S(1)} %fusion.376), custom_call_target="InvertDiagBlocksLowerTriangular" | custom-call | tf_op jit(solution)/shard_map/jvp()/while/body/eval_jaxpr/jit(_solve_triangular)/vmap()/triangular_solve/custom-call.1 | solution.py:62
  250.3 9.8 %custom-call.29 = f32[2,1,64,64]{2,3,1,0:T(8,128)S(1)} custom-call(f32[2,1,64,64]{3,2,1,0:T(8,128)S(1)} %fusion.376), custom_call_target="InvertDiagBlocksLowerTriangular" | custom-call | tf_op jit(solution)/shard_map/jvp()/while/body/eval_jaxpr/jit(_solve_triangular)/vmap()/triangular_solve/custom-call.1 | solution.py:62
  268.0 9.8 %custom-call.29 = f32[2,1,64,64]{2,3,1,0:T(8,128)S(1)} custom-call(f32[2,1,64,64]{3,2,1,0:T(8,128)S(1)} %fusion.376), custom_call_target="InvertDiagBlocksLowerTriangular" | custom-call | tf_op jit(solution)/shard_map/jvp()/while/body/eval_jaxpr/jit(_solve_triangular)/vmap()/triangular_solve/custom-call.1 | solution.py:62
  302.1 12.6 %collective-permute-done.4 = bf16[128,2048]{1,0:T(8,128)(2,1)} collective-permute-done((bf16[128,2048]{1,0:T(8,128)(2,1)S(1)}, bf16[128,2048]{1,0:T(8,128)(2,1)}, u32[]{:S(2)}, u32[]{:S(2)}) %collective-permute-start.4) | collective-permute-done | bytes 524320 | tf_op jit(solution)/shard_map/ppermute | solution.py:134
  319.7 11.7 %collective-permute-done.5 = bf16[128,2048]{1,0:T(8,128)(2,1)S(1)} collective-permute-done((bf16[128,2048]{1,0:T(8,128)(2,1)S(1)}, bf16[128,2048]{1,0:T(8,128)(2,1)S(1)}, u32[]{:S(2)}, u32[]{:S(2)}) %collective-permute-start.5) | collective-permute-done | bytes 524320 | tf_op jit(solution)/shard_map/ppermute | solution.py:134
  336.3 10.2 %fusion.134 = f32[512,2816]{1,0:T(8,128)S(1)} fusion(bf16[512,2048]{1,0:T(8,128)(2,1)} %bitcast.653, bf16[2048,4224]{1,0:T(8,128)(2,1)} %bitcast.733), kind=kOutput, calls=%fused_computation.189 | convolution fusion | flops 5905580032 | bytes 19398656 | tf_op jit(solution)/shard_map/dot_general | solution.py:208
  385.4 11.7 %collective-permute-done.10 = bf16[128,2048]{1,0:T(8,128)(2,1)S(1)} collective-permute-done((bf16[128,2048]{1,0:T(8,128)(2,1)S(1)}, bf16[128,2048]{1,0:T(8,128)(2,1)S(1)}, u32[]{:S(2)}, u32[]{:S(2)}) %collective-permute-start.10) | collective-permute-done | bytes 524320 | tf_op jit(solution)/shard_map/ppermute | solution.py:134
  410.5 10.0 %fusion.132 = f32[512,2048]{1,0:T(8,128)S(1)} fusion(bf16[2048,4224]{1,0:T(8,128)(2,1)} %bitcast.736, bf16[512,1408]{1,0:T(8,128)(2,1)S(1)} %get-tuple-element.1046, bf16[512,1408]{1,0:T(8,128)(2,1)S(1)} %get-tuple-element.1045), kind=kOutput, calls=%fused_computation.187 | convolution fusion | flops 5911347200 | bytes 18612224 | tf_op jit(solution)/shard_map/gf,df->gd/dot_general | solution.py:212
  426.9 12.5 %collective-permute-done.13 = bf16[128,2048]{1,0:T(8,128)(2,1)S(1)} collective-permute-done((bf16[128,2048]{1,0:T(8,128)(2,1)S(1)}, bf16[128,2048]{1,0:T(8,128)(2,1)S(1)}, u32[]{:S(2)}, u32[]{:S(2)}) %collective-permute-start.13) | collective-permute-done | bytes 524320 | tf_op jit(solution)/shard_map/ppermute | solution.py:134
  446.7 9.7 %collective-permute-done.14 = bf16[128,2048]{1,0:T(8,128)(2,1)S(1)} collective-permute-done((bf16[128,2048]{1,0:T(8,128)(2,1)S(1)}, bf16[128,2048]{1,0:T(8,128)(2,1)S(1)}, u32[]{:S(2)}, u32[]{:S(2)}) %collective-permute-start.14) | collective-permute-done | bytes 524320 | tf_op jit(solution)/shard_map/ppermute | solution.py:134
  483.4 199.7 %while.43 = (s32[]{:T(128)}, f32[2,256,128]{2,1,0:T(8,128)S(1)}, f32[8,2,64,128]{3,2,1,0:T(8,128)}, f32[8,2,64,128]{3,2,1,0:T(8,128)}, f32[8,2,64,256]{3,2,1,0:T...) while((s32[]{:T(128)}, f32[2,256,128]{2,1,0:T(8,128)S(1)}, ...), condition=%wide.region_25.27_spmd.clone, body=%wide.region_14.26_spmd.clone.sunk | while | flops 612094144 | bytes 10948683 | solution.py:110
  490.2 9.8 %custom-call.30 = f32[2,1,64,64]{2,3,1,0:T(8,128)S(1)} custom-call(f32[2,1,64,64]{3,2,1,0:T(8,128)S(1)} %get-tuple-element.1375), custom_call_target="InvertDiagBlocksLowerTriangular" | custom-call | tf_op jit(solution)/shard_map/transpose(jvp())/while/body/eval_jaxpr/checkpoint/jit(_solve_triangular)/vmap()/triangular_solve | solution.py:62
  515.1 9.8 %custom-call.30 = f32[2,1,64,64]{2,3,1,0:T(8,128)S(1)} custom-call(f32[2,1,64,64]{3,2,1,0:T(8,128)S(1)} %get-tuple-element.1375), custom_call_target="InvertDiagBlocksLowerTriangular" | custom-call | tf_op jit(solution)/shard_map/transpose(jvp())/while/body/eval_jaxpr/checkpoint/jit(_solve_triangular)/vmap()/triangular_solve | solution.py:62
  540.1 9.8 %custom-call.30 = f32[2,1,64,64]{2,3,1,0:T(8,128)S(1)} custom-call(f32[2,1,64,64]{3,2,1,0:T(8,128)S(1)} %get-tuple-element.1375), custom_call_target="InvertDiagBlocksLowerTriangular" | custom-call | tf_op jit(solution)/shard_map/transpose(jvp())/while/body/eval_jaxpr/checkpoint/jit(_solve_triangular)/vmap()/triangular_solve | solution.py:62
  565.0 9.8 %custom-call.30 = f32[2,1,64,64]{2,3,1,0:T(8,128)S(1)} custom-call(f32[2,1,64,64]{3,2,1,0:T(8,128)S(1)} %get-tuple-element.1375), custom_call_target="InvertDiagBlocksLowerTriangular" | custom-call | tf_op jit(solution)/shard_map/transpose(jvp())/while/body/eval_jaxpr/checkpoint/jit(_solve_triangular)/vmap()/triangular_solve | solution.py:62
  589.9 9.8 %custom-call.30 = f32[2,1,64,64]{2,3,1,0:T(8,128)S(1)} custom-call(f32[2,1,64,64]{3,2,1,0:T(8,128)S(1)} %get-tuple-element.1375), custom_call_target="InvertDiagBlocksLowerTriangular" | custom-call | tf_op jit(solution)/shard_map/transpose(jvp())/while/body/eval_jaxpr/checkpoint/jit(_solve_triangular)/vmap()/triangular_solve | solution.py:62
  614.8 9.8 %custom-call.30 = f32[2,1,64,64]{2,3,1,0:T(8,128)S(1)} custom-call(f32[2,1,64,64]{3,2,1,0:T(8,128)S(1)} %get-tuple-element.1375), custom_call_target="InvertDiagBlocksLowerTriangular" | custom-call | tf_op jit(solution)/shard_map/transpose(jvp())/while/body/eval_jaxpr/checkpoint/jit(_solve_triangular)/vmap()/triangular_solve | solution.py:62
  639.7 9.8 %custom-call.30 = f32[2,1,64,64]{2,3,1,0:T(8,128)S(1)} custom-call(f32[2,1,64,64]{3,2,1,0:T(8,128)S(1)} %get-tuple-element.1375), custom_call_target="InvertDiagBlocksLowerTriangular" | custom-call | tf_op jit(solution)/shard_map/transpose(jvp())/while/body/eval_jaxpr/checkpoint/jit(_solve_triangular)/vmap()/triangular_solve | solution.py:62
  664.6 9.8 %custom-call.30 = f32[2,1,64,64]{2,3,1,0:T(8,128)S(1)} custom-call(f32[2,1,64,64]{3,2,1,0:T(8,128)S(1)} %get-tuple-element.1375), custom_call_target="InvertDiagBlocksLowerTriangular" | custom-call | tf_op jit(solution)/shard_map/transpose(jvp())/while/body/eval_jaxpr/checkpoint/jit(_solve_triangular)/vmap()/triangular_solve | solution.py:62
  732.3 11.7 %copy.532 = bf16[2048,2176]{1,0:T(8,128)(2,1)} copy(bf16[2048,2176]{0,1:T(8,128)(2,1)} %pad_maximum_fusion) | data formatting | bytes 17825792
  746.0 10.2 %convolution_convert_fusion = bf16[2048,2816]{1,0:T(8,128)(2,1)} fusion(bf16[512,2048]{1,0:T(8,128)(2,1)S(1)} %bitcast.654, bf16[512,1408]{1,0:T(8,128)(2,1)} %copy-done.120, bf16[512,1408]{1,0:T(8,128)(2,1)S(1)} %copy-done.119), kind=kOutput, calls=%fused_computation.186 | convolution fusion | flops 5917114368 | bytes 16515072 | tf_op jit(solution)/shard_map/gd,gf->df/dot_general | solution.py:216
  775.9 12.6 %collective-permute-done.17 = bf16[128,2048]{1,0:T(8,128)(2,1)S(1)} collective-permute-done((bf16[128,2048]{1,0:T(8,128)(2,1)S(1)}, bf16[128,2048]{1,0:T(8,128)(2,1)S(1)}, u32[]{:S(2)}, u32[]{:S(2)}) %collective-permute-start.17) | collective-permute-done | bytes 524320 | tf_op jit(solution)/shard_map/ppermute | solution.py:134
  841.5 84.4 %reduce-scatter.6.cloned.1.call-done = bf16[128,2816]{1,0:T(8,128)(2,1)} async-done(((bf16[2048,2816]{1,0:T(8,128)(2,1)}), bf16[128,2816]{1,0:T(8,128)(2,1)}) %reduce-scatter.6.cloned.1.call-update) | async-done | bytes 720912 | tf_op jit(solution)/shard_map/reduce_scatter | solution.py:172
  (1091 shorter events, 508.9 us)
Async XLA Ops:
  7.2 89.5 %all-gather.5.cloned.1.call-start = ((), (), s32[]{:S(2)}) async-start(), calls=%async_computation.5 | async-start | bytes 9469952 | tf_op jit(solution)/shard_map/all_gather | solution.py:166
  11.3 8.3 collective-permute-start.2
  20.6 315.8 %all-gather.7.cloned.1.call-start = ((), (), s32[]{:S(2)}) async-start(), calls=%async_computation.6 | async-start | bytes 18382848 | tf_op jit(solution)/shard_map/all_gather | solution.py:166
  23.1 16.4 %collective-permute-start = (bf16[128,2048]{1,0:T(8,128)(2,1)S(1)}, bf16[128,2048]{1,0:T(8,128)(2,1)S(1)}, u32[]{:S(2)}, u32[]{:S(2)}) collective-permute-start(bf16[128,2048]{1,0:T(8,128)(2,1)S(1)} %copy.527), channel_id=1, source_target_pairs={{0,2},{2,0},{1,3},{3,1},{4,6},{6,4},{5,7},{7,5},{8,10},{10,8},{9,1... | collective-permute-start | bytes 1572872 | tf_op jit(solution)/shard_map/ppermute | solution.py:134
  26.5 23.0 %collective-permute-start.7 = (bf16[64,4224]{1,0:T(8,128)(2,1)S(1)}, bf16[64,4224]{1,0:T(8,128)(2,1)}, u32[]{:S(2)}, u32[]{:S(2)}) collective-permute-start(bf16[64,4224]{1,0:T(8,128)(2,1)S(1)} %constant_dynamic-update-slice_fusion.2), channel_id=1, source_target_pairs={{0,64},{64,0},{1,65},{65,1},{2,66},{66,2},{3,67},{67,3},{4,68},{68... | collective-permute-start | bytes 1622024 | tf_op jit(solution)/shard_map/ppermute | solution.py:134
  39.7 12.2 %collective-permute-start.1 = (bf16[2,128,2048]{2,1,0:T(8,128)(2,1)S(1)}, bf16[2,128,2048]{2,1,0:T(8,128)(2,1)}, u32[]{:S(2)}, u32[]{:S(2)}) collective-permute-start(bf16[2,128,2048]{2,1,0:T(8,128)(2,1)S(1)} %pad_maximum_fusion.8), channel_id=1, source_target_pairs={{0,1},{1,0},{2,3},{3,2},{4,5},{5,4},{6,7},{7,6},{8,9},{9,8},{10,11... | collective-permute-start | bytes 3145736 | tf_op jit(solution)/shard_map/ppermute | solution.py:134
  51.7 774.0 %reduce-scatter.8.cloned.1.call-start = ((), (), s32[]{:S(2)}) async-start(), calls=%async_computation.4 | async-start | bytes 6127616 | tf_op jit(solution)/shard_map/reduce_scatter | solution.py:172
  292.9 2.9 collective-permute-start.3
  299.1 15.7 %collective-permute-start.4 = (bf16[128,2048]{1,0:T(8,128)(2,1)S(1)}, bf16[128,2048]{1,0:T(8,128)(2,1)}, u32[]{:S(2)}, u32[]{:S(2)}) collective-permute-start(bf16[128,2048]{1,0:T(8,128)(2,1)S(1)} %fusion.174), channel_id=1, source_target_pairs={{0,2},{2,0},{1,3},{3,1},{4,6},{6,4},{5,7},{7,5},{8,10},{10,8},{9,1... | collective-permute-start | bytes 1572872 | tf_op jit(solution)/shard_map/ppermute | solution.py:134
  316.6 14.7 %collective-permute-start.5 = (bf16[128,2048]{1,0:T(8,128)(2,1)S(1)}, bf16[128,2048]{1,0:T(8,128)(2,1)S(1)}, u32[]{:S(2)}, u32[]{:S(2)}) collective-permute-start(bf16[128,2048]{1,0:T(8,128)(2,1)S(1)} %multiply_convert_fusion.3), channel_id=1, source_target_pairs={{0,2},{2,0},{1,3},{3,1},{4,6},{6,4},{5,7},{7,5},{8,10},{10,8},{9,1... | collective-permute-start | bytes 1572872 | tf_op jit(solution)/shard_map/ppermute | solution.py:134
  331.8 2.7 collective-permute-start.6
  358.1 3.0 collective-permute-start.8
  364.6 15.7 %collective-permute-start.9 = (bf16[128,2048]{1,0:T(8,128)(2,1)S(1)}, bf16[128,2048]{1,0:T(8,128)(2,1)}, u32[]{:S(2)}, u32[]{:S(2)}) collective-permute-start(bf16[128,2048]{1,0:T(8,128)(2,1)S(1)} %fusion.175), channel_id=1, source_target_pairs={{0,2},{2,0},{1,3},{3,1},{4,6},{6,4},{5,7},{7,5},{8,10},{10,8},{9,1... | collective-permute-start | bytes 1572872 | tf_op jit(solution)/shard_map/ppermute | solution.py:134
  382.4 14.7 %collective-permute-start.10 = (bf16[128,2048]{1,0:T(8,128)(2,1)S(1)}, bf16[128,2048]{1,0:T(8,128)(2,1)S(1)}, u32[]{:S(2)}, u32[]{:S(2)}) collective-permute-start(bf16[128,2048]{1,0:T(8,128)(2,1)S(1)} %get-tuple-element.1014), channel_id=1, source_target_pairs={{0,2},{2,0},{1,3},{3,1},{4,6},{6,4},{5,7},{7,5},{8,10},{10,8},{9,1... | collective-permute-start | bytes 1572872 | tf_op jit(solution)/shard_map/ppermute | solution.py:134
  397.3 2.9 collective-permute-start.11
  420.7 2.7 collective-permute-start.12
  423.8 15.5 %collective-permute-start.13 = (bf16[128,2048]{1,0:T(8,128)(2,1)S(1)}, bf16[128,2048]{1,0:T(8,128)(2,1)S(1)}, u32[]{:S(2)}, u32[]{:S(2)}) collective-permute-start(bf16[128,2048]{1,0:T(8,128)(2,1)S(1)} %fusion.176), channel_id=1, source_target_pairs={{0,2},{2,0},{1,3},{3,1},{4,6},{6,4},{5,7},{7,5},{8,10},{10,8},{9,1... | collective-permute-start | bytes 1572872 | tf_op jit(solution)/shard_map/ppermute | solution.py:134
  441.8 14.6 %collective-permute-start.14 = (bf16[128,2048]{1,0:T(8,128)(2,1)S(1)}, bf16[128,2048]{1,0:T(8,128)(2,1)S(1)}, u32[]{:S(2)}, u32[]{:S(2)}) collective-permute-start(bf16[128,2048]{1,0:T(8,128)(2,1)S(1)} %get-tuple-element.1010), channel_id=1, source_target_pairs={{0,2},{2,0},{1,3},{3,1},{4,6},{6,4},{5,7},{7,5},{8,10},{10,8},{9,1... | collective-permute-start | bytes 1572872 | tf_op jit(solution)/shard_map/ppermute | solution.py:134
  457.9 12.4 %collective-permute-start.15 = (bf16[2,128,2048]{2,1,0:T(8,128)(2,1)}, bf16[2,128,2048]{2,1,0:T(8,128)(2,1)}, u32[]{:S(2)}, u32[]{:S(2)}) collective-permute-start(bf16[2,128,2048]{2,1,0:T(8,128)(2,1)} %pad_maximum_fusion.12), channel_id=1, source_target_pairs={{0,1},{1,0},{2,3},{3,2},{4,5},{5,4},{6,7},{7,6},{8,9},{9,8},{10,11... | collective-permute-start | bytes 3145736 | tf_op jit(solution)/shard_map/ppermute | solution.py:134
  470.1 360.6 %reduce-scatter.10.cloned.1.call-start = ((), (), s32[]{:S(2)}) async-start(), calls=%async_computation.7 | async-start | bytes 9469952
  744.1 181.7 %reduce-scatter.6.cloned.1.call-start = ((), (), s32[]{:S(2)}) async-start(), calls=%async_computation.3 | async-start | bytes 12255232 | tf_op jit(solution)/shard_map/reduce_scatter | solution.py:172
  767.2 3.3 collective-permute-start.16
  772.7 15.8 %collective-permute-start.17 = (bf16[128,2048]{1,0:T(8,128)(2,1)S(1)}, bf16[128,2048]{1,0:T(8,128)(2,1)S(1)}, u32[]{:S(2)}, u32[]{:S(2)}) collective-permute-start(bf16[128,2048]{1,0:T(8,128)(2,1)S(1)} %fusion.177), channel_id=1, source_target_pairs={{0,2},{2,0},{1,3},{3,1},{4,6},{6,4},{5,7},{7,5},{8,10},{10,8},{9,1... | collective-permute-start | bytes 1572872 | tf_op jit(solution)/shard_map/ppermute | solution.py:134
  790.2 6.2 collective-permute-start.18
  796.4 4.0 collective-permute-start.19
  800.5 7.7 collective-permute-start.20
  808.2 4.0 collective-permute-start.21
  812.2 5.7 collective-permute-start.22
  817.9 5.4 collective-permute-start.23
  826.6 7.3 collective-permute-start.27
  831.8 7.8 collective-permute-start.25
  926.9 9.9 %collective-permute-start.26 = (bf16[64,2816]{1,0:T(8,128)(2,1)S(1)}, bf16[64,2816]{1,0:T(8,128)(2,1)S(1)}, u32[]{:S(2)}, u32[]{:S(2)}) collective-permute-start(bf16[64,2816]{1,0:T(8,128)(2,1)S(1)} %slice.441), channel_id=1, source_target_pairs={{0,64},{64,0},{1,65},{65,1},{2,66},{66,2},{3,67},{67,3},{4,68},{68... | collective-permute-start | bytes 1081352 | tf_op jit(solution)/shard_map/ppermute | solution.py:134
  (124 other events, 1871.6 us)
Sparse Core Ops, SparseCore 0:
  20.7 75.9 all-gather.4
  98.8 113.7 all-gather.6
  470.2 80.9 reduce-scatter.7
  744.2 86.4 reduce-scatter.9
  834.4 91.3 reduce-scatter.5

commit v2 on v1

v2 whole, which is shorter than its diff:
```python
from functools import partial

import jax
import jax.numpy as jnp
from jax import lax
from jax.experimental import pallas as pl
from jax.experimental.pallas import tpu as pltpu
from jax.sharding import Mesh, PartitionSpec as P

DK = 128
DV = 256
CONV = 4
EPSILON = 1e-06
MIXER_FLOOR = 0.001
SPAN = 128
HEADS = 2
CHUNKS = 4
ROWS = SPAN * CHUNKS
QK = HEADS * DK
VW = HEADS * DV
CONVW = 2 * QK + VW
SMALL = 128
SMALL_AT = VW + CONVW
PROJ = SMALL_AT + SMALL
GATE_BLOCKS = VW // 128
Q_BLOCK = VW // 128
K_BLOCK = Q_BLOCK + HEADS
PAIRS = [(n, h) for n in range(CHUNKS) for h in range(HEADS)]
F32 = jnp.float32
BF16 = jnp.bfloat16


def contract(left, right, dims):
    return lax.dot_general(left, right, (dims, ((), ())), preferred_element_type=F32)


def halves(values):
    high = values.astype(BF16)
    return high, (values - high.astype(F32)).astype(BF16)


def dot_parts(left, right, dims):
    (lh, ll), (rh, rl) = left, right
    return contract(lh, rh, dims) + (contract(lh, rl, dims) + contract(ll, rh, dims))


NN = ((1,), (0,))
NT = ((1,), (1,))


def mm(left, right):
    return dot_parts(halves(left), halves(right), NN)


def mm_t(left, right):
    return dot_parts(halves(left), halves(right), NT)


def mm_exact(left, right):
    return lax.dot_general(
        left, right, (NN, ((), ())), precision=lax.Precision.HIGHEST, preferred_element_type=F32
    )


def iota(shape, axis):
    return lax.broadcasted_iota(jnp.int32, shape, axis)


def segment(position, first, second):
    return jnp.where(position >= first, 1, 0) + jnp.where(position >= second, 1, 0)


def silu(values):
    return values * jax.nn.sigmoid(values)


def silu_slope(values):
    s = jax.nn.sigmoid(values)
    return s * (1.0 + values * (1.0 - s))


def softplus(values):
    return jnp.maximum(values, 0.0) + jnp.log1p(jnp.exp(-jnp.abs(values)))


def invert_all(lowers):
    r, c = iota((SPAN, SPAN), 0), iota((SPAN, SPAN), 1)
    eye = jnp.where(r == c, 1.0, 0.0)
    near = (r >> 3) == (c >> 3)
    diag = [jnp.where(near, a, 0.0) for a in lowers]
    diag_parts = [halves(d) for d in diag]
    square = [dot_parts(d, d, NN) for d in diag_parts]
    square_parts = [halves(s) for s in square]
    fourth = [dot_parts(s, s, NN) for s in square_parts]
    inverse = [eye - d for d in diag]
    inverse = [x + dot_parts(halves(x), s, NN) for x, s in zip(inverse, square_parts)]
    inverse = [x + mm(x, s) for x, s in zip(inverse, fourth)]
    shift = 3
    while (1 << shift) < SPAN:
        corner = ((r >> (shift + 1)) == (c >> (shift + 1))) & ((r >> shift) != (c >> shift))
        parts = [halves(x) for x in inverse]
        moved = [
            dot_parts(halves(jnp.where(corner, a, 0.0)), x, NN) for a, x in zip(lowers, parts)
        ]
        inverse = [
            x - dot_parts(p, halves(m), NN) for x, p, m in zip(inverse, parts, moved)
        ]
        shift += 1
    return inverse


def chunk(n):
    return slice(n * SPAN, (n + 1) * SPAN)


def lanes(index, width=128):
    return slice(index * width, (index + 1) * width)


def row_scale(values):
    return lax.rsqrt(jnp.sum(values * values, axis=1, keepdims=True) + EPSILON)


def decay_terms(n, small, bias, rate, first, second):
    betas = jax.nn.sigmoid(small)
    decays = -rate * softplus(small + bias)
    r, c = iota((SPAN, SPAN), 0), iota((SPAN, SPAN), 1)
    total = mm_exact(jnp.where(c <= r, 1.0, 0.0), decays)
    turned = total.T
    position = iota((SPAN, 1), 0) + n * SPAN
    own = segment(position, first, second)
    ends = jnp.int32(n * SPAN + SPAN - 1)
    last = own == segment(ends, first, second)
    terms = []
    for h in range(HEADS):
        column = total[:, HEADS + h : HEADS + h + 1]
        if n:
            carried = own == segment(jnp.int32(n * SPAN - 1), first, second)
            growth = jnp.where(carried, jnp.exp(column), 0.0)
        else:
            growth = jnp.zeros((SPAN, 1), F32)
        final = column[SPAN - 1 : SPAN]
        fade = jnp.where(last, jnp.exp(jnp.where(last, final - column, 0.0)), 0.0)
        terms.append((betas[:, h : h + 1], column, turned[HEADS + h : HEADS + h + 1], growth, fade))
    return terms


def same_segment(n, first, second):
    r, c = iota((SPAN, SPAN), 0), iota((SPAN, SPAN), 1)
    base = n * SPAN
    return (segment(r + base, first, second) == segment(c + base, first, second)) & (c <= r)


def mixer_forward_kernel(
    bounds, raw, taps, vectors, gain, gated, conv, ratios, inner, scores, solved, written, states, mixed
):
    first, second = bounds[0], bounds[1]
    bias, rate = vectors[0:1], vectors[1:2]
    queries, keys, values, terms = {}, {}, {}, {}
    for n in range(CHUNKS):
        rows = chunk(n)
        position = iota((SPAN, 1), 0) + n * SPAN
        own = segment(position, first, second)
        joins = [
            jnp.where((position >= o) & (segment(position - o, first, second) == own), 1.0, 0.0)
            for o in range(1, CONV)
        ]

        def convolved(block):
            here = raw[rows, lanes(GATE_BLOCKS + block)]
            summed = here * taps[CONV - 1 : CONV, lanes(block)]
            for o in range(1, CONV):
                if n:
                    moved = raw[n * SPAN - o : (n + 1) * SPAN - o, lanes(GATE_BLOCKS + block)]
                else:
                    moved = pltpu.roll(here, o, 0)
                tap = taps[CONV - 1 - o : CONV - o, lanes(block)]
                summed = summed + tap * (moved * joins[o - 1])
            conv[rows, lanes(block)] = summed
            return silu(summed)

        for h in range(HEADS):
            q = convolved(Q_BLOCK + h)
            queries[n, h] = q * (row_scale(q) * DK ** (-0.5))
            k = convolved(K_BLOCK + h)
            keys[n, h] = k * row_scale(k)
            values[n, h] = jnp.concatenate(
                [convolved(2 * h), convolved(2 * h + 1)], axis=1
            )
        small = raw[rows, SMALL_AT:PROJ]
        for h, term in enumerate(decay_terms(n, small, bias, rate, first, second)):
            terms[n, h] = term

    r, c = iota((SPAN, SPAN), 0), iota((SPAN, SPAN), 1)
    key_parts = {p: halves(keys[p]) for p in PAIRS}
    query_parts = {p: halves(queries[p]) for p in PAIRS}
    lowers, score = [], {}
    for n in range(CHUNKS):
        causal = same_segment(n, first, second)
        for h in range(HEADS):
            p = (n, h)
            beta, column, row, growth, fade = terms[p]
            ratio = jnp.where(causal, jnp.exp(jnp.where(causal, column - row, 0.0)), 0.0)
            met = dot_parts(key_parts[p], key_parts[p], NT)
            lower = jnp.where(c < r, ratio * met, 0.0)
            score[p] = ratio * dot_parts(query_parts[p], key_parts[p], NT)
            at = n * HEADS + h
            ratios[at] = ratio
            inner[at] = lower
            scores[at] = score[p]
            lowers.append(beta * lower)
    inverses = invert_all(lowers)
    own_part, state_part, key_fade = {}, {}, {}
    for p, x in zip(PAIRS, inverses):
        n, h = p
        beta, column, row, growth, fade = terms[p]
        solved[n * HEADS + h] = x
        parts = halves(x)
        own_part[p] = dot_parts(parts, halves(beta * values[p]), NN)
        state_part[p] = halves(dot_parts(parts, halves((beta * growth) * keys[p]), NN))
        key_fade[p] = halves((fade * keys[p]).T)
    held = [jnp.zeros((DK, DV), F32) for h in range(HEADS)]
    for n in range(CHUNKS):
        for h in range(HEADS):
            p = (n, h)
            growth = terms[p][3]
            states[n * HEADS + h] = held[h]
            state = halves(held[h])
            wrote = own_part[p] - dot_parts(state_part[p], state, NN)
            wrote_parts = halves(wrote)
            written[chunk(n), lanes(h, DV)] = wrote
            out = growth * dot_parts(query_parts[p], state, NN)
            out = out + dot_parts(halves(score[p]), wrote_parts, NN)
            held[h] = growth[SPAN - 1 : SPAN] * held[h] + dot_parts(key_fade[p], wrote_parts, NN)
            mixed[chunk(n), lanes(h, DV)] = out
            scale = lax.rsqrt(jnp.mean(out * out, axis=1, keepdims=True) + MIXER_FLOOR)
            gate = raw[chunk(n), lanes(h, DV)]
            gated[chunk(n), lanes(h, DV)] = (out * scale * gain[...] * silu(gate)).astype(BF16)


def mixer_backward_kernel(
    bounds, grad_mixed, raw, taps, vectors, conv, ratios, inner, scores, solved, written, states,
    grad_raw, grad_taps, grad_vectors, slopes,
):
    first, second = bounds[0], bounds[1]
    bias, rate = vectors[0:1], vectors[1:2]
    r, c = iota((SPAN, SPAN), 0), iota((SPAN, SPAN), 1)
    lane = iota((SPAN, SMALL), 1)
    terms, queries, keys, values, grad_out = {}, {}, {}, {}, {}
    for n in range(CHUNKS):
        rows = chunk(n)
        small = raw[rows, SMALL_AT:PROJ]
        for h, term in enumerate(decay_terms(n, small, bias, rate, first, second)):
            p = (n, h)
            terms[p] = term
            q = silu(conv[rows, lanes(Q_BLOCK + h)])
            queries[p] = q * (row_scale(q) * DK ** (-0.5))
            k = silu(conv[rows, lanes(K_BLOCK + h)])
            keys[p] = k * row_scale(k)
            values[p] = silu(conv[rows, lanes(h, DV)])
            grad_out[p] = grad_mixed[rows, lanes(h, DV)]

    from_out, from_state, into_state, key_turned, out_parts = {}, {}, {}, {}, {}
    for p in PAIRS:
        n, h = p
        at = n * HEADS + h
        beta, column, row, growth, fade = terms[p]
        turned = halves(solved[at].T)
        out_parts[p] = halves(grad_out[p])
        pulled = dot_parts(halves(scores[at].T), out_parts[p], NN)
        from_out[p] = dot_parts(turned, halves(pulled), NN)
        from_state[p] = halves(dot_parts(turned, halves(fade * keys[p]), NN))
        into_state[p] = mm(queries[p].T, growth * grad_out[p])
        key_turned[p] = halves(((beta * growth) * keys[p]).T)
    held = [jnp.zeros((DK, DV), F32) for h in range(HEADS)]
    grad_target, grad_held, grad_held_parts = {}, {}, {}
    for n in reversed(range(CHUNKS)):
        for h in range(HEADS):
            p = (n, h)
            growth = terms[p][3]
            grad_held[p] = held[h]
            grad_held_parts[p] = halves(held[h])
            target = from_out[p] + dot_parts(from_state[p], grad_held_parts[p], NN)
            grad_target[p] = halves(target), target
            kept = growth[SPAN - 1 : SPAN] * held[h] + into_state[p]
            held[h] = kept - dot_parts(key_turned[p], grad_target[p][0], NN)

    log_sum = jnp.zeros((1, SMALL), F32)
    bias_sum = jnp.zeros((1, SMALL), F32)
    for n in range(CHUNKS):
        rows = chunk(n)
        grad_total = jnp.zeros((SPAN, SMALL), F32)
        grad_beta = jnp.zeros((SPAN, SMALL), F32)
        for h in range(HEADS):
            p = (n, h)
            at = n * HEADS + h
            beta, column, row, growth, fade = terms[p]
            target_parts, target = grad_target[p]
            state = states[at]
            state_parts = halves(state)
            wrote_parts = halves(written[rows, lanes(h, DV)])
            q, k, v = queries[p], keys[p], values[p]
            q_parts, k_parts = halves(q), halves(k)
            score, lower, ratio = scores[at], inner[at], ratios[at]
            out_state = dot_parts(out_parts[p], state_parts, NT)
            target_state = dot_parts(target_parts, state_parts, NT)
            wrote_state = dot_parts(wrote_parts, grad_held_parts[p], NT)
            grad_score = dot_parts(out_parts[p], wrote_parts, NT)
            grad_lower = -dot_parts(target_parts, wrote_parts, NT)
            grad_met = beta * grad_lower * jnp.where(c < r, ratio, 0.0)
            grad_pair = grad_score * ratio
            recall = jnp.sum(target_state * k, axis=1, keepdims=True)
            grad_growth = jnp.sum(out_state * q, axis=1, keepdims=True) - beta * recall
            beta_col = jnp.sum(target * v, axis=1, keepdims=True) - growth * recall
            beta_col = beta_col + jnp.sum(grad_lower * lower, axis=1, keepdims=True)
            faded = jnp.sum(wrote_state * k, axis=1, keepdims=True) * fade
            grad_q = growth * out_state + dot_parts(halves(grad_pair), k_parts, NN)
            grad_k = fade * wrote_state - (beta * growth) * target_state
            grad_k = grad_k + dot_parts(halves(grad_pair.T), q_parts, NN)
            grad_k = grad_k + dot_parts(halves(grad_met + grad_met.T), k_parts, NN)
            grad_v = beta * target
            held_grad = jnp.sum(state * grad_held[p], axis=1, keepdims=True)
            at_end = jnp.sum(held_grad, axis=0, keepdims=True) * growth[SPAN - 1 : SPAN]
            at_end = at_end + jnp.sum(faded, axis=0, keepdims=True)
            moved = grad_score * score + beta * (grad_lower * lower)
            col = jnp.sum(moved, axis=1, keepdims=True) - jnp.sum(moved.T, axis=1, keepdims=True)
            col = col + grad_growth * growth - faded
            col = col + jnp.where(iota((SPAN, 1), 0) == SPAN - 1, at_end, 0.0)
            grad_total = jnp.where(lane == HEADS + h, col, grad_total)
            grad_beta = jnp.where(lane == h, beta_col, grad_beta)
            pre = conv[rows, lanes(Q_BLOCK + h)]
            raw_q = silu(pre)
            scale = row_scale(raw_q)
            along = jnp.sum(grad_q * raw_q, axis=1, keepdims=True)
            back = (grad_q - raw_q * ((scale * scale) * along)) * (scale * DK ** (-0.5))
            slopes[rows, lanes(Q_BLOCK + h)] = back * silu_slope(pre)
            pre = conv[rows, lanes(K_BLOCK + h)]
            raw_k = silu(pre)
            scale = row_scale(raw_k)
            along = jnp.sum(grad_k * raw_k, axis=1, keepdims=True)
            back = (grad_k - raw_k * ((scale * scale) * along)) * scale
            slopes[rows, lanes(K_BLOCK + h)] = back * silu_slope(pre)
            wide = lanes(h, DV)
            slopes[rows, wide] = grad_v * silu_slope(conv[rows, wide])
        grad_decays = mm_exact(jnp.where(c >= r, 1.0, 0.0), grad_total)
        small = raw[rows, SMALL_AT:PROJ]
        shifted = small + bias
        grad_step = -grad_decays * rate * jax.nn.sigmoid(shifted)
        betas = jax.nn.sigmoid(small)
        grad_raw[rows, CONVW : CONVW + SMALL] = (
            grad_beta * betas * (1.0 - betas) + grad_step
        ).astype(BF16)
        bias_sum = bias_sum + jnp.sum(grad_step, axis=0, keepdims=True)
        log_sum = log_sum - jnp.sum(
            grad_decays * rate * softplus(shifted), axis=0, keepdims=True
        )
    grad_vectors[0:1] = log_sum
    grad_vectors[1:2] = bias_sum

    slopes[ROWS : ROWS + 8] = jnp.zeros((8, CONVW), F32)
    for block in range(CONVW // 128):
        sums = [jnp.zeros((1, 128), F32) for o in range(CONV)]
        for n in range(CHUNKS):
            rows = chunk(n)
            position = iota((SPAN, 1), 0) + n * SPAN
            own = segment(position, first, second)
            here = raw[rows, lanes(GATE_BLOCKS + block)]
            total = jnp.zeros((SPAN, 128), F32)
            for o in range(CONV):
                moved = slopes[n * SPAN + o : (n + 1) * SPAN + o, lanes(block)]
                if o:
                    moved = jnp.where(segment(position + o, first, second) == own, moved, 0.0)
                total = total + taps[CONV - 1 - o : CONV - o, lanes(block)] * moved
                sums[o] = sums[o] + jnp.sum(moved * here, axis=0, keepdims=True)
            grad_raw[rows, lanes(block)] = total.astype(BF16)
        for o in range(CONV):
            grad_taps[CONV - 1 - o : CONV - o, lanes(block)] = sums[o]


def vmem(count):
    return [pl.BlockSpec(memory_space=pltpu.VMEM)] * count


LIMIT = pltpu.CompilerParams(vmem_limit_bytes=56 * 1024 * 1024)
SMEM = pl.BlockSpec(memory_space=pltpu.SMEM)
SAVED = [
    jax.ShapeDtypeStruct((ROWS, CONVW), F32),
    jax.ShapeDtypeStruct((len(PAIRS), SPAN, SPAN), F32),
    jax.ShapeDtypeStruct((len(PAIRS), SPAN, SPAN), F32),
    jax.ShapeDtypeStruct((len(PAIRS), SPAN, SPAN), F32),
    jax.ShapeDtypeStruct((len(PAIRS), SPAN, SPAN), F32),
    jax.ShapeDtypeStruct((ROWS, VW), F32),
    jax.ShapeDtypeStruct((len(PAIRS), DK, DV), F32),
    jax.ShapeDtypeStruct((ROWS, VW), F32),
]


def mixer_forward(bounds, raw, taps, vectors, gain):
    outs = [jax.ShapeDtypeStruct((ROWS, VW), BF16)] + SAVED
    return pl.pallas_call(
        mixer_forward_kernel,
        out_shape=outs,
        in_specs=[SMEM] + vmem(4),
        out_specs=vmem(len(outs)),
        compiler_params=LIMIT,
        name="mixer_forward",
    )(bounds, raw, taps, vectors, gain)


def mixer_backward(bounds, grad_mixed, raw, taps, vectors, saved):
    outs = [
        jax.ShapeDtypeStruct((ROWS, CONVW + SMALL), BF16),
        jax.ShapeDtypeStruct((8, CONVW), F32),
        jax.ShapeDtypeStruct((8, SMALL), F32),
    ]
    return pl.pallas_call(
        mixer_backward_kernel,
        out_shape=outs,
        in_specs=[SMEM] + vmem(4 + len(saved)),
        out_specs=vmem(len(outs)),
        scratch_shapes=[pltpu.VMEM((ROWS + 8, CONVW), F32)],
        compiler_params=LIMIT,
        name="mixer_backward",
    )(bounds, grad_mixed, raw, taps, vectors, *saved)


TN = ((0,), (0,))
OWN = ROWS // 4
TILE = 512
STEP = 512
WIDE = 384


def whole(*shape):
    return pl.BlockSpec(shape, lambda i: (0,) * len(shape))


def place_rows(places, j):
    return pl.ds(pl.multiple_of(places[j] * OWN, OWN), OWN)


def project_kernel(places, x0, x1, x2, x3, small, weights, raw, normed, gains, steps):
    step = pl.program_id(0)

    @pl.when(step == 0)
    def prepare():
        r, c = iota((8, SMALL), 0), iota((8, SMALL), 1)
        pick = jnp.where((r < 2) & (c == r + 2 * HEADS), 1.0, 0.0).astype(BF16)
        gains[...] = contract(pick, small[...], NT)
        for j, x in enumerate((x0, x1, x2, x3)):
            values = x[...].astype(F32)
            scale = lax.rsqrt(jnp.mean(values * values, axis=1, keepdims=True) + EPSILON)
            low = (values * scale * gains[0:1]).astype(BF16)
            rows = place_rows(places, j)
            normed[rows, :] = low
            for s in range(steps.shape[0]):
                steps[s, rows, :] = low[:, s * STEP : (s + 1) * STEP]

    product = contract(steps[step], weights[:, VW:], NN)

    @pl.when(step == 0)
    def start():
        raw[...] = product

    @pl.when(step > 0)
    def add():
        raw[...] += product


def project(places, blocks, weights):
    features = weights.shape[0]
    count = features // STEP
    return pl.pallas_call(
        project_kernel,
        grid=(count,),
        out_shape=[
            jax.ShapeDtypeStruct((ROWS, PROJ), F32),
            jax.ShapeDtypeStruct((ROWS, features), BF16),
            jax.ShapeDtypeStruct((8, features), F32),
        ],
        in_specs=[SMEM]
        + [whole(OWN, features)] * 4
        + [
            pl.BlockSpec((features, SMALL), lambda i: (0, (VW + SMALL_AT) // SMALL)),
            pl.BlockSpec((STEP, weights.shape[1]), lambda i: (i, 0)),
        ],
        out_specs=[whole(ROWS, PROJ), whole(ROWS, features), whole(8, features)],
        scratch_shapes=[pltpu.VMEM((count, ROWS, STEP), BF16)],
        compiler_params=LIMIT,
        name="project",
    )(places, *blocks, weights, weights)


def split_rows(product, kept_own, kept_other, sent_own, sent_other):
    kept_own[...] = product[:OWN]
    kept_other[...] = product[OWN : 2 * OWN]
    sent_own[...] = product[2 * OWN : 3 * OWN].astype(BF16)
    sent_other[...] = product[3 * OWN :].astype(BF16)


def split_outs(features):
    shape = (OWN, features)
    outs = [jax.ShapeDtypeStruct(shape, F32)] * 2 + [jax.ShapeDtypeStruct(shape, BF16)] * 2
    return outs, [pl.BlockSpec((OWN, TILE), lambda i: (0, i))] * 4


def mix_out_kernel(places, gated, weights, kept_own, kept_other, sent_own, sent_other, turned):
    @pl.when(pl.program_id(0) == 0)
    def prepare():
        for j in range(4):
            turned[j * OWN : (j + 1) * OWN] = gated[place_rows(places, j), :]

    split_rows(
        contract(turned[...], weights[...], NT), kept_own, kept_other, sent_own, sent_other
    )


def mix_out(places, gated, weights):
    features = weights.shape[0]
    outs, specs = split_outs(features)
    return pl.pallas_call(
        mix_out_kernel,
        grid=(features // TILE,),
        out_shape=outs + [jax.ShapeDtypeStruct((ROWS, VW), BF16)],
        in_specs=[SMEM, whole(ROWS, VW), pl.BlockSpec((TILE, VW), lambda i: (i, 0))],
        out_specs=specs + [whole(ROWS, VW)],
        compiler_params=LIMIT,
        name="mix_out",
    )(places, gated, weights)


def gate_up_kernel(x0, x1, x2, x3, weights, act, gate, up, rows, held, *, units):
    step = pl.program_id(0)

    for j, x in enumerate((x0, x1, x2, x3)):

        @pl.when(step == 0)
        def prepare():
            held[j * OWN : (j + 1) * OWN] = x[...]

        @pl.when(step == j)
        def keep():
            rows[...] = x[...]

    for q in range(WIDE // 128):

        @pl.when(step * WIDE + q * 128 < units)
        def pair():
            product = contract(held[...], weights[:, lanes(q, 256)], NN)
            gate_in, up_in = product[:, :128], product[:, 128:]
            gate[:, lanes(q)] = gate_in
            up[:, lanes(q)] = up_in
            act[:, lanes(q)] = (silu(gate_in) * up_in).astype(BF16)


def gate_up(blocks, weights, units):
    features = weights.shape[0]
    tile = pl.BlockSpec((ROWS, WIDE), lambda i: (0, i))
    return pl.pallas_call(
        partial(gate_up_kernel, units=units),
        grid=(pl.cdiv(units, WIDE),),
        out_shape=[
            jax.ShapeDtypeStruct((ROWS, units), BF16),
            jax.ShapeDtypeStruct((ROWS, units), F32),
            jax.ShapeDtypeStruct((ROWS, units), F32),
            jax.ShapeDtypeStruct((ROWS, features), BF16),
        ],
        in_specs=[whole(OWN, features)] * 4
        + [pl.BlockSpec((features, 2 * WIDE), lambda i: (0, i))],
        out_specs=[
            tile,
            tile,
            tile,
            pl.BlockSpec((OWN, features), lambda i: (jnp.minimum(i, 3), 0)),
        ],
        scratch_shapes=[pltpu.VMEM((ROWS, features), BF16)],
        compiler_params=LIMIT,
        name="gate_up",
    )(*blocks, weights)


def rows_back_kernel(left, weights, kept_own, kept_other, sent_own, sent_other):
    split_rows(contract(left[...], weights[...], NT), kept_own, kept_other, sent_own, sent_other)


def rows_back(left, weights, block, name):
    features = weights.shape[0]
    width = left.shape[1]
    outs, specs = split_outs(features)
    return pl.pallas_call(
        rows_back_kernel,
        grid=(features // TILE,),
        out_shape=outs,
        in_specs=[whole(ROWS, width), pl.BlockSpec((TILE, width), lambda i: (i, block))],
        out_specs=specs,
        compiler_params=LIMIT,
        name=name,
    )(left, weights)


def act_back_kernel(x0, x1, x2, x3, weights, gate, up, grads, rows, steps, total, gates, ups):
    step = pl.program_id(0)

    for j, x in enumerate((x0, x1, x2, x3)):
        at = slice(j * OWN, (j + 1) * OWN)

        @pl.when(step == 0)
        def prepare():
            for s in range(steps.shape[0]):
                steps[s, at, :] = x[:, s * STEP : (s + 1) * STEP]

        @pl.when(step == j)
        def keep():
            rows[...] = x[...]
            gates[at] = gate[...]
            ups[at] = up[...]

    product = contract(steps[step], weights[...], NN)

    @pl.when(step == 0)
    def start():
        total[...] = product

    @pl.when(step > 0)
    def add():
        total[...] += product

    @pl.when(step == pl.num_programs(0) - 1)
    def finish():
        for b in range(total.shape[1] // 128):
            grad, gate_in, up_in = total[:, lanes(b)], gates[:, lanes(b)], ups[:, lanes(b)]
            s = jax.nn.sigmoid(gate_in)
            grads[:, lanes(2 * b)] = (grad * up_in * s * (1.0 + gate_in * (1.0 - s))).astype(BF16)
            grads[:, lanes(2 * b + 1)] = (grad * gate_in * s).astype(BF16)


def act_back(blocks, weights, gate, up):
    features = weights.shape[0]
    units = gate.shape[1]
    count = features // STEP
    part = pl.BlockSpec((OWN, units), lambda i: (i, 0))
    return pl.pallas_call(
        act_back_kernel,
        grid=(count,),
        out_shape=[
            jax.ShapeDtypeStruct((ROWS, 2 * units), BF16),
            jax.ShapeDtypeStruct((ROWS, features), BF16),
        ],
        in_specs=[whole(OWN, features)] * 4
        + [pl.BlockSpec((STEP, units), lambda i: (i, 2)), part, part],
        out_specs=[
            whole(ROWS, 2 * units),
            pl.BlockSpec((OWN, features), lambda i: (i, 0)),
        ],
        scratch_shapes=[
            pltpu.VMEM((count, ROWS, STEP), BF16),
            pltpu.VMEM((ROWS, units), F32),
            pltpu.VMEM((ROWS, units), F32),
            pltpu.VMEM((ROWS, units), F32),
        ],
        compiler_params=LIMIT,
        name="act_back",
    )(*blocks, weights, gate, up)


def gated_back_kernel(
    places, x0, x1, x2, x3, weights, raw_gate, mixed, gain, grad_mixed, grad_gate, grad_gain, turned
):
    gain_sum = jnp.zeros((1, DV), F32)
    for j, x in enumerate((x0, x1, x2, x3)):
        turned[j * OWN : (j + 1) * OWN] = x[...]
        grads = contract(x[...], weights[...], NN)
        rows = place_rows(places, j)
        for h in range(HEADS):
            out = mixed[rows, lanes(h, DV)]
            gate = raw_gate[rows, lanes(h, DV)]
            grad = grads[:, lanes(h, DV)]
            scale = lax.rsqrt(jnp.mean(out * out, axis=1, keepdims=True) + MIXER_FLOOR)
            opened = grad * silu(gate)
            scaled = out * scale
            gain_sum = gain_sum + jnp.sum(opened * scaled, axis=0, keepdims=True)
            grad_gate[rows, lanes(h, DV)] = (
                grad * scaled * gain[...] * silu_slope(gate)
            ).astype(BF16)
            inward = opened * gain[...]
            along = jnp.mean(inward * out, axis=1, keepdims=True)
            grad_mixed[rows, lanes(h, DV)] = scale * inward - out * (
                (scale * scale * scale) * along
            )
    grad_gain[0:1] = gain_sum


def gated_back(places, blocks, weights, raw, mixed, gain):
    features = weights.shape[0]
    return pl.pallas_call(
        gated_back_kernel,
        grid=(1,),
        out_shape=[
            jax.ShapeDtypeStruct((ROWS, VW), F32),
            jax.ShapeDtypeStruct((ROWS, VW), BF16),
            jax.ShapeDtypeStruct((8, DV), F32),
            jax.ShapeDtypeStruct((ROWS, features), BF16),
        ],
        in_specs=[SMEM]
        + [whole(OWN, features)] * 4
        + [whole(features, VW), whole(ROWS, VW), whole(ROWS, VW), whole(1, DV)],
        out_specs=[whole(ROWS, VW), whole(ROWS, VW), whole(8, DV), whole(ROWS, features)],
        compiler_params=LIMIT,
        name="gated_back",
    )(places, *blocks, weights, raw, mixed, gain)


def input_back_kernel(
    places, gate, conv, weights, kept_own, kept_other, sent_own, sent_other, turned
):
    @pl.when(pl.program_id(0) == 0)
    def prepare():
        for j in range(4):
            rows = place_rows(places, j)
            turned[j * OWN : (j + 1) * OWN, :VW] = gate[rows, :]
            turned[j * OWN : (j + 1) * OWN, VW:] = conv[rows, :]

    split_rows(
        contract(turned[...], weights[:, VW:], NT), kept_own, kept_other, sent_own, sent_other
    )


def input_back(places, gate, conv, weights):
    features = weights.shape[0]
    outs, specs = split_outs(features)
    return pl.pallas_call(
        input_back_kernel,
        grid=(features // TILE,),
        out_shape=outs,
        in_specs=[
            SMEM,
            whole(ROWS, VW),
            whole(ROWS, CONVW + SMALL),
            pl.BlockSpec((TILE, weights.shape[1]), lambda i: (i, 0)),
        ],
        out_specs=specs,
        scratch_shapes=[pltpu.VMEM((ROWS, PROJ), BF16)],
        compiler_params=LIMIT,
        name="input_back",
    )(places, gate, conv, weights)


def grads_kernel(count, *refs):
    out = refs[-1]
    at = 0
    for i in range(count):
        left, right = refs[2 * i], refs[2 * i + 1]
        width = right.shape[1]
        out[:, at : at + width] = contract(left[...], right[...], TN).astype(BF16)
        at += width


def weight_grads(pairs, name):
    features = pairs[0][0].shape[1]
    width = sum(right.shape[1] for left, right in pairs)
    specs = []
    for left, right in pairs:
        specs += [pl.BlockSpec((ROWS, STEP), lambda i: (0, i)), whole(ROWS, right.shape[1])]
    return pl.pallas_call(
        partial(grads_kernel, len(pairs)),
        grid=(features // STEP,),
        out_shape=jax.ShapeDtypeStruct((features, width), BF16),
        in_specs=specs,
        out_specs=pl.BlockSpec((STEP, width), lambda i: (i, 0)),
        compiler_params=LIMIT,
        name=name,
    )(*[operand for pair in pairs for operand in pair])


SWAP = [(0, 1), (1, 0)]
PLANE = ("z", "y")


def trade(values, axis):
    return lax.ppermute(values, axis, SWAP)


def gather_tokens(own):
    across = trade(own, "xh")
    return own, across, trade(own, "c"), trade(across, "c")


def scatter_tokens(kept_own, kept_other, sent_own, sent_other):
    other = kept_other + trade(sent_other, "c").astype(jnp.float32)
    own = kept_own + trade(sent_own, "c").astype(jnp.float32)
    return own + trade(other.astype(jnp.bfloat16), "xh").astype(jnp.float32)


def gather_weights(*blocks):
    other = jnp.concatenate([trade(block, "xl") for block in blocks], axis=1)
    both = jnp.stack([jnp.concatenate(blocks, axis=1), other], axis=0)
    full = lax.all_gather(both, PLANE, axis=0, tiled=False)
    return full.reshape(-1, other.shape[1])


def scatter_grads(grads):
    both = lax.psum_scatter(grads, PLANE, scatter_dimension=0, tiled=True)
    both = both.reshape(2, -1, grads.shape[1])
    return both[0].astype(jnp.float32) + trade(both[1], "xl").astype(jnp.float32)


def features_in(rows):
    count = rows.shape[0]
    halves = rows.reshape(count, 2, -1)
    flip = lax.axis_index("xl") == 1
    first = jnp.where(flip, halves[:, 1], halves[:, 0]).reshape(count, 16, 64)
    second = jnp.where(flip, halves[:, 0], halves[:, 1]).reshape(count, 16, 64)
    return jnp.concatenate([first, second], axis=2).reshape(count, -1)


def features_out(rows):
    count = rows.shape[0]
    blocks = rows.reshape(count, 16, 2, 64)
    flip = lax.axis_index("xl") == 1
    first = blocks[:, :, 0].reshape(count, -1)
    second = blocks[:, :, 1].reshape(count, -1)
    low = jnp.where(flip, second, first)
    high = jnp.where(flip, first, second)
    return jnp.concatenate([low, high], axis=1)


def sum_over(values, axes):
    for axis in axes:
        size = lax.axis_size(axis)
        step = 1
        while step < size:
            values = values + lax.ppermute(values, axis, [(i, i ^ step) for i in range(size)])
            step *= 2
    return values


def shards(
    layer_input,
    teacher_out,
    lengths,
    norm1_gain,
    query_weight,
    key_weight,
    value_weight,
    output_gate,
    beta_weight,
    decay_weight,
    decay_log,
    step_bias,
    query_taps,
    key_taps,
    value_taps,
    mixer_gain,
    out_weight,
    norm2_gain,
    gate_weight,
    up_weight,
    down_weight,
):
    tok_rows = layer_input.shape[0]
    rows_dp = norm1_gain.shape[0]
    group_index = lax.axis_index("xl") * 16 + lax.axis_index("z") * 4 + lax.axis_index("y")
    half, core = lax.axis_index("xh"), lax.axis_index("c")
    tensor_index = half * 2 + core
    places = jnp.stack(
        [tensor_index, 2 - 2 * half + core, 2 * half + 1 - core, 3 - tensor_index]
    ).astype(jnp.int32)
    heads_here = decay_log.shape[0]
    own_lengths = lax.dynamic_index_in_dim(lengths, group_index, 0, keepdims=False)
    boundary = jnp.cumsum(own_lengths)
    own_rows = tensor_index * tok_rows + jnp.arange(tok_rows, dtype=jnp.int32)
    validity = (own_rows < boundary[-1]).astype(jnp.float32)[:, None]
    loss_scale = jnp.float32(128 * tok_rows) / jnp.sum(lengths).astype(jnp.float32)

    qk_width = query_taps.shape[1]
    v_width = value_taps.shape[1]
    f_width = gate_weight.shape[1]
    filler = jnp.zeros((rows_dp, SMALL - 2 * heads_here - 2), jnp.bfloat16)
    mixer_block = jnp.concatenate(
        [out_weight, output_gate, value_weight, query_weight, key_weight], axis=1
    )
    small_block = jnp.concatenate(
        [beta_weight, decay_weight, norm1_gain[:, None], norm2_gain[:, None], filler], axis=1
    )
    paired_units = jnp.stack(
        [gate_weight.reshape(rows_dp, -1, 128), up_weight.reshape(rows_dp, -1, 128)], axis=2
    ).reshape(rows_dp, 2 * f_width)
    mixer_full = gather_weights(mixer_block, small_block)
    ffn_full = gather_weights(jnp.concatenate([paired_units, down_weight], axis=1))
    input_own = features_in(layer_input)
    teacher_own = features_in(teacher_out).astype(jnp.float32)
    conv_taps = jnp.concatenate([value_taps, query_taps, key_taps], axis=1).astype(jnp.float32)
    vectors = jnp.pad(
        jnp.stack([step_bias, jnp.exp(decay_log)]),
        ((0, 6), (heads_here, SMALL - 2 * heads_here)),
    )
    gain_mixer = mixer_gain.astype(jnp.float32)[None, :]

    input_blocks = gather_tokens(input_own)
    raw, normed_one, gains = project(places, input_blocks, mixer_full)
    gain_first, gain_second = gains[0:1], gains[1:2]
    input_float = input_own.astype(jnp.float32)
    scale_one = lax.rsqrt(jnp.mean(input_float * input_float, axis=-1, keepdims=True) + EPSILON)
    gated_low, *saved, mixed = mixer_forward(boundary, raw, conv_taps, vectors, gain_mixer)
    *terms, gated_turned = mix_out(places, gated_low, mixer_full)
    hidden = input_float + scatter_tokens(*terms)
    scale_two = lax.rsqrt(jnp.mean(hidden * hidden, axis=-1, keepdims=True) + EPSILON)
    normed_two = (hidden * scale_two * gain_second).astype(jnp.bfloat16)
    act_low, gate_in, up_in, normed_rows = gate_up(gather_tokens(normed_two), ffn_full, f_width)
    layer_out = hidden + scatter_tokens(*rows_back(act_low, ffn_full, 2, "down"))
    grad_layer = loss_scale * validity * (layer_out - teacher_own)
    grad_gate_up, grad_rows = act_back(
        gather_tokens(grad_layer.astype(jnp.bfloat16)), ffn_full, gate_in, up_in
    )
    units_grad = weight_grads([(normed_rows, grad_gate_up)], "units_grads")
    units_grad, grad_gate_up = lax.optimization_barrier((units_grad, grad_gate_up))
    units_sum = scatter_grads(units_grad)
    grad_normed_two = scatter_tokens(*rows_back(grad_gate_up, ffn_full, 0, "normed_back"))

    weighted_two = gain_second * grad_normed_two
    grad_gain_two = jnp.sum(grad_normed_two * hidden * scale_two, axis=0)
    grad_hidden = (
        grad_layer
        + scale_two * weighted_two
        - hidden
        * (scale_two * scale_two * scale_two)
        * jnp.mean(weighted_two * hidden, axis=-1, keepdims=True)
    )
    grad_mixed, gate_low, gain_grad, grad_turned = gated_back(
        places, gather_tokens(grad_hidden.astype(jnp.bfloat16)), mixer_full, raw, mixed, gain_mixer
    )
    raw_low, taps_grad, vectors_grad = mixer_backward(
        boundary, grad_mixed, raw, conv_taps, vectors, saved
    )
    last_grad = weight_grads(
        [
            (grad_turned, gated_turned),
            (normed_one, gate_low),
            (normed_one, raw_low),
            (grad_rows, act_low),
        ],
        "mixer_grads",
    )
    last_grad, raw_low = lax.optimization_barrier((last_grad, raw_low))
    last_sum = scatter_grads(last_grad)
    grad_normed_one = scatter_tokens(*input_back(places, gate_low, raw_low, mixer_full))
    weighted_one = gain_first * grad_normed_one
    grad_gain_one = jnp.sum(grad_normed_one * input_float * scale_one, axis=0)
    grad_input = (
        grad_hidden
        + scale_one * weighted_one
        - input_float
        * (scale_one * scale_one * scale_one)
        * jnp.mean(weighted_one * input_float, axis=-1, keepdims=True)
    )

    gain_pair = features_out(jnp.stack([grad_gain_one, grad_gain_two]))
    features = gain_pair.shape[1]
    taps = taps_grad[:CONV]
    n_all = 2 * features + DV
    flat = jnp.concatenate(
        [
            gain_pair.reshape(-1),
            gain_grad[0],
            taps.reshape(-1),
            vectors_grad[:2, heads_here : 2 * heads_here].reshape(-1),
        ]
    )
    flat = jnp.pad(flat, (0, -flat.shape[0] % 1024)).reshape(-1, 128)
    flat = sum_over(flat, ("xl", "z", "y"))
    shared = sum_over(flat[: n_all // 128], ("xh", "c")).reshape(-1)
    flat = flat.reshape(-1)
    taps_sum = flat[n_all : n_all + taps.size].reshape(CONV, -1)
    heads_at = n_all + taps.size
    norm1_grad = lax.dynamic_slice_in_dim(shared, group_index * rows_dp, rows_dp)
    norm2_grad = lax.dynamic_slice_in_dim(shared, features + group_index * rows_dp, rows_dp)
    q_at = 2 * VW + v_width
    k_at = q_at + qk_width
    small_at = k_at + qk_width
    units_sum = units_sum.reshape(rows_dp, -1, 2, 128)
    return (
        features_out(layer_out),
        features_out(grad_input),
        norm1_grad,
        last_sum[:, q_at:k_at],
        last_sum[:, k_at:small_at],
        last_sum[:, 2 * VW : q_at],
        last_sum[:, VW : 2 * VW],
        last_sum[:, small_at : small_at + heads_here],
        last_sum[:, small_at + heads_here : small_at + 2 * heads_here],
        flat[heads_at : heads_at + heads_here],
        flat[heads_at + heads_here : heads_at + 2 * heads_here],
        taps_sum[:, v_width : v_width + qk_width],
        taps_sum[:, v_width + qk_width :],
        taps_sum[:, :v_width],
        shared[2 * features :],
        last_sum[:, :VW],
        norm2_grad,
        units_sum[:, :, 0].reshape(rows_dp, f_width),
        units_sum[:, :, 1].reshape(rows_dp, f_width),
        last_sum[:, VW + PROJ :],
    )


def solution(mesh):
    fine = Mesh(mesh.devices.reshape(2, 4, 4, 2, 2), ("xl", "z", "y", "xh", "c"))
    dp = ("xl", "z", "y")
    tensor = ("xh", "c")
    tokens = P(dp + tensor, None)
    weight = P(dp, tensor)
    gain = P(dp)
    heads = P(tensor)
    taps = P(None, tensor)
    in_specs = (
        (tokens, tokens, P(), gain)
        + (weight,) * 6
        + (heads, heads, taps, taps, taps, P(), weight, gain)
        + (weight,) * 3
    )
    out_specs = (
        (tokens, tokens, gain)
        + (weight,) * 6
        + (heads, heads, taps, taps, taps, P(), weight, gain)
        + (weight,) * 3
    )
    return jax.shard_map(shards, mesh=fine, in_specs=in_specs, out_specs=out_specs, check_vma=False)
```

time: 951 us -> 523 us (0.55)
  other arithmetic: 260 us -> 25.3 us
  matrix products: 187 us -> 0 us
  local copies, waits for them, and re-layouts: 168 us -> 34.5 us
  Pallas kernels: 0 us -> 132 us
    another operation x123 -> x7, other arithmetic: 176 us -> 4.03 us  [the longest x3 1.98 us: gather_weights(): both = jnp.stack([jnp.concatenate(blocks, axis=1), other], axis=0)]
    dot_general x196 -> x0, matrix products: 172 us -> none  [the longest x4 25.4 us: product_t(): jnp.einsum('gf,df->gd', left, right, preferred_element_type=jnp.float32)]
    pallas_call x0 -> x12, Pallas kernels: none -> 132 us  [the longest x2 25 us: weight_grads(): pl.pallas_call(partial(grads_kernel, len(pairs)), grid=(features // STEP,...]
    reduce_scatter x2, waiting for transfers between devices: 84.4 us -> 28.2 us  [scatter_grads(): both = lax.psum_scatter(grads, PLANE, scatter_dimension=0, tiled=True)]
    all_gather x2, waiting for transfers between devices: 40.3 us -> 93.4 us  [gather_weights(): full = lax.all_gather(both, PLANE, axis=0, tiled=False)]
    unnamed x272 -> x89, local copies, waits for them, and re-layouts: 55.1 us -> 12.5 us
    squeeze x48 -> x0, local copies, waits for them, and re-layouts: 22.8 us -> none  [mixer_core(): lax.scan(jax.checkpoint(block_step), initial, (heads_first(queries), head...]
    reduce_sum x38 -> x1, other arithmetic: 18.3 us -> 0.63 us  [shards(): jnp.sum(lengths).astype(jnp.float32)]
  transfers between devices with their start and end apart: 33 -> 40, of which waited for: 26 -> 26; matrix products, arithmetic and copies ran while one was open for 57% -> 9% of each run, Pallas kernels for 0% -> 17%
where the time goes in v2:
time: 523 us; the launch traced here: 518 us
  waiting for transfers between devices  266 us (51%)
  Pallas kernels  132 us (25%)
  starting transfers between devices  45.8 us (9%)
  local copies, waits for them, and re-layouts  34.5 us (7%)
  other arithmetic  25.3 us (5%)
  between operations  15.4 us (3%)
    ppermute x29, waiting for transfers between devices, trade(): return lax.ppermute(values, axis, SWAP)  130 us
    all_gather x2, waiting for transfers between devices, gather_weights(): full = lax.all_gather(both, PLANE, axis=0, tiled=False)  93.4 us
    ppermute x29, starting transfers between devices, trade(): return lax.ppermute(values, axis, SWAP)  33.9 us
    reduce_scatter x2, waiting for transfers between devices, scatter_grads(): both = lax.psum_scatter(grads, PLANE, scatter_dimension=0, tiled=True)  28.2 us
    pallas_call x2, Pallas kernels, weight_grads(): pl.pallas_call(partial(grads_kernel, len(pairs)), grid=(features // STEP,...  25 us
    pallas_call x1, Pallas kernels, mixer_backward(): pl.pallas_call(mixer_backward_kernel, out_shape=outs, in_specs=[SMEM] + v...  18.5 us
    pallas_call x2, Pallas kernels, rows_back(): pl.pallas_call(rows_back_kernel, grid=(features // TILE,), out_shape=outs...  18.2 us
    ppermute x7, waiting for transfers between devices, sum_over(): lax.ppermute(values, axis, [(i, i ^ step) for i in range(size)])  13.9 us
  transfers between devices with their start and end apart: 40, of which 26 were waited for; matrix products, arithmetic and copies ran while one was open for 9% of the time, Pallas kernels for 17%

profile of v2, /device:TPU:0, one launch (start us, length us, event | category | flops | bytes accessed | tf_op | source)
XLA Modules:
  0.0 518.2 jit_solution(9271550886094641878)
XLA Ops:
  23.5 11.7 %collective-permute-done.11 = bf16[64,4224]{1,0:T(8,128)(2,1)S(1)} collective-permute-done((bf16[64,4224]{1,0:T(8,128)(2,1)S(1)}, bf16[64,4224]{1,0:T(8,128)(2,1)S(1)}, u32[]{:S(2)}, u32[]{:S(2)}) %collective-permute-start.11) | collective-permute-done | bytes 540704 | tf_op jit(solution)/shard_map/ppermute | solution.py:780
  37.0 3.0 collective-permute-start
  41.5 8.9 %collective-permute-done.x1 = bf16[128,2048]{1,0:T(8,128)(2,1)S(1)} collective-permute-done((bf16[128,2048]{1,0:T(8,128)(2,1)S(1)}, bf16[128,2048]{1,0:T(8,128)(2,1)S(1)}, u32[]{:S(2)}, u32[]{:S(2)}) %collective-permute-start) | collective-permute-done | bytes 524320 | tf_op jit(solution)/shard_map/ppermute | solution.py:780
  52.6 44.1 %all-gather.5.cloned.1.call-done = bf16[32,64,2176]{2,1,0:T(8,128)(2,1)} async-done(((bf16[2,64,2176]{2,1,0:T(8,128)(2,1)}), bf16[32,64,2176]{2,1,0:T(8,128)(2,1)}) %all-gather.5.cloned.1.call-update) | async-done | bytes 8912912 | tf_op jit(solution)/shard_map/all_gather | solution.py:797
  96.7 11.9 %project.1 = (f32[512,1664]{1,0:T(8,128)}, bf16[512,2048]{1,0:T(8,128)(2,1)}, f32[8,2048]{1,0:T(8,128)}) custom-call(s32[4]{0:T(128)} %pad_add_fusion.places, bf16[128,2048]{1,0:T(8,128)(2,1)} %copy-done, bf16[128,2048]{1,0:T(8,128)(2,1)} %copy-done.11, bf16[128,2048]{1,0:T(8,128)(2,1)} %copy-done.12, bf16[128,2048]{1,0:T(8,128)(2,1)} %copy-done.15, ...), custom_call_target="tpu_custom_call" | custom-call | tf_op jit(solution)/shard_map/project/pallas_call | solution.py:473
  108.7 12.6 %mixer_forward.1 = (bf16[512,512]{1,0:T(8,128)(2,1)}, f32[512,1024]{1,0:T(8,128)}, f32[8,128,128]{2,1,0:T(8,128)}, f32[8,128,128]{2,1,0:T(8,128)}, f32[8,128,128...) custom-call(s32[2]{0:T(128)} %bitcast.110, ...), custom_call_target="tpu_custom_call" | custom-call | tf_op jit(solution)/shard_map/mixer_forward/pallas_call | solution.py:400
  121.3 5.2 mix_out.1
  130.0 3.5 collective-permute-start.7
  134.4 11.6 %collective-permute-done.7 = bf16[128,2048]{1,0:T(8,128)(2,1)S(1)} collective-permute-done((bf16[128,2048]{1,0:T(8,128)(2,1)S(1)}, bf16[128,2048]{1,0:T(8,128)(2,1)S(1)}, u32[]{:S(2)}, u32[]{:S(2)}) %collective-permute-start.7) | collective-permute-done | bytes 524320 | tf_op jit(solution)/shard_map/ppermute | solution.py:780
  149.6 11.7 %collective-permute-done.8.x1 = bf16[128,2048]{1,0:T(8,128)(2,1)S(1)} collective-permute-done((bf16[128,2048]{1,0:T(8,128)(2,1)S(1)}, bf16[128,2048]{1,0:T(8,128)(2,1)S(1)}, u32[]{:S(2)}, u32[]{:S(2)}) %collective-permute-start.8) | collective-permute-done | bytes 524320 | tf_op jit(solution)/shard_map/ppermute | solution.py:780
  163.3 49.3 %all-gather.7.cloned.1.call-done = bf16[32,64,4224]{2,1,0:T(8,128)(2,1)} async-done(((bf16[2,64,4224]{2,1,0:T(8,128)(2,1)}), bf16[32,64,4224]{2,1,0:T(8,128)(2,1)}) %all-gather.7.cloned.1.call-update) | async-done | bytes 17301520 | tf_op jit(solution)/shard_map/all_gather | solution.py:797
  212.6 12.9 %gate_up.1 = (bf16[512,1408]{1,0:T(8,128)(2,1)}, f32[512,1408]{1,0:T(8,128)}, f32[512,1408]{1,0:T(8,128)}, bf16[512,2048]{1,0:T(8,128)(2,1)}) custom-call(bf16[128,2048]{1,0:T(8,128)(2,1)} %copy-done.7, bf16[128,2048]{1,0:T(8,128)(2,1)} %copy-done.13, bf16[128,2048]{1,0:T(8,128)(2,1)} %copy-done.16, bf16[128,2048]{1,0:T(8,128)(2,1)} %collective-permute-done.10.x3, ...), custom_call_target="tpu_custom_call" | custom-call | tf_op jit(solution)/shard_map/gate_up/pallas_call | solution.py:559
  225.5 7.5 %down.1 = (f32[128,2048]{1,0:T(8,128)}, f32[128,2048]{1,0:T(8,128)}, bf16[128,2048]{1,0:T(8,128)(2,1)}, bf16[128,2048]{1,0:T(8,128)(2,1)}) custom-call(bf16[512,1408]{1,0:T(8,128)(2,1)} %get-tuple-element.73.left.refs_7_, bf16[2048,4224]{1,0:T(8,128)(2,1)} %bitcast.64), custom_call_target="tpu_custom_call" | custom-call | tf_op jit(solution)/shard_map/down/pallas_call | solution.py:590
  243.4 11.0 %collective-permute-done.14 = bf16[128,2048]{1,0:T(8,128)(2,1)} collective-permute-done((bf16[128,2048]{1,0:T(8,128)(2,1)}, bf16[128,2048]{1,0:T(8,128)(2,1)}, u32[]{:S(2)}, u32[]{:S(2)}) %collective-permute-start.14) | collective-permute-done | bytes 524320 | tf_op jit(solution)/shard_map/ppermute | solution.py:780
  256.7 3.1 collective-permute-start.15
  259.8 12.1 %collective-permute-done.15.x1 = bf16[128,2048]{1,0:T(8,128)(2,1)S(1)} collective-permute-done((bf16[128,2048]{1,0:T(8,128)(2,1)S(1)}, bf16[128,2048]{1,0:T(8,128)(2,1)S(1)}, u32[]{:S(2)}, u32[]{:S(2)}) %collective-permute-start.15) | collective-permute-done | bytes 524320 | tf_op jit(solution)/shard_map/ppermute | solution.py:780
  274.6 12.0 %act_back.1 = (bf16[512,2816]{1,0:T(8,128)(2,1)}, bf16[512,2048]{1,0:T(8,128)(2,1)}) custom-call(bf16[128,2048]{1,0:T(8,128)(2,1)} %copy-done.6, bf16[128,2048]{1,0:T(8,128)(2,1)} %copy-done.17, bf16[128,2048]{1,0:T(8,128)(2,1)} %copy-done.19, bf16[128,2048]{1,0:T(8,128)(2,1)} %copy-done.21, bf16[2048,4224]{1,0:T(8,128)(2,1)} %bitcast.65, ...), custom_call_target="tpu_custom_call" | custom-call | tf_op jit(solution)/shard_map/act_back/pallas_call | solution.py:642
  286.6 10.5 %units_grads.1 = bf16[2048,2816]{1,0:T(8,128)(2,1)} custom-call(bf16[512,2048]{1,0:T(8,128)(2,1)} %get-tuple-element.78.refs_0_, bf16[512,2816]{1,0:T(8,128)(2,1)} %get-tuple-element.82.refs_1_.left), custom_call_target="tpu_custom_call" | custom-call | tf_op jit(solution)/shard_map/units_grads/pallas_call | solution.py:764
  297.4 10.7 %normed_back.1 = (f32[128,2048]{1,0:T(8,128)}, f32[128,2048]{1,0:T(8,128)}, bf16[128,2048]{1,0:T(8,128)(2,1)}, bf16[128,2048]{1,0:T(8,128)(2,1)}) custom-call(bf16[512,2816]{1,0:T(8,128)(2,1)} %get-tuple-element.82.refs_1_.left, bf16[2048,4224]{1,0:T(8,128)(2,1)} %bitcast.66), custom_call_target="tpu_custom_call" | custom-call | tf_op jit(solution)/shard_map/normed_back/pallas_call | solution.py:590
  311.6 3.1 collective-permute-start.20
  314.6 12.5 %collective-permute-done.20 = bf16[128,2048]{1,0:T(8,128)(2,1)S(1)} collective-permute-done((bf16[128,2048]{1,0:T(8,128)(2,1)S(1)}, bf16[128,2048]{1,0:T(8,128)(2,1)S(1)}, u32[]{:S(2)}, u32[]{:S(2)}) %collective-permute-start.20) | collective-permute-done | bytes 524320 | tf_op jit(solution)/shard_map/ppermute | solution.py:780
  332.2 11.7 %collective-permute-done.21.x1 = bf16[128,2048]{1,0:T(8,128)(2,1)S(1)} collective-permute-done((bf16[128,2048]{1,0:T(8,128)(2,1)S(1)}, bf16[128,2048]{1,0:T(8,128)(2,1)S(1)}, u32[]{:S(2)}, u32[]{:S(2)}) %collective-permute-start.21) | collective-permute-done | bytes 524320 | tf_op jit(solution)/shard_map/ppermute | solution.py:780
  346.5 6.6 %gated_back.1 = (f32[512,512]{1,0:T(8,128)}, bf16[512,512]{1,0:T(8,128)(2,1)}, f32[8,256]{1,0:T(8,128)}, bf16[512,2048]{1,0:T(8,128)(2,1)}) custom-call(s32[4]{0:T(128)} %pad_add_fusion.places, bf16[128,2048]{1,0:T(8,128)(2,1)} %copy-done.5, bf16[128,2048]{1,0:T(8,128)(2,1)} %copy-done.14, bf16[128,2048]{1,0:T(8,128)(2,1)} %copy-done.18, ...), custom_call_target="tpu_custom_call" | custom-call | tf_op jit(solution)/shard_map/gated_back/pallas_call | solution.py:695
  353.1 18.5 %mixer_backward.1 = (bf16[512,1152]{1,0:T(8,128)(2,1)}, f32[8,1024]{1,0:T(8,128)}, f32[8,128]{1,0:T(8,128)}) custom-call(s32[2]{0:T(128)} %bitcast.111, f32[512,512]{1,0:T(8,128)} %get-tuple-element.92.grad_mixed, f32[512,1664]{1,0:T(8,128)} %get-tuple-element.66.raw.raw_gate, f32[4,1024]{1,0:T(4,128)} %maximum_convert_fusion.taps, ...), custom_call_target="tpu_custom_call" | custom-call | tf_op jit(solution)/shard_map/mixer_backward/pallas_call | solution.py:416
  371.6 14.5 %mixer_grads.1 = bf16[2048,3584]{1,0:T(8,128)(2,1)} custom-call(bf16[512,2048]{1,0:T(8,128)(2,1)} %get-tuple-element.89.refs_0_, bf16[512,512]{1,0:T(8,128)(2,1)} %get-tuple-element.90.refs_1_, bf16[512,2048]{1,0:T(8,128)(2,1)} %get-tuple-element.91.refs_2_.refs_4_, bf16[512,512]{1,0:T(8,128)(2,1)} %get-tuple-element.88.refs_3_.gate, ...), custom_call_target="tpu_custom_call" | custom-call | tf_op jit(solution)/shard_map/mixer_grads/pallas_call | solution.py:764
  386.2 8.6 %input_back.1 = (f32[128,2048]{1,0:T(8,128)}, f32[128,2048]{1,0:T(8,128)}, bf16[128,2048]{1,0:T(8,128)(2,1)}, bf16[128,2048]{1,0:T(8,128)(2,1)}) custom-call(s32[4]{0:T(128)} %pad_add_fusion.places, bf16[512,512]{1,0:T(8,128)(2,1)} %get-tuple-element.88.refs_3_.gate, bf16[512,1152]{1,0:T(8,128)(2,1)} %get-tuple-element.102.refs_5_.conv, ...), custom_call_target="tpu_custom_call" | custom-call | tf_op jit(solution)/shard_map/input_back/pallas_call | solution.py:731
  404.4 10.4 %collective-permute-done.26 = bf16[128,2048]{1,0:T(8,128)(2,1)} collective-permute-done((bf16[128,2048]{1,0:T(8,128)(2,1)}, bf16[128,2048]{1,0:T(8,128)(2,1)}, u32[]{:S(2)}, u32[]{:S(2)}) %collective-permute-start.26) | collective-permute-done | bytes 524320 | tf_op jit(solution)/shard_map/ppermute | solution.py:780
  430.7 3.3 collective-permute-done.29
  434.7 4.4 collective-permute-done.30
  456.0 7.2 %collective-permute-done.35 = bf16[64,2816]{1,0:T(8,128)(2,1)S(1)} collective-permute-done((bf16[64,2816]{1,0:T(8,128)(2,1)S(1)}, bf16[64,2816]{1,0:T(8,128)(2,1)S(1)}, u32[]{:S(2)}, u32[]{:S(2)}) %collective-permute-start.35) | collective-permute-done | bytes 360480 | tf_op jit(solution)/shard_map/ppermute | solution.py:780
  466.5 28.2 %reduce-scatter.3.cloned.1.call-done = bf16[128,3584]{1,0:T(8,128)(2,1)} async-done(((bf16[2048,3584]{1,0:T(8,128)(2,1)}), bf16[128,3584]{1,0:T(8,128)(2,1)}) %reduce-scatter.3.cloned.1.call-update) | async-done | bytes 917520 | tf_op jit(solution)/shard_map/reduce_scatter | solution.py:802
  498.5 9.3 %collective-permute-done.34 = bf16[64,3584]{1,0:T(8,128)(2,1)S(1)} collective-permute-done((bf16[64,3584]{1,0:T(8,128)(2,1)S(1)}, bf16[64,3584]{1,0:T(8,128)(2,1)S(1)}, u32[]{:S(2)}, u32[]{:S(2)}) %collective-permute-start.34) | collective-permute-done | bytes 458784 | tf_op jit(solution)/shard_map/ppermute | solution.py:780
  (244 shorter events, 111.3 us)
Async XLA Ops:
  7.2 89.5 %all-gather.5.cloned.1.call-start = ((), (), s32[]{:S(2)}) async-start(), calls=%async_computation.4 | async-start | bytes 9469952 | tf_op jit(solution)/shard_map/all_gather | solution.py:797
  11.4 8.6 %collective-permute-start.3 = (bf16[64,2048]{1,0:T(8,128)(2,1)S(1)}, bf16[64,2048]{1,0:T(8,128)(2,1)S(1)}, u32[]{:S(2)}, u32[]{:S(2)}) collective-permute-start(bf16[64,2048]{1,0:T(8,128)(2,1)S(1)} %constant_dynamic-update-slice_fusion), channel_id=1, source_target_pairs={{0,64},{64,0},{1,65},{65,1},{2,66},{66,2},{3,67},{67,3},{4,68},{68... | collective-permute-start | bytes 786440 | tf_op jit(solution)/shard_map/ppermute | solution.py:780
  16.1 3.8 collective-permute-start.4
  20.9 191.7 %all-gather.7.cloned.1.call-start = ((), (), s32[]{:S(2)}) async-start(), calls=%async_computation.5 | async-start | bytes 18382848 | tf_op jit(solution)/shard_map/all_gather | solution.py:797
  22.0 13.2 %collective-permute-start.11 = (bf16[64,4224]{1,0:T(8,128)(2,1)S(1)}, bf16[64,4224]{1,0:T(8,128)(2,1)S(1)}, u32[]{:S(2)}, u32[]{:S(2)}) collective-permute-start(bf16[64,4224]{1,0:T(8,128)(2,1)S(1)} %constant_dynamic-update-slice_fusion.5), channel_id=1, source_target_pairs={{0,64},{64,0},{1,65},{65,1},{2,66},{66,2},{3,67},{67,3},{4,68},{68... | collective-permute-start | bytes 1622024 | tf_op jit(solution)/shard_map/ppermute | solution.py:780
  36.3 414.6 %reduce-scatter.5.cloned.1.call-start = ((), (), s32[]{:S(2)}) async-start(), calls=%async_computation.3 | async-start | bytes 12255232 | tf_op jit(solution)/shard_map/reduce_scatter | solution.py:802
  37.0 13.4 %collective-permute-start = (bf16[128,2048]{1,0:T(8,128)(2,1)S(1)}, bf16[128,2048]{1,0:T(8,128)(2,1)S(1)}, u32[]{:S(2)}, u32[]{:S(2)}) collective-permute-start(bf16[128,2048]{1,0:T(8,128)(2,1)S(1)} %copy.108.x0), channel_id=1, source_target_pairs={{0,2},{2,0},{1,3},{3,1},{4,6},{6,4},{5,7},{7,5},{8,10},{10,8},{9,1... | collective-permute-start | bytes 1572872 | tf_op jit(solution)/shard_map/ppermute | solution.py:780
  40.1 12.5 %collective-permute-start.1 = (bf16[128,2048]{1,0:T(8,128)(2,1)S(1)}, bf16[128,2048]{1,0:T(8,128)(2,1)S(1)}, u32[]{:S(2)}, u32[]{:S(2)}) collective-permute-start(bf16[128,2048]{1,0:T(8,128)(2,1)S(1)} %copy.108.x0), channel_id=1, source_target_pairs={{0,1},{1,0},{2,3},{3,2},{4,5},{5,4},{6,7},{7,6},{8,9},{9,8},{10,11... | collective-permute-start | bytes 1572872 | tf_op jit(solution)/shard_map/ppermute | solution.py:780
  126.6 7.8 %collective-permute-start.5 = (bf16[128,2048]{1,0:T(8,128)(2,1)}, bf16[128,2048]{1,0:T(8,128)(2,1)S(1)}, u32[]{:S(2)}, u32[]{:S(2)}) collective-permute-start(bf16[128,2048]{1,0:T(8,128)(2,1)} %get-tuple-element.69), channel_id=1, source_target_pairs={{0,1},{1,0},{2,3},{3,2},{4,5},{5,4},{6,7},{7,6},{8,9},{9,8},{10,11... | collective-permute-start | bytes 1572872 | tf_op jit(solution)/shard_map/ppermute | solution.py:780
  130.0 16.0 %collective-permute-start.7 = (bf16[128,2048]{1,0:T(8,128)(2,1)S(1)}, bf16[128,2048]{1,0:T(8,128)(2,1)S(1)}, u32[]{:S(2)}, u32[]{:S(2)}) collective-permute-start(bf16[128,2048]{1,0:T(8,128)(2,1)S(1)} %add_convert_fusion.3), channel_id=1, source_target_pairs={{0,2},{2,0},{1,3},{3,1},{4,6},{6,4},{5,7},{7,5},{8,10},{10,8},{9,1... | collective-permute-start | bytes 1572872 | tf_op jit(solution)/shard_map/ppermute | solution.py:780
  146.6 14.7 %collective-permute-start.8 = (bf16[128,2048]{1,0:T(8,128)(2,1)S(1)}, bf16[128,2048]{1,0:T(8,128)(2,1)S(1)}, u32[]{:S(2)}, u32[]{:S(2)}) collective-permute-start(bf16[128,2048]{1,0:T(8,128)(2,1)S(1)} %multiply_convert_fusion.x0), channel_id=1, source_target_pairs={{0,2},{2,0},{1,3},{3,1},{4,6},{6,4},{5,7},{7,5},{8,10},{10,8},{9,1... | collective-permute-start | bytes 1572872 | tf_op jit(solution)/shard_map/ppermute | solution.py:780
  149.6 11.7 %collective-permute-start.9 = (bf16[128,2048]{1,0:T(8,128)(2,1)S(1)}, bf16[128,2048]{1,0:T(8,128)(2,1)S(1)}, u32[]{:S(2)}, u32[]{:S(2)}) collective-permute-start(bf16[128,2048]{1,0:T(8,128)(2,1)S(1)} %multiply_convert_fusion.x0), channel_id=1, source_target_pairs={{0,1},{1,0},{2,3},{3,2},{4,5},{5,4},{6,7},{7,6},{8,9},{9,8},{10,11... | collective-permute-start | bytes 1572872 | tf_op jit(solution)/shard_map/ppermute | solution.py:780
  235.2 8.2 %collective-permute-start.12 = (bf16[128,2048]{1,0:T(8,128)(2,1)}, bf16[128,2048]{1,0:T(8,128)(2,1)}, u32[]{:S(2)}, u32[]{:S(2)}) collective-permute-start(bf16[128,2048]{1,0:T(8,128)(2,1)} %get-tuple-element.75), channel_id=1, source_target_pairs={{0,1},{1,0},{2,3},{3,2},{4,5},{5,4},{6,7},{7,6},{8,9},{9,8},{10,11... | collective-permute-start | bytes 1572872 | tf_op jit(solution)/shard_map/ppermute | solution.py:780
  238.3 16.2 %collective-permute-start.14 = (bf16[128,2048]{1,0:T(8,128)(2,1)}, bf16[128,2048]{1,0:T(8,128)(2,1)}, u32[]{:S(2)}, u32[]{:S(2)}) collective-permute-start(bf16[128,2048]{1,0:T(8,128)(2,1)} %add_convert_fusion.2), channel_id=1, source_target_pairs={{0,2},{2,0},{1,3},{3,1},{4,6},{6,4},{5,7},{7,5},{8,10},{10,8},{9,1... | collective-permute-start | bytes 1572872 | tf_op jit(solution)/shard_map/ppermute | solution.py:780
  256.7 15.1 %collective-permute-start.15 = (bf16[128,2048]{1,0:T(8,128)(2,1)S(1)}, bf16[128,2048]{1,0:T(8,128)(2,1)S(1)}, u32[]{:S(2)}, u32[]{:S(2)}) collective-permute-start(bf16[128,2048]{1,0:T(8,128)(2,1)S(1)} %get-tuple-element.202.x0), channel_id=1, source_target_pairs={{0,2},{2,0},{1,3},{3,1},{4,6},{6,4},{5,7},{7,5},{8,10},{10,8},{9,1... | collective-permute-start | bytes 1572872 | tf_op jit(solution)/shard_map/ppermute | solution.py:780
  259.8 12.1 %collective-permute-start.16 = (bf16[128,2048]{1,0:T(8,128)(2,1)S(1)}, bf16[128,2048]{1,0:T(8,128)(2,1)S(1)}, u32[]{:S(2)}, u32[]{:S(2)}) collective-permute-start(bf16[128,2048]{1,0:T(8,128)(2,1)S(1)} %get-tuple-element.202.x0), channel_id=1, source_target_pairs={{0,1},{1,0},{2,3},{3,2},{4,5},{5,4},{6,7},{7,6},{8,9},{9,8},{10,11... | collective-permute-start | bytes 1572872 | tf_op jit(solution)/shard_map/ppermute | solution.py:780
  297.1 197.5 %reduce-scatter.3.cloned.1.call-start = ((), (), s32[]{:S(2)}) async-start(), calls=%async_computation.2 | async-start | bytes 15597568 | tf_op jit(solution)/shard_map/reduce_scatter | solution.py:802
  308.2 6.4 %collective-permute-start.18 = (bf16[128,2048]{1,0:T(8,128)(2,1)}, bf16[128,2048]{1,0:T(8,128)(2,1)S(1)}, u32[]{:S(2)}, u32[]{:S(2)}) collective-permute-start(bf16[128,2048]{1,0:T(8,128)(2,1)} %get-tuple-element.84), channel_id=1, source_target_pairs={{0,1},{1,0},{2,3},{3,2},{4,5},{5,4},{6,7},{7,6},{8,9},{9,8},{10,11... | collective-permute-start | bytes 1572872 | tf_op jit(solution)/shard_map/ppermute | solution.py:780
  311.6 15.5 %collective-permute-start.20 = (bf16[128,2048]{1,0:T(8,128)(2,1)S(1)}, bf16[128,2048]{1,0:T(8,128)(2,1)S(1)}, u32[]{:S(2)}, u32[]{:S(2)}) collective-permute-start(bf16[128,2048]{1,0:T(8,128)(2,1)S(1)} %add_convert_fusion.1), channel_id=1, source_target_pairs={{0,2},{2,0},{1,3},{3,1},{4,6},{6,4},{5,7},{7,5},{8,10},{10,8},{9,1... | collective-permute-start | bytes 1572872 | tf_op jit(solution)/shard_map/ppermute | solution.py:780
  329.2 14.6 %collective-permute-start.21 = (bf16[128,2048]{1,0:T(8,128)(2,1)S(1)}, bf16[128,2048]{1,0:T(8,128)(2,1)S(1)}, u32[]{:S(2)}, u32[]{:S(2)}) collective-permute-start(bf16[128,2048]{1,0:T(8,128)(2,1)S(1)} %get-tuple-element.200.x0), channel_id=1, source_target_pairs={{0,2},{2,0},{1,3},{3,1},{4,6},{6,4},{5,7},{7,5},{8,10},{10,8},{9,1... | collective-permute-start | bytes 1572872 | tf_op jit(solution)/shard_map/ppermute | solution.py:780
  332.2 11.7 %collective-permute-start.22 = (bf16[128,2048]{1,0:T(8,128)(2,1)S(1)}, bf16[128,2048]{1,0:T(8,128)(2,1)S(1)}, u32[]{:S(2)}, u32[]{:S(2)}) collective-permute-start(bf16[128,2048]{1,0:T(8,128)(2,1)S(1)} %get-tuple-element.200.x0), channel_id=1, source_target_pairs={{0,1},{1,0},{2,3},{3,2},{4,5},{5,4},{6,7},{7,6},{8,9},{9,8},{10,11... | collective-permute-start | bytes 1572872 | tf_op jit(solution)/shard_map/ppermute | solution.py:780
  394.9 9.5 %collective-permute-start.24 = (bf16[128,2048]{1,0:T(8,128)(2,1)}, bf16[128,2048]{1,0:T(8,128)(2,1)}, u32[]{:S(2)}, u32[]{:S(2)}) collective-permute-start(bf16[128,2048]{1,0:T(8,128)(2,1)} %get-tuple-element.104), channel_id=1, source_target_pairs={{0,1},{1,0},{2,3},{3,2},{4,5},{5,4},{6,7},{7,6},{8,9},{9,8},{10,11... | collective-permute-start | bytes 1572872 | tf_op jit(solution)/shard_map/ppermute | solution.py:780
  399.0 15.8 %collective-permute-start.26 = (bf16[128,2048]{1,0:T(8,128)(2,1)}, bf16[128,2048]{1,0:T(8,128)(2,1)}, u32[]{:S(2)}, u32[]{:S(2)}) collective-permute-start(bf16[128,2048]{1,0:T(8,128)(2,1)} %add_convert_fusion), channel_id=1, source_target_pairs={{0,2},{2,0},{1,3},{3,1},{4,6},{6,4},{5,7},{7,5},{8,10},{10,8},{9,1... | collective-permute-start | bytes 1572872 | tf_op jit(solution)/shard_map/ppermute | solution.py:780
  417.2 4.0 collective-permute-start.27
  421.2 6.2 %collective-permute-start.28 = (f32[72,128]{1,0:T(8,128)S(1)}, f32[72,128]{1,0:T(8,128)S(1)}, u32[]{:S(2)}, u32[]{:S(2)}) collective-permute-start(f32[72,128]{1,0:T(8,128)S(1)} %fusion.11), channel_id=1, source_target_pairs={{0,16},{16,0},{32,48},{48,32},{1,17},{17,1},{33,49},{49,33},{2,18}... | collective-permute-start | bytes 110600 | tf_op jit(solution)/shard_map/ppermute | solution.py:832
  427.5 6.5 %collective-permute-start.29 = (f32[72,128]{1,0:T(8,128)S(1)}, f32[72,128]{1,0:T(8,128)S(1)}, u32[]{:S(2)}, u32[]{:S(2)}) collective-permute-start(f32[72,128]{1,0:T(8,128)S(1)} %fusion.20), channel_id=1, source_target_pairs={{0,32},{16,48},{32,0},{48,16},{1,33},{17,49},{33,1},{49,17},{2,34}... | collective-permute-start | bytes 110600 | tf_op jit(solution)/shard_map/ppermute | solution.py:832
  434.0 5.1 collective-permute-start.30
  439.1 6.4 %collective-permute-start.31 = (f32[72,128]{1,0:T(8,128)S(1)}, f32[72,128]{1,0:T(8,128)S(1)}, u32[]{:S(2)}, u32[]{:S(2)}) collective-permute-start(f32[72,128]{1,0:T(8,128)S(1)} %add.171), channel_id=1, source_target_pairs={{0,8},{4,12},{8,0},{12,4},{1,9},{5,13},{9,1},{13,5},{2,10},{6,14},... | collective-permute-start | bytes 110600 | tf_op jit(solution)/shard_map/ppermute | solution.py:832
  445.5 5.4 %collective-permute-start.32 = (f32[34,128]{1,0:T(8,128)S(1)}, f32[34,128]{1,0:T(8,128)S(1)}, u32[]{:S(2)}, u32[]{:S(2)}) collective-permute-start(f32[34,128]{1,0:T(8,128)S(1)} %slice.176), channel_id=1, source_target_pairs={{0,2},{2,0},{1,3},{3,1},{4,6},{6,4},{5,7},{7,5},{8,10},{10,8},{9,1... | collective-permute-start | bytes 52232 | tf_op jit(solution)/shard_map/ppermute | solution.py:832
  450.9 3.9 collective-permute-start.33
  451.9 11.2 %collective-permute-start.35 = (bf16[64,2816]{1,0:T(8,128)(2,1)S(1)}, bf16[64,2816]{1,0:T(8,128)(2,1)S(1)}, u32[]{:S(2)}, u32[]{:S(2)}) collective-permute-start(bf16[64,2816]{1,0:T(8,128)(2,1)S(1)} %slice.194), channel_id=1, source_target_pairs={{0,64},{64,0},{1,65},{65,1},{2,66},{66,2},{3,67},{67,3},{4,68},{68... | collective-permute-start | bytes 1081352 | tf_op jit(solution)/shard_map/ppermute | solution.py:780
  495.8 12.0 %collective-permute-start.34 = (bf16[64,3584]{1,0:T(8,128)(2,1)S(1)}, bf16[64,3584]{1,0:T(8,128)(2,1)S(1)}, u32[]{:S(2)}, u32[]{:S(2)}) collective-permute-start(bf16[64,3584]{1,0:T(8,128)(2,1)S(1)} %slice.178), channel_id=1, source_target_pairs={{0,64},{64,0},{1,65},{65,1},{2,66},{66,2},{3,67},{67,3},{4,68},{68... | collective-permute-start | bytes 1376264 | tf_op jit(solution)/shard_map/ppermute | solution.py:780
  (44 other events, 631.8 us)
Sparse Core Ops, SparseCore 0:
  21.0 75.6 all-gather.4
  98.8 113.7 all-gather.6
  297.3 91.8 reduce-scatter.4
  392.8 101.8 reduce-scatter.2

commit v3 on v2

--- a/solution.py
+++ b/solution.py
@@ -377,6 +377,12 @@
             grad_taps[CONV - 1 - o : CONV - o, lanes(block)] = sums[o]
 
 
+def lasting(micros):
+    return pl.CostEstimate(
+        flops=int(micros * 1e9), transcendentals=0, bytes_accessed=int(micros * 3e6)
+    )
+
+
 def vmem(count):
     return [pl.BlockSpec(memory_space=pltpu.VMEM)] * count
 
@@ -403,6 +409,7 @@
         in_specs=[SMEM] + vmem(4),
         out_specs=vmem(len(outs)),
         compiler_params=LIMIT,
+        cost_estimate=lasting(12.5),
         name="mixer_forward",
     )(bounds, raw, taps, vectors, gain)
 
@@ -420,6 +427,7 @@
         out_specs=vmem(len(outs)),
         scratch_shapes=[pltpu.VMEM((ROWS + 8, CONVW), F32)],
         compiler_params=LIMIT,
+        cost_estimate=lasting(18.5),
         name="mixer_backward",
     )(bounds, grad_mixed, raw, taps, vectors, *saved)
 
@@ -429,6 +437,7 @@
 TILE = 512
 STEP = 512
 WIDE = 384
+HALF = 768
 
 
 def whole(*shape):
@@ -482,36 +491,37 @@
         + [whole(OWN, features)] * 4
         + [
             pl.BlockSpec((features, SMALL), lambda i: (0, (VW + SMALL_AT) // SMALL)),
-            pl.BlockSpec((STEP, weights.shape[1]), lambda i: (i, 0)),
+            pl.BlockSpec((STEP, VW + PROJ), lambda i: (i, 0)),
         ],
         out_specs=[whole(ROWS, PROJ), whole(ROWS, features), whole(8, features)],
         scratch_shapes=[pltpu.VMEM((count, ROWS, STEP), BF16)],
         compiler_params=LIMIT,
+        cost_estimate=lasting(12),
         name="project",
     )(places, *blocks, weights, weights)
 
 
-def split_rows(product, kept_own, kept_other, sent_own, sent_other):
+def split_rows(product, kept_other, sent_other, kept_own, sent_own):
     kept_own[...] = product[:OWN]
-    kept_other[...] = product[OWN : 2 * OWN]
-    sent_own[...] = product[2 * OWN : 3 * OWN].astype(BF16)
+    sent_own[...] = product[OWN : 2 * OWN].astype(BF16)
+    kept_other[...] = product[2 * OWN : 3 * OWN]
     sent_other[...] = product[3 * OWN :].astype(BF16)
 
 
 def split_outs(features):
     shape = (OWN, features)
-    outs = [jax.ShapeDtypeStruct(shape, F32)] * 2 + [jax.ShapeDtypeStruct(shape, BF16)] * 2
-    return outs, [pl.BlockSpec((OWN, TILE), lambda i: (0, i))] * 4
-
-
-def mix_out_kernel(places, gated, weights, kept_own, kept_other, sent_own, sent_other, turned):
+    pair = [jax.ShapeDtypeStruct(shape, F32), jax.ShapeDtypeStruct(shape, BF16)]
+    return pair * 2, [pl.BlockSpec((OWN, TILE), lambda i: (0, i))] * 4
+
+
+def mix_out_kernel(places, gated, weights, kept_other, sent_other, kept_own, sent_own, turned):
     @pl.when(pl.program_id(0) == 0)
     def prepare():
         for j in range(4):
             turned[j * OWN : (j + 1) * OWN] = gated[place_rows(places, j), :]
 
     split_rows(
-        contract(turned[...], weights[...], NT), kept_own, kept_other, sent_own, sent_other
+        contract(turned[...], weights[...], NT), kept_other, sent_other, kept_own, sent_own
     )
 
 
@@ -525,6 +535,7 @@
         in_specs=[SMEM, whole(ROWS, VW), pl.BlockSpec((TILE, VW), lambda i: (i, 0))],
         out_specs=specs + [whole(ROWS, VW)],
         compiler_params=LIMIT,
+        cost_estimate=lasting(5),
         name="mix_out",
     )(places, gated, weights)
 
@@ -575,33 +586,78 @@
         ],
         scratch_shapes=[pltpu.VMEM((ROWS, features), BF16)],
         compiler_params=LIMIT,
+        cost_estimate=lasting(12.5),
         name="gate_up",
     )(*blocks, weights)
 
 
-def rows_back_kernel(left, weights, kept_own, kept_other, sent_own, sent_other):
-    split_rows(contract(left[...], weights[...], NT), kept_own, kept_other, sent_own, sent_other)
-
-
-def rows_back(left, weights, block, name):
+def half_back_kernel(left, weights, kept, sent):
+    product = contract(left[...], weights[...], NT)
+    kept[...] = product[:OWN]
+    sent[...] = product[OWN:].astype(BF16)
+
+
+def half_back(left, part, weights, block, tile, micros, name):
     features = weights.shape[0]
     width = left.shape[1]
-    outs, specs = split_outs(features)
-    return pl.pallas_call(
-        rows_back_kernel,
-        grid=(features // TILE,),
-        out_shape=outs,
-        in_specs=[whole(ROWS, width), pl.BlockSpec((TILE, width), lambda i: (i, block))],
-        out_specs=specs,
-        compiler_params=LIMIT,
+    shape = (OWN, features)
+    return pl.pallas_call(
+        half_back_kernel,
+        grid=(features // tile,),
+        out_shape=[jax.ShapeDtypeStruct(shape, F32), jax.ShapeDtypeStruct(shape, BF16)],
+        in_specs=[
+            pl.BlockSpec((2 * OWN, width), lambda i: (part, 0)),
+            pl.BlockSpec((tile, width), lambda i: (i, block)),
+        ],
+        out_specs=[pl.BlockSpec((OWN, tile), lambda i: (0, i))] * 2,
+        compiler_params=LIMIT,
+        cost_estimate=lasting(micros),
         name=name,
     )(left, weights)
 
 
-def act_back_kernel(x0, x1, x2, x3, weights, gate, up, grads, rows, steps, total, gates, ups):
+def down_first_kernel(left, low, low_across, *refs):
+    *high, kept, sent, weights = refs
+    for b in range(low.shape[0] // 64):
+        for o, half in enumerate((low, low_across)):
+            rows = slice(b * 128 + o * 64, b * 128 + o * 64 + 64)
+            weights[rows, :HALF] = half[b * 64 : b * 64 + 64]
+    for i, block in enumerate(high):
+        weights[:, HALF + i * 128 : HALF + (i + 1) * 128] = block[...]
+    product = contract(left[...], weights[...], NT)
+    kept[...] = product[:OWN]
+    sent[...] = product[OWN:].astype(BF16)
+
+
+def down_first(left, part, low, low_across, full):
+    features = full.shape[0]
+    width = left.shape[1]
+    tile = 2 * STEP
+    shape = (OWN, features)
+    half = pl.BlockSpec((tile // 2, HALF), lambda i: (i, 0))
+    column = pl.BlockSpec((OWN, tile), lambda i: (0, i))
+    blocks = range((full.shape[1] + HALF - width) // 128, full.shape[1] // 128)
+    return pl.pallas_call(
+        down_first_kernel,
+        grid=(features // tile,),
+        out_shape=[
+            jax.ShapeDtypeStruct(shape, F32),
+            jax.ShapeDtypeStruct(shape, BF16),
+            jax.ShapeDtypeStruct((features, width), BF16),
+        ],
+        in_specs=[pl.BlockSpec((2 * OWN, width), lambda i: (part, 0)), half, half]
+        + [pl.BlockSpec((tile, 128), partial(lambda b, i: (i, b), b)) for b in blocks],
+        out_specs=[column, column, pl.BlockSpec((tile, width), lambda i: (i, 0))],
+        compiler_params=LIMIT,
+        cost_estimate=lasting(6),
+        name="down_first",
+    )(left, low, low_across, *[full] * len(blocks))
+
+
+def act_back_kernel(x0, x1, weights, gate, up, grads, rows, steps, total, gates, ups):
     step = pl.program_id(0)
 
-    for j, x in enumerate((x0, x1, x2, x3)):
+    for j, x in enumerate((x0, x1)):
         at = slice(j * OWN, (j + 1) * OWN)
 
         @pl.when(step == 0)
@@ -634,31 +690,32 @@
             grads[:, lanes(2 * b + 1)] = (grad * gate_in * s).astype(BF16)
 
 
-def act_back(blocks, weights, gate, up):
+def act_back(blocks, part, weights, block, gate, up):
     features = weights.shape[0]
     units = gate.shape[1]
     count = features // STEP
-    part = pl.BlockSpec((OWN, units), lambda i: (i, 0))
+    rows = pl.BlockSpec((OWN, units), lambda i: (2 * part + jnp.minimum(i, 1), 0))
     return pl.pallas_call(
         act_back_kernel,
         grid=(count,),
         out_shape=[
-            jax.ShapeDtypeStruct((ROWS, 2 * units), BF16),
-            jax.ShapeDtypeStruct((ROWS, features), BF16),
+            jax.ShapeDtypeStruct((2 * OWN, 2 * units), BF16),
+            jax.ShapeDtypeStruct((2 * OWN, features), BF16),
         ],
-        in_specs=[whole(OWN, features)] * 4
-        + [pl.BlockSpec((STEP, units), lambda i: (i, 2)), part, part],
+        in_specs=[whole(OWN, features)] * 2
+        + [pl.BlockSpec((STEP, units), lambda i: (i, block)), rows, rows],
         out_specs=[
-            whole(ROWS, 2 * units),
-            pl.BlockSpec((OWN, features), lambda i: (i, 0)),
+            whole(2 * OWN, 2 * units),
+            pl.BlockSpec((OWN, features), lambda i: (jnp.minimum(i, 1), 0)),
         ],
         scratch_shapes=[
-            pltpu.VMEM((count, ROWS, STEP), BF16),
-            pltpu.VMEM((ROWS, units), F32),
-            pltpu.VMEM((ROWS, units), F32),
-            pltpu.VMEM((ROWS, units), F32),
+            pltpu.VMEM((count, 2 * OWN, STEP), BF16),
+            pltpu.VMEM((2 * OWN, units), F32),
+            pltpu.VMEM((2 * OWN, units), F32),
+            pltpu.VMEM((2 * OWN, units), F32),
         ],
         compiler_params=LIMIT,
+        cost_estimate=lasting(8),
         name="act_back",
     )(*blocks, weights, gate, up)
 
@@ -706,12 +763,13 @@
         + [whole(features, VW), whole(ROWS, VW), whole(ROWS, VW), whole(1, DV)],
         out_specs=[whole(ROWS, VW), whole(ROWS, VW), whole(8, DV), whole(ROWS, features)],
         compiler_params=LIMIT,
+        cost_estimate=lasting(6.5),
         name="gated_back",
     )(places, *blocks, weights, raw, mixed, gain)
 
 
 def input_back_kernel(
-    places, gate, conv, weights, kept_own, kept_other, sent_own, sent_other, turned
+    places, gate, conv, weights, kept_other, sent_other, kept_own, sent_own, turned
 ):
     @pl.when(pl.program_id(0) == 0)
     def prepare():
@@ -721,7 +779,7 @@
             turned[j * OWN : (j + 1) * OWN, VW:] = conv[rows, :]
 
     split_rows(
-        contract(turned[...], weights[:, VW:], NT), kept_own, kept_other, sent_own, sent_other
+        contract(turned[...], weights[:, VW:], NT), kept_other, sent_other, kept_own, sent_own
     )
 
 
@@ -736,40 +794,105 @@
             SMEM,
             whole(ROWS, VW),
             whole(ROWS, CONVW + SMALL),
-            pl.BlockSpec((TILE, weights.shape[1]), lambda i: (i, 0)),
+            pl.BlockSpec((TILE, VW + PROJ), lambda i: (i, 0)),
         ],
         out_specs=specs,
         scratch_shapes=[pltpu.VMEM((ROWS, PROJ), BF16)],
         compiler_params=LIMIT,
+        cost_estimate=lasting(8.5),
         name="input_back",
     )(places, gate, conv, weights)
 
 
-def grads_kernel(count, *refs):
+def grads_kernel(counts, *refs):
     out = refs[-1]
-    at = 0
-    for i in range(count):
-        left, right = refs[2 * i], refs[2 * i + 1]
-        width = right.shape[1]
-        out[:, at : at + width] = contract(left[...], right[...], TN).astype(BF16)
+    at, used = 0, 0
+    for count in counts:
+        total = contract(refs[used][...], refs[used + 1][...], TN)
+        for i in range(1, count):
+            total = total + contract(refs[used + 2 * i][...], refs[used + 2 * i + 1][...], TN)
+        used += 2 * count
+        width = total.shape[1]
+        out[:, at : at + width] = total.astype(BF16)
         at += width
 
 
-def weight_grads(pairs, name):
-    features = pairs[0][0].shape[1]
-    width = sum(right.shape[1] for left, right in pairs)
-    specs = []
-    for left, right in pairs:
-        specs += [pl.BlockSpec((ROWS, STEP), lambda i: (0, i)), whole(ROWS, right.shape[1])]
-    return pl.pallas_call(
-        partial(grads_kernel, len(pairs)),
+def weight_grads(groups, micros, name):
+    operands, specs, counts, width = [], [], [], 0
+    for group in groups:
+        counts.append(len(group))
+        for left, right in group:
+            (left, part), (right, other) = left, right
+            rows = min(left.shape[0], right.shape[0])
+            operands += [left, right]
+            specs += [
+                pl.BlockSpec((rows, STEP), partial(lambda p, i: (p, i), part)),
+                pl.BlockSpec((rows, right.shape[1]), partial(lambda p, i: (p, 0), other)),
+            ]
+        width += right.shape[1]
+    features = groups[0][0][0][0].shape[1]
+    return pl.pallas_call(
+        partial(grads_kernel, counts),
         grid=(features // STEP,),
         out_shape=jax.ShapeDtypeStruct((features, width), BF16),
         in_specs=specs,
         out_specs=pl.BlockSpec((STEP, width), lambda i: (i, 0)),
         compiler_params=LIMIT,
+        cost_estimate=lasting(micros),
         name=name,
-    )(*[operand for pair in pairs for operand in pair])
+    )(*operands)
+
+
+def pack_kernel(*refs):
+    out = refs[-1]
+    at = 0
+    for ref in refs[:-1]:
+        out[:, at : at + ref.shape[1]] = ref[...]
+        at += ref.shape[1]
+
+
+def pack(*blocks):
+    shape = (blocks[0].shape[0], sum(block.shape[1] for block in blocks))
+    return pl.pallas_call(
+        pack_kernel,
+        out_shape=jax.ShapeDtypeStruct(shape, BF16),
+        in_specs=vmem(len(blocks)),
+        out_specs=pl.BlockSpec(memory_space=pltpu.VMEM),
+        compiler_params=LIMIT,
+        cost_estimate=lasting(1.7),
+        name="pack",
+    )(*blocks)
+
+
+def pack_both_kernel(count, *refs):
+    rows = refs[0].shape[0]
+    out = refs[-1]
+    at = 0
+    for i in range(count):
+        width = refs[2 * i].shape[1]
+        out[:rows, at : at + width] = refs[2 * i][...]
+        out[rows:, at : at + width] = refs[2 * i + 1][...]
+        at += width
+    for ref in refs[2 * count : -1]:
+        half = ref.shape[1] // 2
+        out[:rows, at : at + half] = ref[:, :half]
+        out[rows:, at : at + half] = ref[:, half:]
+        at += half
+
+
+def pack_both(pairs, *halved):
+    rows = pairs[0][0].shape[0]
+    width = sum(own.shape[1] for own, other in pairs) + sum(b.shape[1] for b in halved) // 2
+    operands = [block for pair in pairs for block in pair] + list(halved)
+    return pl.pallas_call(
+        partial(pack_both_kernel, len(pairs)),
+        out_shape=jax.ShapeDtypeStruct((2 * rows, width), BF16),
+        in_specs=vmem(len(operands)),
+        out_specs=pl.BlockSpec(memory_space=pltpu.VMEM),
+        compiler_params=LIMIT,
+        cost_estimate=lasting(2),
+        name="pack_both",
+    )(*operands)
 
 
 SWAP = [(0, 1), (1, 0)]
@@ -782,20 +905,26 @@
 
 def gather_tokens(own):
     across = trade(own, "xh")
-    return own, across, trade(own, "c"), trade(across, "c")
-
-
-def scatter_tokens(kept_own, kept_other, sent_own, sent_other):
+    return own, trade(own, "c"), across, trade(across, "c")
+
+
+def scatter_tokens(kept_other, sent_other, kept_own, sent_own):
     other = kept_other + trade(sent_other, "c").astype(jnp.float32)
     own = kept_own + trade(sent_own, "c").astype(jnp.float32)
     return own + trade(other.astype(jnp.bfloat16), "xh").astype(jnp.float32)
 
 
-def gather_weights(*blocks):
-    other = jnp.concatenate([trade(block, "xl") for block in blocks], axis=1)
-    both = jnp.stack([jnp.concatenate(blocks, axis=1), other], axis=0)
-    full = lax.all_gather(both, PLANE, axis=0, tiled=False)
-    return full.reshape(-1, other.shape[1])
+def scatter_halves(far, near, operand):
+    kept, sent = far
+    low = (kept + trade(sent, "c").astype(jnp.float32)).astype(jnp.bfloat16)
+    low, operand = lax.optimization_barrier((low, operand))
+    kept, sent = near(operand)
+    own = kept + trade(sent, "c").astype(jnp.float32)
+    return own + trade(low, "xh").astype(jnp.float32)
+
+
+def gather_plane(block):
+    return lax.all_gather(block, PLANE, axis=0, tiled=False).reshape(-1, block.shape[1])
 
 
 def scatter_grads(grads):
@@ -863,7 +992,7 @@
     half, core = lax.axis_index("xh"), lax.axis_index("c")
     tensor_index = half * 2 + core
     places = jnp.stack(
-        [tensor_index, 2 - 2 * half + core, 2 * half + 1 - core, 3 - tensor_index]
+        [tensor_index, 2 * half + 1 - core, 2 - 2 * half + core, 3 - tensor_index]
     ).astype(jnp.int32)
     heads_here = decay_log.shape[0]
     own_lengths = lax.dynamic_index_in_dim(lengths, group_index, 0, keepdims=False)
@@ -876,17 +1005,21 @@
     v_width = value_taps.shape[1]
     f_width = gate_weight.shape[1]
     filler = jnp.zeros((rows_dp, SMALL - 2 * heads_here - 2), jnp.bfloat16)
-    mixer_block = jnp.concatenate(
-        [out_weight, output_gate, value_weight, query_weight, key_weight], axis=1
-    )
+    mixer_block = pack(out_weight, output_gate, value_weight, query_weight, key_weight)
     small_block = jnp.concatenate(
         [beta_weight, decay_weight, norm1_gain[:, None], norm2_gain[:, None], filler], axis=1
     )
     paired_units = jnp.stack(
         [gate_weight.reshape(rows_dp, -1, 128), up_weight.reshape(rows_dp, -1, 128)], axis=2
     ).reshape(rows_dp, 2 * f_width)
-    mixer_full = gather_weights(mixer_block, small_block)
-    ffn_full = gather_weights(jnp.concatenate([paired_units, down_weight], axis=1))
+    mixer_full = gather_plane(
+        pack_both(
+            [(mixer_block, trade(mixer_block, "xl")), (small_block, trade(small_block, "xl"))],
+            down_weight[:, :HALF],
+        )
+    )
+    ffn_block = jnp.concatenate([paired_units, down_weight[:, HALF:]], axis=1)
+    ffn_full = gather_plane(pack_both([(ffn_block, trade(ffn_block, "xl"))]))
     input_own = features_in(layer_input)
     teacher_own = features_in(teacher_out).astype(jnp.float32)
     conv_taps = jnp.concatenate([value_taps, query_taps, key_taps], axis=1).astype(jnp.float32)
@@ -896,26 +1029,46 @@
     )
     gain_mixer = mixer_gain.astype(jnp.float32)[None, :]
 
-    input_blocks = gather_tokens(input_own)
+    mixer_full, *input_blocks = lax.optimization_barrier((mixer_full, *gather_tokens(input_own)))
+    down_low = mixer_full[:, VW + PROJ :].reshape(16, 2, rows_dp, HALF // 2)
+    down_low = down_low.swapaxes(1, 2).reshape(-1, HALF)
+    down_low, mixer_full = lax.optimization_barrier((down_low, mixer_full))
+    low_across = trade(down_low, "xl")
     raw, normed_one, gains = project(places, input_blocks, mixer_full)
     gain_first, gain_second = gains[0:1], gains[1:2]
     input_float = input_own.astype(jnp.float32)
     scale_one = lax.rsqrt(jnp.mean(input_float * input_float, axis=-1, keepdims=True) + EPSILON)
     gated_low, *saved, mixed = mixer_forward(boundary, raw, conv_taps, vectors, gain_mixer)
+    gated_low, low_across = lax.optimization_barrier((gated_low, low_across))
     *terms, gated_turned = mix_out(places, gated_low, mixer_full)
     hidden = input_float + scatter_tokens(*terms)
     scale_two = lax.rsqrt(jnp.mean(hidden * hidden, axis=-1, keepdims=True) + EPSILON)
     normed_two = (hidden * scale_two * gain_second).astype(jnp.bfloat16)
-    act_low, gate_in, up_in, normed_rows = gate_up(gather_tokens(normed_two), ffn_full, f_width)
-    layer_out = hidden + scatter_tokens(*rows_back(act_low, ffn_full, 2, "down"))
+    blocks = gather_tokens(normed_two)
+    act_low, gate_in, up_in, normed_rows = gate_up(blocks, ffn_full, f_width)
+    *far, down_full = down_first(act_low, 1, down_low, low_across, ffn_full)
+    layer_out = hidden + scatter_halves(
+        far, lambda act: half_back(act, 0, down_full, 0, 1024, 5, "down_near"), act_low
+    )
     grad_layer = loss_scale * validity * (layer_out - teacher_own)
-    grad_gate_up, grad_rows = act_back(
-        gather_tokens(grad_layer.astype(jnp.bfloat16)), ffn_full, gate_in, up_in
-    )
-    units_grad = weight_grads([(normed_rows, grad_gate_up)], "units_grads")
-    units_grad, grad_gate_up = lax.optimization_barrier((units_grad, grad_gate_up))
+    grad_low = grad_layer.astype(jnp.bfloat16)
+    across = trade(grad_low, "xh")
+    grads_near, rows_near = act_back(
+        (grad_low, trade(grad_low, "c")), 0, down_full, 0, gate_in, up_in
+    )
+    across, grads_near = lax.optimization_barrier((across, grads_near))
+    grads_far, rows_far = act_back(
+        (across, trade(across, "c")), 1, down_full, 0, gate_in, up_in
+    )
+    units_grad = weight_grads(
+        [[((normed_rows, 0), (grads_near, 0)), ((normed_rows, 1), (grads_far, 0))]], 10.5, "units_grads"
+    )
+    units_grad, grads_far, grads_near = lax.optimization_barrier((units_grad, grads_far, grads_near))
     units_sum = scatter_grads(units_grad)
-    grad_normed_two = scatter_tokens(*rows_back(grad_gate_up, ffn_full, 0, "normed_back"))
+    far = half_back(grads_far, 0, ffn_full, 0, 512, 8, "normed_far")
+    grad_normed_two = scatter_halves(
+        far, lambda grads: half_back(grads, 0, ffn_full, 0, 512, 8, "normed_near"), grads_near
+    )
 
     weighted_two = gain_second * grad_normed_two
     grad_gain_two = jnp.sum(grad_normed_two * hidden * scale_two, axis=0)
@@ -934,11 +1087,12 @@
     )
     last_grad = weight_grads(
         [
-            (grad_turned, gated_turned),
-            (normed_one, gate_low),
-            (normed_one, raw_low),
-            (grad_rows, act_low),
+            [((grad_turned, 0), (gated_turned, 0))],
+            [((normed_one, 0), (gate_low, 0))],
+            [((normed_one, 0), (raw_low, 0))],
+            [((rows_near, 0), (act_low, 0)), ((rows_far, 0), (act_low, 1))],
         ],
+        14.5,
         "mixer_grads",
     )
     last_grad, raw_low = lax.optimization_barrier((last_grad, raw_low))

time: 523 us -> 510 us (0.975)
  waiting for transfers between devices: 266 us -> 231 us
  Pallas kernels: 132 us -> 152 us
    all_gather x2, waiting for transfers between devices: 93.4 us -> 68.5 us  [gather_plane(): lax.all_gather(block, PLANE, axis=0, tiled=False)]
    pallas_call x4 -> x9, Pallas kernels: 43.2 us -> 58.9 us  [the longest x2 25.5 us: weight_grads(): pl.pallas_call(partial(grads_kernel, counts), grid=(features // STEP,), o...]
    ppermute x29 -> x30, waiting for transfers between devices: 130 us -> 120 us  [trade(): return lax.ppermute(values, axis, SWAP)]
    pallas_call x1 -> x2, Pallas kernels: 12 us -> 16.4 us  [act_back(): pl.pallas_call(act_back_kernel, grid=(count,), out_shape=[jax.ShapeDtypeS...]
    unnamed x89 -> x119, local copies, waits for them, and re-layouts: 12.5 us -> 10.3 us
    ppermute x29 -> x30, starting transfers between devices: 33.9 us -> 35.8 us  [trade(): return lax.ppermute(values, axis, SWAP)]
  transfers between devices with their start and end apart: 40 -> 41, of which waited for: 26 -> 28; matrix products, arithmetic and copies ran while one was open for 9% -> 8% of each run, Pallas kernels for 17% -> 22%
where the time goes in v3:
time: 510 us; the launch traced here: 504 us
  waiting for transfers between devices  231 us (45%)
  Pallas kernels  152 us (30%)
  starting transfers between devices  48.1 us (9%)
  local copies, waits for them, and re-layouts  32.5 us (6%)
  other arithmetic  24.4 us (5%)
  between operations  15.5 us (3%)
    ppermute x30, waiting for transfers between devices, trade(): return lax.ppermute(values, axis, SWAP)  120 us
    all_gather x2, waiting for transfers between devices, gather_plane(): lax.all_gather(block, PLANE, axis=0, tiled=False)  68.5 us
    ppermute x30, starting transfers between devices, trade(): return lax.ppermute(values, axis, SWAP)  35.8 us
    reduce_scatter x2, waiting for transfers between devices, scatter_grads(): both = lax.psum_scatter(grads, PLANE, scatter_dimension=0, tiled=True)  29.6 us
    pallas_call x2, Pallas kernels, weight_grads(): pl.pallas_call(partial(grads_kernel, counts), grid=(features // STEP,), o...  25.5 us
    pallas_call x3, Pallas kernels, half_back(): pl.pallas_call(half_back_kernel, grid=(features // tile,), out_shape=[jax...  21 us
    pallas_call x1, Pallas kernels, mixer_backward(): pl.pallas_call(mixer_backward_kernel, out_shape=outs, in_specs=[SMEM] + v...  18.6 us
    pallas_call x2, Pallas kernels, act_back(): pl.pallas_call(act_back_kernel, grid=(count,), out_shape=[jax.ShapeDtypeS...  16.4 us
  transfers between devices with their start and end apart: 41, of which 28 were waited for; matrix products, arithmetic and copies ran while one was open for 8% of the time, Pallas kernels for 22%

profile of v3, /device:TPU:0, one launch (start us, length us, event | category | flops | bytes accessed | tf_op | source)
XLA Modules:
  0.0 503.7 jit_solution(11312042996658112474)
XLA Ops:
  12.3 5.1 %collective-permute-done.1.refs_3_ = bf16[64,128]{1,0:T(8,128)(2,1)S(1)} collective-permute-done((bf16[64,128]{1,0:T(8,128)(2,1)S(1)}, bf16[64,128]{1,0:T(8,128)(2,1)S(1)}, u32[]{:S(2)}, u32[]{:S(2)}) %collective-permute-start.1) | collective-permute-done | bytes 16416 | tf_op jit(solution)/shard_map/ppermute | solution.py:903
  23.6 9.3 %collective-permute-done.12.refs_1_ = bf16[64,3456]{1,0:T(8,128)(2,1)S(1)} collective-permute-done((bf16[64,3456]{1,0:T(8,128)(2,1)S(1)}, bf16[64,3456]{1,0:T(8,128)(2,1)S(1)}, u32[]{:S(2)}, u32[]{:S(2)}) %collective-permute-start.12) | collective-permute-done | bytes 442400 | tf_op jit(solution)/shard_map/ppermute | solution.py:903
  42.2 8.7 %collective-permute-done.3.x2 = bf16[128,2048]{1,0:T(8,128)(2,1)S(1)} collective-permute-done((bf16[128,2048]{1,0:T(8,128)(2,1)S(1)}, bf16[128,2048]{1,0:T(8,128)(2,1)S(1)}, u32[]{:S(2)}, u32[]{:S(2)}) %collective-permute-start.3) | collective-permute-done | bytes 524320 | tf_op jit(solution)/shard_map/ppermute | solution.py:903
  52.9 51.1 %all-gather.5.cloned.1.call-done.small.weights = bf16[2048,2560]{1,0:T(8,128)(2,1)} async-done(((bf16[128,2560]{1,0:T(8,128)(2,1)}), bf16[2048,2560]{1,0:T(8,128)(2,1)}) %all-gather.5.cloned.1.call-update) | async-done | bytes 10485776 | tf_op jit(solution)/shard_map/all_gather | solution.py:927
  109.2 12.2 %project.1 = (f32[512,1664]{1,0:T(8,128)}, bf16[512,2048]{1,0:T(8,128)(2,1)}, f32[8,2048]{1,0:T(8,128)}) custom-call(s32[4]{0:T(128)} %pad_add_fusion.places, bf16[128,2048]{1,0:T(8,128)(2,1)} %copy-done, bf16[128,2048]{1,0:T(8,128)(2,1)} %copy-done.36, bf16[128,2048]{1,0:T(8,128)(2,1)} %copy-done.35, bf16[128,2048]{1,0:T(8,128)(2,1)} %copy-done.37, ...), custom_call_target="tpu_custom_call" | custom-call | flops 12000000000 | bytes 36000000 | tf_op jit(solution)/shard_map/project/pallas_call | solution.py:482
  121.4 12.4 %mixer_forward.1 = (bf16[512,512]{1,0:T(8,128)(2,1)}, f32[512,1024]{1,0:T(8,128)}, f32[8,128,128]{2,1,0:T(8,128)}, f32[8,128,128]{2,1,0:T(8,128)}, f32[8,128,128...) custom-call(s32[2]{0:T(128)} %bitcast.105, ...), custom_call_target="tpu_custom_call" | custom-call | flops 12499999744 | bytes 37500000 | tf_op jit(solution)/shard_map/mixer_forward/pallas_call | solution.py:406
  133.8 10.1 %collective-permute-done.5.low_across = bf16[1024,768]{1,0:T(8,128)(2,1)S(1)} collective-permute-done((bf16[1024,768]{1,0:T(8,128)(2,1)S(1)}, bf16[1024,768]{1,0:T(8,128)(2,1)S(1)}, u32[]{:S(2)}, u32[]{:S(2)}) %collective-permute-start.5) | collective-permute-done | bytes 1572896 | tf_op jit(solution)/shard_map/ppermute | solution.py:903
  143.8 5.8 %mix_out.1 = (f32[128,2048]{1,0:T(8,128)}, bf16[128,2048]{1,0:T(8,128)(2,1)}, f32[128,2048]{1,0:T(8,128)}, bf16[128,2048]{1,0:T(8,128)(2,1)}, bf16[512,512]{1,0:T(8,128)(2,1)}) custom-call(s32[4]{0:T(128)} %pad_add_fusion.places, bf16[512,512]{1,0:T(8,128)(2,1)} %get-tuple-element.94.gated, bf16[2048,2560]{1,0:T(8,128)(2,1)} %all-gather.5.cloned.1.call-done.small.weights), custom_call_target="tpu_custom_call" | custom-call | flops 5000000000 | bytes 15000000 | tf_op jit(solution)/shard_map/mix_out/pallas_call | solution.py:531
  158.3 10.9 %collective-permute-done.8 = bf16[128,2048]{1,0:T(8,128)(2,1)S(1)} collective-permute-done((bf16[128,2048]{1,0:T(8,128)(2,1)S(1)}, bf16[128,2048]{1,0:T(8,128)(2,1)S(1)}, u32[]{:S(2)}, u32[]{:S(2)}) %collective-permute-start.8) | collective-permute-done | bytes 524320 | tf_op jit(solution)/shard_map/ppermute | solution.py:903
  172.9 11.6 %collective-permute-done.10.x2 = bf16[128,2048]{1,0:T(8,128)(2,1)S(1)} collective-permute-done((bf16[128,2048]{1,0:T(8,128)(2,1)S(1)}, bf16[128,2048]{1,0:T(8,128)(2,1)S(1)}, u32[]{:S(2)}, u32[]{:S(2)}) %collective-permute-start.10) | collective-permute-done | bytes 524320 | tf_op jit(solution)/shard_map/ppermute | solution.py:903
  186.5 17.4 %all-gather.7.cloned.1.call-done.weights.refs_0_.refs_1_.refs_2_.refs_3_.refs_4_ = bf16[2048,3456]{1,0:T(8,128)(2,1)} async-done(((bf16[128,3456]{1,0:T(8,128)(2,1)}), bf16[2048,3456]{1,0:T(8,128)(2,1)}) %all-gather.7.cloned.1.call-update) | async-done | bytes 14155792 | tf_op jit(solution)/shard_map/all_gather | solution.py:927
  203.9 12.9 %gate_up.1 = (bf16[512,1408]{1,0:T(8,128)(2,1)}, f32[512,1408]{1,0:T(8,128)}, f32[512,1408]{1,0:T(8,128)}, bf16[512,2048]{1,0:T(8,128)(2,1)}) custom-call(bf16[128,2048]{1,0:T(8,128)(2,1)} %copy-done.18, bf16[128,2048]{1,0:T(8,128)(2,1)} %copy-done.40, bf16[128,2048]{1,0:T(8,128)(2,1)} %copy-done.38, bf16[128,2048]{1,0:T(8,128)(2,1)} %copy-done.43, ...), custom_call_target="tpu_custom_call" | custom-call | flops 12499999744 | bytes 37500000 | tf_op jit(solution)/shard_map/gate_up/pallas_call | solution.py:570
  216.8 6.5 %down_first.1 = (f32[128,2048]{1,0:T(8,128)}, bf16[128,2048]{1,0:T(8,128)(2,1)}, bf16[2048,1408]{1,0:T(8,128)(2,1)}) custom-call(bf16[512,1408]{1,0:T(8,128)(2,1)} %get-tuple-element.104.left.refs_7_.refs_9_, bf16[1024,768]{1,0:T(8,128)(2,1)} %bitcast.65, bf16[1024,768]{1,0:T(8,128)(2,1)} %copy-done.10, ...), custom_call_target="tpu_custom_call" | custom-call | flops 6000000000 | bytes 18000000 | tf_op jit(solution)/shard_map/down_first/pallas_call | solution.py:640
  230.6 4.9 down_near.1
  237.3 6.1 %collective-permute-done.15 = bf16[128,2048]{1,0:T(8,128)(2,1)} collective-permute-done((bf16[128,2048]{1,0:T(8,128)(2,1)}, bf16[128,2048]{1,0:T(8,128)(2,1)}, u32[]{:S(2)}, u32[]{:S(2)}) %collective-permute-start.15) | collective-permute-done | bytes 524320 | tf_op jit(solution)/shard_map/ppermute | solution.py:903
  249.3 8.2 %act_back.2 = (bf16[256,2816]{1,0:T(8,128)(2,1)}, bf16[256,2048]{1,0:T(8,128)(2,1)}) custom-call(bf16[128,2048]{1,0:T(8,128)(2,1)} %copy-done.15, bf16[128,2048]{1,0:T(8,128)(2,1)} %copy-done.45, bf16[2048,1408]{1,0:T(8,128)(2,1)} %get-tuple-element.105.weights, f32[512,1408]{1,0:T(8,128)} %get-tuple-element.110.gate, f32[512,1408]{1,0:T(8,128)} %get-tuple-element.111.up), custom_call_target="tpu_custom_call" | custom-call | flops 8000000000 | bytes 24000000 | tf_op jit(solution)/shard_map/act_back/pallas_call | solution.py:698
  257.5 3.8 collective-permute-done.16.x0
  264.0 8.2 %act_back.3 = (bf16[256,2816]{1,0:T(8,128)(2,1)}, bf16[256,2048]{1,0:T(8,128)(2,1)}) custom-call(bf16[128,2048]{1,0:T(8,128)(2,1)} %copy-done.41, bf16[128,2048]{1,0:T(8,128)(2,1)} %copy-done.46, bf16[2048,1408]{1,0:T(8,128)(2,1)} %get-tuple-element.105.weights, f32[512,1408]{1,0:T(8,128)} %get-tuple-element.110.gate, f32[512,1408]{1,0:T(8,128)} %get-tuple-element.111.up), custom_call_target="tpu_custom_call" | custom-call | flops 8000000000 | bytes 24000000 | tf_op jit(solution)/shard_map/act_back/pallas_call | solution.py:698
  272.3 10.5 %units_grads.1 = bf16[2048,2816]{1,0:T(8,128)(2,1)} custom-call(bf16[512,2048]{1,0:T(8,128)(2,1)} %get-tuple-element.109.refs_0_.refs_2_, bf16[256,2816]{1,0:T(8,128)(2,1)} %get-tuple-element.120.refs_1_.left, bf16[512,2048]{1,0:T(8,128)(2,1)} %get-tuple-element.109.refs_0_.refs_2_, bf16[256,2816]{1,0:T(8,128)(2,1)} %get-tuple-element.116.refs_3_.left), custom_call_target="tpu_custom_call" | custom-call | flops 10499999744 | bytes 31500000 | tf_op jit(solution)/shard_map/units_grads/pallas_call | solution.py:834
  282.8 8.0 %normed_far.1 = (f32[128,2048]{1,0:T(8,128)}, bf16[128,2048]{1,0:T(8,128)(2,1)}) custom-call(bf16[256,2816]{1,0:T(8,128)(2,1)} %get-tuple-element.116.refs_3_.left, bf16[2048,3456]{1,0:T(8,128)(2,1)} %all-gather.7.cloned.1.call-done.weights.refs_0_.refs_1_.refs_2_.refs_3_.refs_4_), custom_call_target="tpu_custom_call" | custom-call | flops 8000000000 | bytes 24000000 | tf_op jit(solution)/shard_map/normed_far/pallas_call | solution.py:604
  297.4 8.1 %normed_near.1 = (f32[128,2048]{1,0:T(8,128)}, bf16[128,2048]{1,0:T(8,128)(2,1)}) custom-call(bf16[256,2816]{1,0:T(8,128)(2,1)} %get-tuple-element.120.refs_1_.left, bf16[2048,3456]{1,0:T(8,128)(2,1)} %all-gather.7.cloned.1.call-done.weights.refs_0_.refs_1_.refs_2_.refs_3_.refs_4_), custom_call_target="tpu_custom_call" | custom-call | flops 8000000000 | bytes 24000000 | tf_op jit(solution)/shard_map/normed_near/pallas_call | solution.py:604
  305.5 4.4 collective-permute-done.21
  316.1 11.7 %collective-permute-done.23.x2 = bf16[128,2048]{1,0:T(8,128)(2,1)S(1)} collective-permute-done((bf16[128,2048]{1,0:T(8,128)(2,1)S(1)}, bf16[128,2048]{1,0:T(8,128)(2,1)S(1)}, u32[]{:S(2)}, u32[]{:S(2)}) %collective-permute-start.23) | collective-permute-done | bytes 524320 | tf_op jit(solution)/shard_map/ppermute | solution.py:903
  330.6 6.5 %gated_back.1 = (f32[512,512]{1,0:T(8,128)}, bf16[512,512]{1,0:T(8,128)(2,1)}, f32[8,256]{1,0:T(8,128)}, bf16[512,2048]{1,0:T(8,128)(2,1)}) custom-call(s32[4]{0:T(128)} %pad_add_fusion.places, bf16[128,2048]{1,0:T(8,128)(2,1)} %copy-done.14, bf16[128,2048]{1,0:T(8,128)(2,1)} %copy-done.42, bf16[128,2048]{1,0:T(8,128)(2,1)} %copy-done.39, ...), custom_call_target="tpu_custom_call" | custom-call | flops 6499999744 | bytes 19500000 | tf_op jit(solution)/shard_map/gated_back/pallas_call | solution.py:752
  337.1 18.6 %mixer_backward.1 = (bf16[512,1152]{1,0:T(8,128)(2,1)}, f32[8,1024]{1,0:T(8,128)}, f32[8,128]{1,0:T(8,128)}) custom-call(s32[2]{0:T(128)} %bitcast.106, f32[512,512]{1,0:T(8,128)} %get-tuple-element.129.grad_mixed, f32[512,1664]{1,0:T(8,128)} %get-tuple-element.91.raw.raw_gate, f32[4,1024]{1,0:T(4,128)} %maximum_convert_fusion.taps, ...), custom_call_target="tpu_custom_call" | custom-call | flops 18499999744 | bytes 55500000 | tf_op jit(solution)/shard_map/mixer_backward/pallas_call | solution.py:423
  355.7 15.0 %mixer_grads.1 = bf16[2048,3584]{1,0:T(8,128)(2,1)} custom-call(bf16[512,2048]{1,0:T(8,128)(2,1)} %get-tuple-element.126.refs_0_, bf16[512,512]{1,0:T(8,128)(2,1)} %get-tuple-element.127.refs_1_, bf16[512,2048]{1,0:T(8,128)(2,1)} %get-tuple-element.128.refs_2_.refs_4_, bf16[512,512]{1,0:T(8,128)(2,1)} %get-tuple-element.125.refs_3_.gate, ...), custom_call_target="tpu_custom_call" | custom-call | flops 14499999744 | bytes 43500000 | tf_op jit(solution)/shard_map/mixer_grads/pallas_call | solution.py:834
  370.7 8.6 %input_back.1 = (f32[128,2048]{1,0:T(8,128)}, bf16[128,2048]{1,0:T(8,128)(2,1)}, f32[128,2048]{1,0:T(8,128)}, bf16[128,2048]{1,0:T(8,128)(2,1)}) custom-call(s32[4]{0:T(128)} %pad_add_fusion.places, bf16[512,512]{1,0:T(8,128)(2,1)} %get-tuple-element.125.refs_3_.gate, bf16[512,1152]{1,0:T(8,128)(2,1)} %get-tuple-element.140.refs_5_.conv, ...), custom_call_target="tpu_custom_call" | custom-call | flops 8499999744 | bytes 25500000 | tf_op jit(solution)/shard_map/input_back/pallas_call | solution.py:789
  389.2 10.6 %collective-permute-done.27 = bf16[128,2048]{1,0:T(8,128)(2,1)} collective-permute-done((bf16[128,2048]{1,0:T(8,128)(2,1)}, bf16[128,2048]{1,0:T(8,128)(2,1)}, u32[]{:S(2)}, u32[]{:S(2)}) %collective-permute-start.27) | collective-permute-done | bytes 524320 | tf_op jit(solution)/shard_map/ppermute | solution.py:903
  419.1 4.0 collective-permute-done.31
  440.2 6.9 %collective-permute-done.36 = bf16[64,2816]{1,0:T(8,128)(2,1)S(1)} collective-permute-done((bf16[64,2816]{1,0:T(8,128)(2,1)S(1)}, bf16[64,2816]{1,0:T(8,128)(2,1)S(1)}, u32[]{:S(2)}, u32[]{:S(2)}) %collective-permute-start.36) | collective-permute-done | bytes 360480 | tf_op jit(solution)/shard_map/ppermute | solution.py:903
  450.5 29.6 %reduce-scatter.3.cloned.1.call-done = bf16[128,3584]{1,0:T(8,128)(2,1)} async-done(((bf16[2048,3584]{1,0:T(8,128)(2,1)}), bf16[128,3584]{1,0:T(8,128)(2,1)}) %reduce-scatter.3.cloned.1.call-update) | async-done | bytes 917520 | tf_op jit(solution)/shard_map/reduce_scatter | solution.py:931
  483.9 9.4 %collective-permute-done.35 = bf16[64,3584]{1,0:T(8,128)(2,1)S(1)} collective-permute-done((bf16[64,3584]{1,0:T(8,128)(2,1)S(1)}, bf16[64,3584]{1,0:T(8,128)(2,1)S(1)}, u32[]{:S(2)}, u32[]{:S(2)}) %collective-permute-start.35) | collective-permute-done | bytes 458784 | tf_op jit(solution)/shard_map/ppermute | solution.py:903
  (283 shorter events, 131.0 us)
Async XLA Ops:
  7.2 96.8 %all-gather.5.cloned.1.call-start = ((), (), s32[]{:S(2)}) async-start(), calls=%async_computation.4 | async-start | bytes 11141120 | tf_op jit(solution)/shard_map/all_gather | solution.py:927
  9.0 8.4 %collective-permute-start = (bf16[64,2048]{1,0:T(8,128)(2,1)}, bf16[64,2048]{1,0:T(8,128)(2,1)S(1)}, u32[]{:S(2)}, u32[]{:S(2)}) collective-permute-start(bf16[64,2048]{1,0:T(8,128)(2,1)} %pack.1.refs_0_), channel_id=1, source_target_pairs={{0,64},{64,0},{1,65},{65,1},{2,66},{66,2},{3,67},{67,3},{4,68},{68... | collective-permute-start | bytes 786440 | tf_op jit(solution)/shard_map/ppermute | solution.py:903
  11.2 6.3 %collective-permute-start.1 = (bf16[64,128]{1,0:T(8,128)(2,1)S(1)}, bf16[64,128]{1,0:T(8,128)(2,1)S(1)}, u32[]{:S(2)}, u32[]{:S(2)}) collective-permute-start(bf16[64,128]{1,0:T(8,128)(2,1)S(1)} %concatenate.29.refs_2_), channel_id=1, source_target_pairs={{0,64},{64,0},{1,65},{65,1},{2,66},{66,2},{3,67},{67,3},{4,68},{68... | collective-permute-start | bytes 49160 | tf_op jit(solution)/shard_map/ppermute | solution.py:903
  20.7 183.1 %all-gather.7.cloned.1.call-start = ((), (), s32[]{:S(2)}) async-start(), calls=%async_computation.5 | async-start | bytes 15040512 | tf_op jit(solution)/shard_map/all_gather | solution.py:927
  21.8 11.1 %collective-permute-start.12 = (bf16[64,3456]{1,0:T(8,128)(2,1)S(1)}, bf16[64,3456]{1,0:T(8,128)(2,1)S(1)}, u32[]{:S(2)}, u32[]{:S(2)}) collective-permute-start(bf16[64,3456]{1,0:T(8,128)(2,1)S(1)} %pad_maximum_fusion.5.refs_0_), channel_id=1, source_target_pairs={{0,64},{64,0},{1,65},{65,1},{2,66},{66,2},{3,67},{67,3},{4,68},{68... | collective-permute-start | bytes 1327112 | tf_op jit(solution)/shard_map/ppermute | solution.py:903
  35.9 399.0 %reduce-scatter.5.cloned.1.call-start = ((), (), s32[]{:S(2)}) async-start(), calls=%async_computation.3 | async-start | bytes 12255232 | tf_op jit(solution)/shard_map/reduce_scatter | solution.py:931
  37.4 13.5 %collective-permute-start.3 = (bf16[128,2048]{1,0:T(8,128)(2,1)S(1)}, bf16[128,2048]{1,0:T(8,128)(2,1)S(1)}, u32[]{:S(2)}, u32[]{:S(2)}) collective-permute-start(bf16[128,2048]{1,0:T(8,128)(2,1)S(1)} %copy.66.x0), channel_id=1, source_target_pairs={{0,2},{2,0},{1,3},{3,1},{4,6},{6,4},{5,7},{7,5},{8,10},{10,8},{9,1... | collective-permute-start | bytes 1572872 | tf_op jit(solution)/shard_map/ppermute | solution.py:903
  40.8 12.2 %collective-permute-start.2 = (bf16[128,2048]{1,0:T(8,128)(2,1)S(1)}, bf16[128,2048]{1,0:T(8,128)(2,1)S(1)}, u32[]{:S(2)}, u32[]{:S(2)}) collective-permute-start(bf16[128,2048]{1,0:T(8,128)(2,1)S(1)} %copy.66.x0), channel_id=1, source_target_pairs={{0,1},{1,0},{2,3},{3,2},{4,5},{5,4},{6,7},{7,6},{8,9},{9,8},{10,11... | collective-permute-start | bytes 1572872 | tf_op jit(solution)/shard_map/ppermute | solution.py:903
  107.4 36.4 %collective-permute-start.5 = (bf16[1024,768]{1,0:T(8,128)(2,1)S(1)}, bf16[1024,768]{1,0:T(8,128)(2,1)S(1)}, u32[]{:S(2)}, u32[]{:S(2)}) collective-permute-start(bf16[1024,768]{1,0:T(8,128)(2,1)S(1)} %bitcast.64), channel_id=1, source_target_pairs={{0,64},{64,0},{1,65},{65,1},{2,66},{66,2},{3,67},{67,3},{4,68},{68... | collective-permute-start | bytes 4718600 | tf_op jit(solution)/shard_map/ppermute | solution.py:903
  149.8 8.5 %collective-permute-start.6 = (bf16[128,2048]{1,0:T(8,128)(2,1)}, bf16[128,2048]{1,0:T(8,128)(2,1)S(1)}, u32[]{:S(2)}, u32[]{:S(2)}) collective-permute-start(bf16[128,2048]{1,0:T(8,128)(2,1)} %get-tuple-element.96), channel_id=1, source_target_pairs={{0,1},{1,0},{2,3},{3,2},{4,5},{5,4},{6,7},{7,6},{8,9},{9,8},{10,11... | collective-permute-start | bytes 1572872 | tf_op jit(solution)/shard_map/ppermute | solution.py:903
  153.3 16.0 %collective-permute-start.8 = (bf16[128,2048]{1,0:T(8,128)(2,1)S(1)}, bf16[128,2048]{1,0:T(8,128)(2,1)S(1)}, u32[]{:S(2)}, u32[]{:S(2)}) collective-permute-start(bf16[128,2048]{1,0:T(8,128)(2,1)S(1)} %add_convert_fusion.3), channel_id=1, source_target_pairs={{0,2},{2,0},{1,3},{3,1},{4,6},{6,4},{5,7},{7,5},{8,10},{10,8},{9,1... | collective-permute-start | bytes 1572872 | tf_op jit(solution)/shard_map/ppermute | solution.py:903
  169.8 14.7 %collective-permute-start.10 = (bf16[128,2048]{1,0:T(8,128)(2,1)S(1)}, bf16[128,2048]{1,0:T(8,128)(2,1)S(1)}, u32[]{:S(2)}, u32[]{:S(2)}) collective-permute-start(bf16[128,2048]{1,0:T(8,128)(2,1)S(1)} %multiply_convert_fusion.x0), channel_id=1, source_target_pairs={{0,2},{2,0},{1,3},{3,1},{4,6},{6,4},{5,7},{7,5},{8,10},{10,8},{9,1... | collective-permute-start | bytes 1572872 | tf_op jit(solution)/shard_map/ppermute | solution.py:903
  172.9 11.6 %collective-permute-start.9 = (bf16[128,2048]{1,0:T(8,128)(2,1)S(1)}, bf16[128,2048]{1,0:T(8,128)(2,1)S(1)}, u32[]{:S(2)}, u32[]{:S(2)}) collective-permute-start(bf16[128,2048]{1,0:T(8,128)(2,1)S(1)} %multiply_convert_fusion.x0), channel_id=1, source_target_pairs={{0,1},{1,0},{2,3},{3,2},{4,5},{5,4},{6,7},{7,6},{8,9},{9,8},{10,11... | collective-permute-start | bytes 1572872 | tf_op jit(solution)/shard_map/ppermute | solution.py:903
  227.6 15.8 %collective-permute-start.15 = (bf16[128,2048]{1,0:T(8,128)(2,1)}, bf16[128,2048]{1,0:T(8,128)(2,1)}, u32[]{:S(2)}, u32[]{:S(2)}) collective-permute-start(bf16[128,2048]{1,0:T(8,128)(2,1)} %add_convert_fusion.2), channel_id=1, source_target_pairs={{0,2},{2,0},{1,3},{3,1},{4,6},{6,4},{5,7},{7,5},{8,10},{10,8},{9,1... | collective-permute-start | bytes 1572872 | tf_op jit(solution)/shard_map/ppermute | solution.py:903
  235.5 7.9 %collective-permute-start.14 = (bf16[128,2048]{1,0:T(8,128)(2,1)}, bf16[128,2048]{1,0:T(8,128)(2,1)}, u32[]{:S(2)}, u32[]{:S(2)}) collective-permute-start(bf16[128,2048]{1,0:T(8,128)(2,1)} %get-tuple-element.107), channel_id=1, source_target_pairs={{0,1},{1,0},{2,3},{3,2},{4,5},{5,4},{6,7},{7,6},{8,9},{9,8},{10,11... | collective-permute-start | bytes 1572872 | tf_op jit(solution)/shard_map/ppermute | solution.py:903
  245.5 15.8 %collective-permute-start.16 = (bf16[128,2048]{1,0:T(8,128)(2,1)S(1)}, bf16[128,2048]{1,0:T(8,128)(2,1)S(1)}, u32[]{:S(2)}, u32[]{:S(2)}) collective-permute-start(bf16[128,2048]{1,0:T(8,128)(2,1)S(1)} %get-tuple-element.200.x0), channel_id=1, source_target_pairs={{0,2},{2,0},{1,3},{3,1},{4,6},{6,4},{5,7},{7,5},{8,10},{10,8},{9,1... | collective-permute-start | bytes 1572872 | tf_op jit(solution)/shard_map/ppermute | solution.py:903
  282.8 197.3 %reduce-scatter.3.cloned.1.call-start = ((), (), s32[]{:S(2)}) async-start(), calls=%async_computation.2 | async-start | bytes 15597568 | tf_op jit(solution)/shard_map/reduce_scatter | solution.py:931
  294.3 15.6 %collective-permute-start.21 = (bf16[128,2048]{1,0:T(8,128)(2,1)S(1)}, bf16[128,2048]{1,0:T(8,128)(2,1)S(1)}, u32[]{:S(2)}, u32[]{:S(2)}) collective-permute-start(bf16[128,2048]{1,0:T(8,128)(2,1)S(1)} %add_convert_fusion.1), channel_id=1, source_target_pairs={{0,2},{2,0},{1,3},{3,1},{4,6},{6,4},{5,7},{7,5},{8,10},{10,8},{9,1... | collective-permute-start | bytes 1572872 | tf_op jit(solution)/shard_map/ppermute | solution.py:903
  305.5 4.4 collective-permute-start.20
  313.1 14.6 %collective-permute-start.23 = (bf16[128,2048]{1,0:T(8,128)(2,1)S(1)}, bf16[128,2048]{1,0:T(8,128)(2,1)S(1)}, u32[]{:S(2)}, u32[]{:S(2)}) collective-permute-start(bf16[128,2048]{1,0:T(8,128)(2,1)S(1)} %get-tuple-element.198.x0), channel_id=1, source_target_pairs={{0,2},{2,0},{1,3},{3,1},{4,6},{6,4},{5,7},{7,5},{8,10},{10,8},{9,1... | collective-permute-start | bytes 1572872 | tf_op jit(solution)/shard_map/ppermute | solution.py:903
  316.1 11.8 %collective-permute-start.22 = (bf16[128,2048]{1,0:T(8,128)(2,1)S(1)}, bf16[128,2048]{1,0:T(8,128)(2,1)S(1)}, u32[]{:S(2)}, u32[]{:S(2)}) collective-permute-start(bf16[128,2048]{1,0:T(8,128)(2,1)S(1)} %get-tuple-element.198.x0), channel_id=1, source_target_pairs={{0,1},{1,0},{2,3},{3,2},{4,5},{5,4},{6,7},{7,6},{8,9},{9,8},{10,11... | collective-permute-start | bytes 1572872 | tf_op jit(solution)/shard_map/ppermute | solution.py:903
  379.8 9.4 %collective-permute-start.25 = (bf16[128,2048]{1,0:T(8,128)(2,1)}, bf16[128,2048]{1,0:T(8,128)(2,1)}, u32[]{:S(2)}, u32[]{:S(2)}) collective-permute-start(bf16[128,2048]{1,0:T(8,128)(2,1)} %get-tuple-element.142), channel_id=1, source_target_pairs={{0,1},{1,0},{2,3},{3,2},{4,5},{5,4},{6,7},{7,6},{8,9},{9,8},{10,11... | collective-permute-start | bytes 1572872 | tf_op jit(solution)/shard_map/ppermute | solution.py:903
  383.8 16.0 %collective-permute-start.27 = (bf16[128,2048]{1,0:T(8,128)(2,1)}, bf16[128,2048]{1,0:T(8,128)(2,1)}, u32[]{:S(2)}, u32[]{:S(2)}) collective-permute-start(bf16[128,2048]{1,0:T(8,128)(2,1)} %add_convert_fusion), channel_id=1, source_target_pairs={{0,2},{2,0},{1,3},{3,1},{4,6},{6,4},{5,7},{7,5},{8,10},{10,8},{9,1... | collective-permute-start | bytes 1572872 | tf_op jit(solution)/shard_map/ppermute | solution.py:903
  402.2 4.0 collective-permute-start.28
  406.2 5.8 %collective-permute-start.29 = (f32[72,128]{1,0:T(8,128)S(1)}, f32[72,128]{1,0:T(8,128)S(1)}, u32[]{:S(2)}, u32[]{:S(2)}) collective-permute-start(f32[72,128]{1,0:T(8,128)S(1)} %fusion.11), channel_id=1, source_target_pairs={{0,16},{16,0},{32,48},{48,32},{1,17},{17,1},{33,49},{49,33},{2,18}... | collective-permute-start | bytes 110600 | tf_op jit(solution)/shard_map/ppermute | solution.py:961
  412.0 6.5 %collective-permute-start.30 = (f32[72,128]{1,0:T(8,128)S(1)}, f32[72,128]{1,0:T(8,128)S(1)}, u32[]{:S(2)}, u32[]{:S(2)}) collective-permute-start(f32[72,128]{1,0:T(8,128)S(1)} %fusion.20), channel_id=1, source_target_pairs={{0,32},{16,48},{32,0},{48,16},{1,33},{17,49},{33,1},{49,17},{2,34}... | collective-permute-start | bytes 110600 | tf_op jit(solution)/shard_map/ppermute | solution.py:961
  418.6 4.5 collective-permute-start.31
  423.1 6.4 %collective-permute-start.32 = (f32[72,128]{1,0:T(8,128)S(1)}, f32[72,128]{1,0:T(8,128)S(1)}, u32[]{:S(2)}, u32[]{:S(2)}) collective-permute-start(f32[72,128]{1,0:T(8,128)S(1)} %add.171), channel_id=1, source_target_pairs={{0,8},{4,12},{8,0},{12,4},{1,9},{5,13},{9,1},{13,5},{2,10},{6,14},... | collective-permute-start | bytes 110600 | tf_op jit(solution)/shard_map/ppermute | solution.py:961
  429.5 5.4 %collective-permute-start.33 = (f32[34,128]{1,0:T(8,128)S(1)}, f32[34,128]{1,0:T(8,128)S(1)}, u32[]{:S(2)}, u32[]{:S(2)}) collective-permute-start(f32[34,128]{1,0:T(8,128)S(1)} %slice.188), channel_id=1, source_target_pairs={{0,2},{2,0},{1,3},{3,1},{4,6},{6,4},{5,7},{7,5},{8,10},{10,8},{9,1... | collective-permute-start | bytes 52232 | tf_op jit(solution)/shard_map/ppermute | solution.py:961
  434.9 4.2 collective-permute-start.34
  436.0 11.2 %collective-permute-start.36 = (bf16[64,2816]{1,0:T(8,128)(2,1)S(1)}, bf16[64,2816]{1,0:T(8,128)(2,1)S(1)}, u32[]{:S(2)}, u32[]{:S(2)}) collective-permute-start(bf16[64,2816]{1,0:T(8,128)(2,1)S(1)} %slice.206), channel_id=1, source_target_pairs={{0,64},{64,0},{1,65},{65,1},{2,66},{66,2},{3,67},{67,3},{4,68},{68... | collective-permute-start | bytes 1081352 | tf_op jit(solution)/shard_map/ppermute | solution.py:903
  481.2 12.0 %collective-permute-start.35 = (bf16[64,3584]{1,0:T(8,128)(2,1)S(1)}, bf16[64,3584]{1,0:T(8,128)(2,1)S(1)}, u32[]{:S(2)}, u32[]{:S(2)}) collective-permute-start(bf16[64,3584]{1,0:T(8,128)(2,1)S(1)} %slice.190), channel_id=1, source_target_pairs={{0,64},{64,0},{1,65},{65,1},{2,66},{66,2},{3,67},{67,3},{4,68},{68... | collective-permute-start | bytes 1376264 | tf_op jit(solution)/shard_map/ppermute | solution.py:903
  (64 other events, 709.5 us)
Sparse Core Ops, SparseCore 0:
  20.8 83.1 all-gather.4
  106.2 97.6 all-gather.6
  282.9 91.5 reduce-scatter.4
  378.2 101.8 reduce-scatter.2

commit v4 on v3

--- a/solution.py
+++ b/solution.py
@@ -437,7 +437,9 @@
 TILE = 512
 STEP = 512
 WIDE = 384
-HALF = 768
+HALF = 1024
+FIRST = 768
+EARLY = 512
 
 
 def whole(*shape):
@@ -616,12 +618,15 @@
     )(left, weights)
 
 
-def down_first_kernel(left, low, low_across, *refs):
+def down_first_kernel(left, low, early, late, *refs):
     *high, kept, sent, weights = refs
     for b in range(low.shape[0] // 64):
-        for o, half in enumerate((low, low_across)):
-            rows = slice(b * 128 + o * 64, b * 128 + o * 64 + 64)
-            weights[rows, :HALF] = half[b * 64 : b * 64 + 64]
+        own = slice(b * 128, b * 128 + 64)
+        other = slice(b * 128 + 64, b * 128 + 128)
+        part = slice(b * 64, b * 64 + 64)
+        weights[own, :HALF] = low[part]
+        weights[other, :FIRST] = early[part]
+        weights[other, FIRST:HALF] = late[part]
     for i, block in enumerate(high):
         weights[:, HALF + i * 128 : HALF + (i + 1) * 128] = block[...]
     product = contract(left[...], weights[...], NT)
@@ -629,12 +634,14 @@
     sent[...] = product[OWN:].astype(BF16)
 
 
-def down_first(left, part, low, low_across, full):
+def down_first(left, part, low, early, late, full):
     features = full.shape[0]
     width = left.shape[1]
     tile = 2 * STEP
     shape = (OWN, features)
-    half = pl.BlockSpec((tile // 2, HALF), lambda i: (i, 0))
+    parts = [
+        pl.BlockSpec((tile // 2, half.shape[1]), lambda i: (i, 0)) for half in (low, early, late)
+    ]
     column = pl.BlockSpec((OWN, tile), lambda i: (0, i))
     blocks = range((full.shape[1] + HALF - width) // 128, full.shape[1] // 128)
     return pl.pallas_call(
@@ -645,13 +652,14 @@
             jax.ShapeDtypeStruct(shape, BF16),
             jax.ShapeDtypeStruct((features, width), BF16),
         ],
-        in_specs=[pl.BlockSpec((2 * OWN, width), lambda i: (part, 0)), half, half]
+        in_specs=[pl.BlockSpec((2 * OWN, width), lambda i: (part, 0))]
+        + parts
         + [pl.BlockSpec((tile, 128), partial(lambda b, i: (i, b), b)) for b in blocks],
         out_specs=[column, column, pl.BlockSpec((tile, width), lambda i: (i, 0))],
         compiler_params=LIMIT,
         cost_estimate=lasting(6),
         name="down_first",
-    )(left, low, low_across, *[full] * len(blocks))
+    )(left, low, early, late, *[full] * len(blocks))
 
 
 def act_back_kernel(x0, x1, weights, gate, up, grads, rows, steps, total, gates, ups):
@@ -893,6 +901,117 @@
         cost_estimate=lasting(2),
         name="pack_both",
     )(*operands)
+
+
+def down_part_kernel(left_a, right_a, left_b, right_b, own, other):
+    product = contract(left_a[...], right_a[...], TN) + contract(left_b[...], right_b[...], TN)
+    product = product.astype(BF16)
+    for b in range(STEP // 128):
+        own[b * 64 : b * 64 + 64] = product[b * 128 : b * 128 + 64]
+        other[b * 64 : b * 64 + 64] = product[b * 128 + 64 : b * 128 + 128]
+
+
+def down_part(near, far, act):
+    features = near.shape[1]
+    left = pl.BlockSpec((2 * OWN, STEP), lambda i: (0, i))
+    return pl.pallas_call(
+        down_part_kernel,
+        grid=(features // STEP,),
+        out_shape=[jax.ShapeDtypeStruct((features // 2, EARLY), BF16)] * 2,
+        in_specs=[
+            left,
+            pl.BlockSpec((2 * OWN, EARLY), lambda i: (0, 0)),
+            left,
+            pl.BlockSpec((2 * OWN, EARLY), lambda i: (1, 0)),
+        ],
+        out_specs=[pl.BlockSpec((STEP // 2, EARLY), lambda i: (i, 0))] * 2,
+        compiler_params=LIMIT,
+        cost_estimate=lasting(3),
+        name="down_part",
+    )(near, act, far, act)
+
+
+def last_grads_kernel(turned, gated, normed, gate, conv, near, far, act, own, other, out):
+    here = normed[...]
+    at = 0
+    for left, right in ((turned[...], gated), (here, gate), (here, conv)):
+        width = right.shape[1]
+        out[:, at : at + width] = contract(left, right[...], TN).astype(BF16)
+        at += width
+    down = contract(near[...], act[: 2 * OWN, EARLY:], TN)
+    down = down + contract(far[...], act[2 * OWN :, EARLY:], TN)
+    out[:, at : at + down.shape[1]] = down.astype(BF16)
+    at += down.shape[1]
+    total = (own[...].astype(F32) + other[...].astype(F32)).astype(BF16)
+    for b in range(STEP // 128):
+        rows = slice(b * 64, b * 64 + 64)
+        out[b * 128 : b * 128 + 64, at:] = total[rows, : EARLY // 2]
+        out[b * 128 + 64 : b * 128 + 128, at:] = total[rows, EARLY // 2 :]
+
+
+def last_grads(turned, gated, normed, gate, conv, near, far, act, own, other):
+    features = normed.shape[1]
+    width = VW + PROJ + act.shape[1] - EARLY // 2
+    left = pl.BlockSpec((ROWS, STEP), lambda i: (0, i))
+    half = pl.BlockSpec((2 * OWN, STEP), lambda i: (0, i))
+    early = pl.BlockSpec((STEP // 2, EARLY), lambda i: (i, 0))
+    return pl.pallas_call(
+        last_grads_kernel,
+        grid=(features // STEP,),
+        out_shape=jax.ShapeDtypeStruct((features, width), BF16),
+        in_specs=[
+            left,
+            whole(ROWS, VW),
+            left,
+            whole(ROWS, VW),
+            whole(ROWS, CONVW + SMALL),
+            half,
+            half,
+            whole(ROWS, act.shape[1]),
+            early,
+            early,
+        ],
+        out_specs=pl.BlockSpec((STEP, width), lambda i: (i, 0)),
+        compiler_params=LIMIT,
+        cost_estimate=lasting(13),
+        name="last_grads",
+    )(turned, gated, normed, gate, conv, near, far, act, own, other)
+
+
+def finish_kernel(both, arrived, out, gate, value, query, key, beta, decay, down):
+    rows = arrived.shape[0]
+
+    def total(left, right):
+        return both[:rows, left:right].astype(F32) + arrived[:, left:right].astype(F32)
+
+    at = 0
+    for ref in (out, gate, value, query, key):
+        ref[...] = total(at, at + ref.shape[1])
+        at += ref.shape[1]
+    small = total(at, at + SMALL).T
+    beta[...] = small[:HEADS]
+    decay[...] = small[HEADS : 2 * HEADS]
+    at += SMALL
+    end = arrived.shape[1]
+    down[:, : EARLY // 2] = both[:rows, end:].astype(F32)
+    down[:, EARLY // 2 : EARLY] = both[rows:, end:].astype(F32)
+    down[:, EARLY:] = total(at, end)
+
+
+def finish(both, arrived, units):
+    rows = arrived.shape[0]
+    widths = (VW, VW, VW, QK, QK)
+    return pl.pallas_call(
+        finish_kernel,
+        out_shape=[jax.ShapeDtypeStruct((rows, width), F32) for width in widths]
+        + [jax.ShapeDtypeStruct((HEADS, rows), F32)] * 2
+        + [jax.ShapeDtypeStruct((rows, units), F32)],
+        in_specs=vmem(2),
+        out_specs=vmem(8),
+        compiler_params=LIMIT,
+        cost_estimate=lasting(2),
+        name="finish",
+    )(both, arrived)
 
 
 SWAP = [(0, 1), (1, 0)]
@@ -1032,21 +1151,24 @@
     mixer_full, *input_blocks = lax.optimization_barrier((mixer_full, *gather_tokens(input_own)))
     down_low = mixer_full[:, VW + PROJ :].reshape(16, 2, rows_dp, HALF // 2)
     down_low = down_low.swapaxes(1, 2).reshape(-1, HALF)
-    down_low, mixer_full = lax.optimization_barrier((down_low, mixer_full))
-    low_across = trade(down_low, "xl")
+    low_first, low_last = down_low[:, :FIRST], down_low[:, FIRST:]
+    low_first, mixer_full = lax.optimization_barrier((low_first, mixer_full))
+    early = trade(low_first, "xl")
     raw, normed_one, gains = project(places, input_blocks, mixer_full)
     gain_first, gain_second = gains[0:1], gains[1:2]
     input_float = input_own.astype(jnp.float32)
     scale_one = lax.rsqrt(jnp.mean(input_float * input_float, axis=-1, keepdims=True) + EPSILON)
     gated_low, *saved, mixed = mixer_forward(boundary, raw, conv_taps, vectors, gain_mixer)
-    gated_low, low_across = lax.optimization_barrier((gated_low, low_across))
+    gated_low, early = lax.optimization_barrier((gated_low, early))
     *terms, gated_turned = mix_out(places, gated_low, mixer_full)
     hidden = input_float + scatter_tokens(*terms)
     scale_two = lax.rsqrt(jnp.mean(hidden * hidden, axis=-1, keepdims=True) + EPSILON)
     normed_two = (hidden * scale_two * gain_second).astype(jnp.bfloat16)
     blocks = gather_tokens(normed_two)
+    low_last, *blocks = lax.optimization_barrier((low_last, *blocks))
+    late = trade(low_last, "xl")
     act_low, gate_in, up_in, normed_rows = gate_up(blocks, ffn_full, f_width)
-    *far, down_full = down_first(act_low, 1, down_low, low_across, ffn_full)
+    *far, down_full = down_first(act_low, 1, down_low, early, late, ffn_full)
     layer_out = hidden + scatter_halves(
         far, lambda act: half_back(act, 0, down_full, 0, 1024, 5, "down_near"), act_low
     )
@@ -1079,24 +1201,34 @@
         * (scale_two * scale_two * scale_two)
         * jnp.mean(weighted_two * hidden, axis=-1, keepdims=True)
     )
+    down_own, down_other = down_part(rows_near, rows_far, act_low)
+    blocks = gather_tokens(grad_hidden.astype(jnp.bfloat16))
+    down_other, *blocks = lax.optimization_barrier((down_other, *blocks))
+    down_across = trade(down_other, "xl")
     grad_mixed, gate_low, gain_grad, grad_turned = gated_back(
-        places, gather_tokens(grad_hidden.astype(jnp.bfloat16)), mixer_full, raw, mixed, gain_mixer
+        places, blocks, mixer_full, raw, mixed, gain_mixer
     )
     raw_low, taps_grad, vectors_grad = mixer_backward(
         boundary, grad_mixed, raw, conv_taps, vectors, saved
     )
-    last_grad = weight_grads(
-        [
-            [((grad_turned, 0), (gated_turned, 0))],
-            [((normed_one, 0), (gate_low, 0))],
-            [((normed_one, 0), (raw_low, 0))],
-            [((rows_near, 0), (act_low, 0)), ((rows_far, 0), (act_low, 1))],
-        ],
-        14.5,
-        "mixer_grads",
+    last_grad = last_grads(
+        grad_turned,
+        gated_turned,
+        normed_one,
+        gate_low,
+        raw_low,
+        rows_near,
+        rows_far,
+        act_low,
+        down_own,
+        down_across,
     )
     last_grad, raw_low = lax.optimization_barrier((last_grad, raw_low))
-    last_sum = scatter_grads(last_grad)
+    last_both = lax.psum_scatter(last_grad, PLANE, scatter_dimension=0, tiled=True)
+    last_arrived = trade(last_both[rows_dp:, : last_grad.shape[1] - EARLY // 2], "xl")
+    out_grad, gate_grad, value_grad, query_grad, key_grad, beta_grad, decay_grad, down_grad = finish(
+        last_both, last_arrived, f_width
+    )
     grad_normed_one = scatter_tokens(*input_back(places, gate_low, raw_low, mixer_full))
     weighted_one = gain_first * grad_normed_one
     grad_gain_one = jnp.sum(grad_normed_one * input_float * scale_one, axis=0)
@@ -1128,31 +1260,28 @@
     heads_at = n_all + taps.size
     norm1_grad = lax.dynamic_slice_in_dim(shared, group_index * rows_dp, rows_dp)
     norm2_grad = lax.dynamic_slice_in_dim(shared, features + group_index * rows_dp, rows_dp)
-    q_at = 2 * VW + v_width
-    k_at = q_at + qk_width
-    small_at = k_at + qk_width
     units_sum = units_sum.reshape(rows_dp, -1, 2, 128)
     return (
         features_out(layer_out),
         features_out(grad_input),
         norm1_grad,
-        last_sum[:, q_at:k_at],
-        last_sum[:, k_at:small_at],
-        last_sum[:, 2 * VW : q_at],
-        last_sum[:, VW : 2 * VW],
-        last_sum[:, small_at : small_at + heads_here],
-        last_sum[:, small_at + heads_here : small_at + 2 * heads_here],
+        query_grad,
+        key_grad,
+        value_grad,
+        gate_grad,
+        beta_grad.T,
+        decay_grad.T,
         flat[heads_at : heads_at + heads_here],
         flat[heads_at + heads_here : heads_at + 2 * heads_here],
         taps_sum[:, v_width : v_width + qk_width],
         taps_sum[:, v_width + qk_width :],
         taps_sum[:, :v_width],
         shared[2 * features :],
-        last_sum[:, :VW],
+        out_grad,
         norm2_grad,
         units_sum[:, :, 0].reshape(rows_dp, f_width),
         units_sum[:, :, 1].reshape(rows_dp, f_width),
-        last_sum[:, VW + PROJ :],
+        down_grad,
     )
 
 

time: 510 us -> 503 us (0.986)
  waiting for transfers between devices: 231 us -> 217 us
  Pallas kernels: 152 us -> 158 us
    reduce_scatter x2 -> x1, waiting for transfers between devices: 29.6 us -> 0.02 us  [scatter_grads(): both = lax.psum_scatter(grads, PLANE, scatter_dimension=0, tiled=True)]
    reduce_scatter x0 -> x1, waiting for transfers between devices: none -> 21.7 us  [shards(): lax.psum_scatter(last_grad, PLANE, scatter_dimension=0, tiled=True)]
    pallas_call x0 -> x3, Pallas kernels: none -> 21.1 us  [the longest x1 13.8 us: last_grads(): pl.pallas_call(last_grads_kernel, grid=(features // STEP,), out_shape=jax...]
    pallas_call x2 -> x1, Pallas kernels: 25.5 us -> 10.5 us  [weight_grads(): pl.pallas_call(partial(grads_kernel, counts), grid=(features // STEP,), o...]
    all_gather x2, waiting for transfers between devices: 68.5 us -> 63 us  [gather_plane(): lax.all_gather(block, PLANE, axis=0, tiled=False)]
    ppermute x30 -> x32, waiting for transfers between devices: 120 us -> 117 us  [trade(): return lax.ppermute(values, axis, SWAP)]
    ppermute x30 -> x32, starting transfers between devices: 35.8 us -> 37.6 us  [trade(): return lax.ppermute(values, axis, SWAP)]
  transfers between devices with their start and end apart: 41 -> 43, of which waited for: 28 -> 27; matrix products, arithmetic and copies ran while one was open for 8% -> 9% of each run, Pallas kernels for 22% -> 26%
where the time goes in v4:
time: 503 us; the launch traced here: 496 us
  waiting for transfers between devices  217 us (43%)
  Pallas kernels  158 us (31%)
  starting transfers between devices  47 us (9%)
  local copies, waits for them, and re-layouts  33 us (7%)
  other arithmetic  24.5 us (5%)
  between operations  15.8 us (3%)
    ppermute x32, waiting for transfers between devices, trade(): return lax.ppermute(values, axis, SWAP)  117 us
    all_gather x2, waiting for transfers between devices, gather_plane(): lax.all_gather(block, PLANE, axis=0, tiled=False)  63 us
    ppermute x32, starting transfers between devices, trade(): return lax.ppermute(values, axis, SWAP)  37.6 us
    reduce_scatter x1, waiting for transfers between devices, shards(): lax.psum_scatter(last_grad, PLANE, scatter_dimension=0, tiled=True)  21.7 us
    pallas_call x3, Pallas kernels, half_back(): pl.pallas_call(half_back_kernel, grid=(features // tile,), out_shape=[jax...  21 us
    pallas_call x1, Pallas kernels, mixer_backward(): pl.pallas_call(mixer_backward_kernel, out_shape=outs, in_specs=[SMEM] + v...  18.5 us
    pallas_call x2, Pallas kernels, act_back(): pl.pallas_call(act_back_kernel, grid=(count,), out_shape=[jax.ShapeDtypeS...  16.4 us
    ppermute x7, waiting for transfers between devices, sum_over(): lax.ppermute(values, axis, [(i, i ^ step) for i in range(size)])  15.3 us
  transfers between devices with their start and end apart: 43, of which 27 were waited for; matrix products, arithmetic and copies ran while one was open for 9% of the time, Pallas kernels for 26%

profile of v4, /device:TPU:0, one launch (start us, length us, event | category | flops | bytes accessed | tf_op | source)
XLA Modules:
  0.0 495.7 jit_solution(9599592180903688436)
XLA Ops:
  12.4 5.1 %collective-permute-done.1.refs_3_ = bf16[64,128]{1,0:T(8,128)(2,1)S(1)} collective-permute-done((bf16[64,128]{1,0:T(8,128)(2,1)S(1)}, bf16[64,128]{1,0:T(8,128)(2,1)S(1)}, u32[]{:S(2)}, u32[]{:S(2)}) %collective-permute-start.1) | collective-permute-done | bytes 16416 | tf_op jit(solution)/shard_map/ppermute | solution.py:1022
  23.6 8.6 %collective-permute-done.12.refs_1_ = bf16[64,3200]{1,0:T(8,128)(2,1)S(1)} collective-permute-done((bf16[64,3200]{1,0:T(8,128)(2,1)S(1)}, bf16[64,3200]{1,0:T(8,128)(2,1)S(1)}, u32[]{:S(2)}, u32[]{:S(2)}) %collective-permute-start.12) | collective-permute-done | bytes 409632 | tf_op jit(solution)/shard_map/ppermute | solution.py:1022
  41.5 8.6 %collective-permute-done.3.x2 = bf16[128,2048]{1,0:T(8,128)(2,1)S(1)} collective-permute-done((bf16[128,2048]{1,0:T(8,128)(2,1)S(1)}, bf16[128,2048]{1,0:T(8,128)(2,1)S(1)}, u32[]{:S(2)}, u32[]{:S(2)}) %collective-permute-start.3) | collective-permute-done | bytes 524320 | tf_op jit(solution)/shard_map/ppermute | solution.py:1022
  52.1 54.4 %all-gather.5.cloned.1.call-done.small.weights = bf16[2048,2688]{1,0:T(8,128)(2,1)} async-done(((bf16[128,2688]{1,0:T(8,128)(2,1)}), bf16[2048,2688]{1,0:T(8,128)(2,1)}) %all-gather.5.cloned.1.call-update) | async-done | bytes 11010064 | tf_op jit(solution)/shard_map/all_gather | solution.py:1046
  112.7 12.2 %project.1 = (f32[512,1664]{1,0:T(8,128)}, bf16[512,2048]{1,0:T(8,128)(2,1)}, f32[8,2048]{1,0:T(8,128)}) custom-call(s32[4]{0:T(128)} %pad_add_fusion.places, bf16[128,2048]{1,0:T(8,128)(2,1)} %copy-done.1, bf16[128,2048]{1,0:T(8,128)(2,1)} %copy-done.36, bf16[128,2048]{1,0:T(8,128)(2,1)} %copy-done.35, bf16[128,2048]{1,0:T(8,128)(2,1)} %copy-done.37, ...), custom_call_target="tpu_custom_call" | custom-call | flops 12000000000 | bytes 36000000 | tf_op jit(solution)/shard_map/project/pallas_call | solution.py:484
  124.9 12.4 %mixer_forward.1 = (bf16[512,512]{1,0:T(8,128)(2,1)}, f32[512,1024]{1,0:T(8,128)}, f32[8,128,128]{2,1,0:T(8,128)}, f32[8,128,128]{2,1,0:T(8,128)}, f32[8,128,128...) custom-call(s32[2]{0:T(128)} %bitcast.108, ...), custom_call_target="tpu_custom_call" | custom-call | flops 12499999744 | bytes 37500000 | tf_op jit(solution)/shard_map/mixer_forward/pallas_call | solution.py:406
  137.4 10.0 %collective-permute-done.5.early = bf16[1024,768]{1,0:T(8,128)(2,1)S(1)} collective-permute-done((bf16[1024,768]{1,0:T(8,128)(2,1)S(1)}, bf16[1024,768]{1,0:T(8,128)(2,1)S(1)}, u32[]{:S(2)}, u32[]{:S(2)}) %collective-permute-start.5) | collective-permute-done | bytes 1572896 | tf_op jit(solution)/shard_map/ppermute | solution.py:1022
  147.4 5.8 %mix_out.1 = (f32[128,2048]{1,0:T(8,128)}, bf16[128,2048]{1,0:T(8,128)(2,1)}, f32[128,2048]{1,0:T(8,128)}, bf16[128,2048]{1,0:T(8,128)(2,1)}, bf16[512,512]{1,0:T(8,128)(2,1)}) custom-call(s32[4]{0:T(128)} %pad_add_fusion.places, bf16[512,512]{1,0:T(8,128)(2,1)} %get-tuple-element.114.gated, bf16[2048,2688]{1,0:T(8,128)(2,1)} %all-gather.5.cloned.1.call-done.small.weights), custom_call_target="tpu_custom_call" | custom-call | flops 5000000000 | bytes 15000000 | tf_op jit(solution)/shard_map/mix_out/pallas_call | solution.py:533
  161.1 11.6 %collective-permute-done.8 = bf16[128,2048]{1,0:T(8,128)(2,1)S(1)} collective-permute-done((bf16[128,2048]{1,0:T(8,128)(2,1)S(1)}, bf16[128,2048]{1,0:T(8,128)(2,1)S(1)}, u32[]{:S(2)}, u32[]{:S(2)}) %collective-permute-start.8) | collective-permute-done | bytes 524320 | tf_op jit(solution)/shard_map/ppermute | solution.py:1022
  176.3 11.7 %collective-permute-done.10.x2 = bf16[128,2048]{1,0:T(8,128)(2,1)S(1)} collective-permute-done((bf16[128,2048]{1,0:T(8,128)(2,1)S(1)}, bf16[128,2048]{1,0:T(8,128)(2,1)S(1)}, u32[]{:S(2)}, u32[]{:S(2)}) %collective-permute-start.10) | collective-permute-done | bytes 524320 | tf_op jit(solution)/shard_map/ppermute | solution.py:1022
  192.3 8.6 %all-gather.7.cloned.1.call-done.weights.refs_0_.refs_1_.refs_2_ = bf16[2048,3200]{1,0:T(8,128)(2,1)} async-done(((bf16[128,3200]{1,0:T(8,128)(2,1)}), bf16[2048,3200]{1,0:T(8,128)(2,1)}) %all-gather.7.cloned.1.call-update) | async-done | bytes 13107216 | tf_op jit(solution)/shard_map/all_gather | solution.py:1046
  200.9 12.8 %gate_up.1 = (bf16[512,1408]{1,0:T(8,128)(2,1)}, f32[512,1408]{1,0:T(8,128)}, f32[512,1408]{1,0:T(8,128)}, bf16[512,2048]{1,0:T(8,128)(2,1)}) custom-call(bf16[128,2048]{1,0:T(8,128)(2,1)} %copy-done.18, bf16[128,2048]{1,0:T(8,128)(2,1)} %copy-done.41, bf16[128,2048]{1,0:T(8,128)(2,1)} %copy-done.39, bf16[128,2048]{1,0:T(8,128)(2,1)} %copy-done.44, ...), custom_call_target="tpu_custom_call" | custom-call | flops 12499999744 | bytes 37500000 | tf_op jit(solution)/shard_map/gate_up/pallas_call | solution.py:572
  214.6 6.3 %down_first.1 = (f32[128,2048]{1,0:T(8,128)}, bf16[128,2048]{1,0:T(8,128)(2,1)}, bf16[2048,1408]{1,0:T(8,128)(2,1)}) custom-call(bf16[512,1408]{1,0:T(8,128)(2,1)} %get-tuple-element.129.left.right_a.right_b.act, bf16[1024,1024]{1,0:T(8,128)(2,1)} %bitcast.66, bf16[1024,768]{1,0:T(8,128)(2,1)} %copy-done.10, bf16[1024,256]{1,0:T(8,128)(2,1)} %copy-done.13, ...), custom_call_target="tpu_custom_call" | custom-call | flops 6000000000 | bytes 18000000 | tf_op jit(solution)/shard_map/down_first/pallas_call | solution.py:647
  228.1 4.9 down_near.1
  234.9 6.1 %collective-permute-done.16 = bf16[128,2048]{1,0:T(8,128)(2,1)} collective-permute-done((bf16[128,2048]{1,0:T(8,128)(2,1)}, bf16[128,2048]{1,0:T(8,128)(2,1)}, u32[]{:S(2)}, u32[]{:S(2)}) %collective-permute-start.16) | collective-permute-done | bytes 524320 | tf_op jit(solution)/shard_map/ppermute | solution.py:1022
  246.9 8.2 %act_back.2 = (bf16[256,2816]{1,0:T(8,128)(2,1)}, bf16[256,2048]{1,0:T(8,128)(2,1)}) custom-call(bf16[128,2048]{1,0:T(8,128)(2,1)} %copy-done.15, bf16[128,2048]{1,0:T(8,128)(2,1)} %copy-done.45, bf16[2048,1408]{1,0:T(8,128)(2,1)} %get-tuple-element.130.weights, f32[512,1408]{1,0:T(8,128)} %get-tuple-element.135.gate, f32[512,1408]{1,0:T(8,128)} %get-tuple-element.136.up), custom_call_target="tpu_custom_call" | custom-call | flops 8000000000 | bytes 24000000 | tf_op jit(solution)/shard_map/act_back/pallas_call | solution.py:706
  261.7 8.2 %act_back.3 = (bf16[256,2816]{1,0:T(8,128)(2,1)}, bf16[256,2048]{1,0:T(8,128)(2,1)}) custom-call(bf16[128,2048]{1,0:T(8,128)(2,1)} %copy-done.43, bf16[128,2048]{1,0:T(8,128)(2,1)} %copy-done.46, bf16[2048,1408]{1,0:T(8,128)(2,1)} %get-tuple-element.130.weights, f32[512,1408]{1,0:T(8,128)} %get-tuple-element.135.gate, f32[512,1408]{1,0:T(8,128)} %get-tuple-element.136.up), custom_call_target="tpu_custom_call" | custom-call | flops 8000000000 | bytes 24000000 | tf_op jit(solution)/shard_map/act_back/pallas_call | solution.py:706
  269.9 10.5 %units_grads.1 = bf16[2048,2816]{1,0:T(8,128)(2,1)} custom-call(bf16[512,2048]{1,0:T(8,128)(2,1)} %get-tuple-element.134.refs_0_.refs_2_, bf16[256,2816]{1,0:T(8,128)(2,1)} %get-tuple-element.145.refs_1_.left, bf16[512,2048]{1,0:T(8,128)(2,1)} %get-tuple-element.134.refs_0_.refs_2_, bf16[256,2816]{1,0:T(8,128)(2,1)} %get-tuple-element.141.refs_3_.left), custom_call_target="tpu_custom_call" | custom-call | flops 10499999744 | bytes 31500000 | tf_op jit(solution)/shard_map/units_grads/pallas_call | solution.py:842
  280.4 8.0 %normed_far.1 = (f32[128,2048]{1,0:T(8,128)}, bf16[128,2048]{1,0:T(8,128)(2,1)}) custom-call(bf16[256,2816]{1,0:T(8,128)(2,1)} %get-tuple-element.141.refs_3_.left, bf16[2048,3200]{1,0:T(8,128)(2,1)} %all-gather.7.cloned.1.call-done.weights.refs_0_.refs_1_.refs_2_), custom_call_target="tpu_custom_call" | custom-call | flops 8000000000 | bytes 24000000 | tf_op jit(solution)/shard_map/normed_far/pallas_call | solution.py:606
  294.9 8.1 %normed_near.1 = (f32[128,2048]{1,0:T(8,128)}, bf16[128,2048]{1,0:T(8,128)(2,1)}) custom-call(bf16[256,2816]{1,0:T(8,128)(2,1)} %get-tuple-element.145.refs_1_.left, bf16[2048,3200]{1,0:T(8,128)(2,1)} %all-gather.7.cloned.1.call-done.weights.refs_0_.refs_1_.refs_2_), custom_call_target="tpu_custom_call" | custom-call | flops 8000000000 | bytes 24000000 | tf_op jit(solution)/shard_map/normed_near/pallas_call | solution.py:606
  303.0 4.4 collective-permute-done.22
  313.6 11.6 %collective-permute-done.24.x2 = bf16[128,2048]{1,0:T(8,128)(2,1)S(1)} collective-permute-done((bf16[128,2048]{1,0:T(8,128)(2,1)S(1)}, bf16[128,2048]{1,0:T(8,128)(2,1)S(1)}, u32[]{:S(2)}, u32[]{:S(2)}) %collective-permute-start.24) | collective-permute-done | bytes 524320 | tf_op jit(solution)/shard_map/ppermute | solution.py:1022
  325.3 5.1 %down_part.1 = (bf16[1024,512]{1,0:T(8,128)(2,1)}, bf16[1024,512]{1,0:T(8,128)(2,1)}) custom-call(bf16[256,2048]{1,0:T(8,128)(2,1)} %get-tuple-element.149.left_a.near, bf16[512,1408]{1,0:T(8,128)(2,1)} %get-tuple-element.129.left.right_a.right_b.act, bf16[256,2048]{1,0:T(8,128)(2,1)} %get-tuple-element.150.left_b.far, ...), custom_call_target="tpu_custom_call" | custom-call | flops 3000000000 | bytes 9000000 | tf_op jit(solution)/shard_map/down_part/pallas_call | solution.py:917
  332.1 6.9 %gated_back.1 = (f32[512,512]{1,0:T(8,128)}, bf16[512,512]{1,0:T(8,128)(2,1)}, f32[8,256]{1,0:T(8,128)}, bf16[512,2048]{1,0:T(8,128)(2,1)}) custom-call(s32[4]{0:T(128)} %pad_add_fusion.places, bf16[128,2048]{1,0:T(8,128)(2,1)} %copy-done.14, bf16[128,2048]{1,0:T(8,128)(2,1)} %copy-done.40, bf16[128,2048]{1,0:T(8,128)(2,1)} %copy-done.38, ...), custom_call_target="tpu_custom_call" | custom-call | flops 6499999744 | bytes 19500000 | tf_op jit(solution)/shard_map/gated_back/pallas_call | solution.py:760
  339.0 18.5 %mixer_backward.1 = (bf16[512,1152]{1,0:T(8,128)(2,1)}, f32[8,1024]{1,0:T(8,128)}, f32[8,128]{1,0:T(8,128)}) custom-call(s32[2]{0:T(128)} %bitcast.109, f32[512,512]{1,0:T(8,128)} %get-tuple-element.161.grad_mixed, f32[512,1664]{1,0:T(8,128)} %get-tuple-element.111.raw.raw_gate, f32[4,1024]{1,0:T(4,128)} %maximum_convert_fusion.taps, ...), custom_call_target="tpu_custom_call" | custom-call | flops 18499999744 | bytes 55500000 | tf_op jit(solution)/shard_map/mixer_backward/pallas_call | solution.py:423
  358.5 13.8 %last_grads.1 = bf16[2048,3328]{1,0:T(8,128)(2,1)} custom-call(bf16[512,2048]{1,0:T(8,128)(2,1)} %get-tuple-element.158.turned, bf16[512,512]{1,0:T(8,128)(2,1)} %get-tuple-element.159.gated, bf16[512,2048]{1,0:T(8,128)(2,1)} %get-tuple-element.160.normed, bf16[512,512]{1,0:T(8,128)(2,1)} %get-tuple-element.157.gate, ...), custom_call_target="tpu_custom_call" | custom-call | flops 12999999488 | bytes 39000000 | tf_op jit(solution)/shard_map/last_grads/pallas_call | solution.py:958
  372.4 8.6 %input_back.1 = (f32[128,2048]{1,0:T(8,128)}, bf16[128,2048]{1,0:T(8,128)(2,1)}, f32[128,2048]{1,0:T(8,128)}, bf16[128,2048]{1,0:T(8,128)(2,1)}) custom-call(s32[4]{0:T(128)} %pad_add_fusion.places, bf16[512,512]{1,0:T(8,128)(2,1)} %get-tuple-element.157.gate, bf16[512,1152]{1,0:T(8,128)(2,1)} %get-tuple-element.172.conv, ...), custom_call_target="tpu_custom_call" | custom-call | flops 8499999744 | bytes 25500000 | tf_op jit(solution)/shard_map/input_back/pallas_call | solution.py:797
  390.4 10.9 %collective-permute-done.29 = bf16[128,2048]{1,0:T(8,128)(2,1)} collective-permute-done((bf16[128,2048]{1,0:T(8,128)(2,1)}, bf16[128,2048]{1,0:T(8,128)(2,1)}, u32[]{:S(2)}, u32[]{:S(2)}) %collective-permute-start.29) | collective-permute-done | bytes 524320 | tf_op jit(solution)/shard_map/ppermute | solution.py:1022
  420.7 4.4 collective-permute-done.33
  440.8 8.1 %collective-permute-done.38 = bf16[64,2816]{1,0:T(8,128)(2,1)S(1)} collective-permute-done((bf16[64,2816]{1,0:T(8,128)(2,1)S(1)}, bf16[64,2816]{1,0:T(8,128)(2,1)S(1)}, u32[]{:S(2)}, u32[]{:S(2)}) %collective-permute-start.38) | collective-permute-done | bytes 360480 | tf_op jit(solution)/shard_map/ppermute | solution.py:1022
  452.2 21.7 %reduce-scatter.3.cloned.1.call-done.both = bf16[128,3328]{1,0:T(8,128)(2,1)} async-done(((bf16[2048,3328]{1,0:T(8,128)(2,1)}), bf16[128,3328]{1,0:T(8,128)(2,1)}) %reduce-scatter.3.cloned.1.call-update) | async-done | bytes 851984 | tf_op jit(solution)/shard_map/reduce_scatter | solution.py:1227
  477.6 8.1 %collective-permute-done.37.arrived = bf16[64,3072]{1,0:T(8,128)(2,1)S(1)} collective-permute-done((bf16[64,3072]{1,0:T(8,128)(2,1)S(1)}, bf16[64,3072]{1,0:T(8,128)(2,1)S(1)}, u32[]{:S(2)}, u32[]{:S(2)}) %collective-permute-start.37) | collective-permute-done | bytes 393248 | tf_op jit(solution)/shard_map/ppermute | solution.py:1022
  (286 shorter events, 135.8 us)
Async XLA Ops:
  7.2 99.2 %all-gather.5.cloned.1.call-start = ((), (), s32[]{:S(2)}) async-start(), calls=%async_computation.4 | async-start | bytes 11698176 | tf_op jit(solution)/shard_map/all_gather | solution.py:1046
  9.0 8.4 %collective-permute-start = (bf16[64,2048]{1,0:T(8,128)(2,1)}, bf16[64,2048]{1,0:T(8,128)(2,1)S(1)}, u32[]{:S(2)}, u32[]{:S(2)}) collective-permute-start(bf16[64,2048]{1,0:T(8,128)(2,1)} %pack.1.refs_0_), channel_id=1, source_target_pairs={{0,64},{64,0},{1,65},{65,1},{2,66},{66,2},{3,67},{67,3},{4,68},{68... | collective-permute-start | bytes 786440 | tf_op jit(solution)/shard_map/ppermute | solution.py:1022
  11.2 6.3 %collective-permute-start.1 = (bf16[64,128]{1,0:T(8,128)(2,1)S(1)}, bf16[64,128]{1,0:T(8,128)(2,1)S(1)}, u32[]{:S(2)}, u32[]{:S(2)}) collective-permute-start(bf16[64,128]{1,0:T(8,128)(2,1)S(1)} %concatenate.29.refs_2_), channel_id=1, source_target_pairs={{0,64},{64,0},{1,65},{65,1},{2,66},{66,2},{3,67},{67,3},{4,68},{68... | collective-permute-start | bytes 49160 | tf_op jit(solution)/shard_map/ppermute | solution.py:1022
  20.7 180.2 %all-gather.7.cloned.1.call-start = ((), (), s32[]{:S(2)}) async-start(), calls=%async_computation.5 | async-start | bytes 13926400 | tf_op jit(solution)/shard_map/all_gather | solution.py:1046
  21.8 10.4 %collective-permute-start.12 = (bf16[64,3200]{1,0:T(8,128)(2,1)S(1)}, bf16[64,3200]{1,0:T(8,128)(2,1)S(1)}, u32[]{:S(2)}, u32[]{:S(2)}) collective-permute-start(bf16[64,3200]{1,0:T(8,128)(2,1)S(1)} %pad_maximum_fusion.5.refs_0_), channel_id=1, source_target_pairs={{0,64},{64,0},{1,65},{65,1},{2,66},{66,2},{3,67},{67,3},{4,68},{68... | collective-permute-start | bytes 1228808 | tf_op jit(solution)/shard_map/ppermute | solution.py:1022
  35.2 401.5 %reduce-scatter.5.cloned.1.call-start = ((), (), s32[]{:S(2)}) async-start(), calls=%async_computation.3 | async-start | bytes 12255232 | tf_op jit(solution)/shard_map/reduce_scatter | solution.py:1050
  36.7 13.4 %collective-permute-start.3 = (bf16[128,2048]{1,0:T(8,128)(2,1)S(1)}, bf16[128,2048]{1,0:T(8,128)(2,1)S(1)}, u32[]{:S(2)}, u32[]{:S(2)}) collective-permute-start(bf16[128,2048]{1,0:T(8,128)(2,1)S(1)} %copy.62.x0), channel_id=1, source_target_pairs={{0,2},{2,0},{1,3},{3,1},{4,6},{6,4},{5,7},{7,5},{8,10},{10,8},{9,1... | collective-permute-start | bytes 1572872 | tf_op jit(solution)/shard_map/ppermute | solution.py:1022
  40.0 12.0 %collective-permute-start.2 = (bf16[128,2048]{1,0:T(8,128)(2,1)S(1)}, bf16[128,2048]{1,0:T(8,128)(2,1)S(1)}, u32[]{:S(2)}, u32[]{:S(2)}) collective-permute-start(bf16[128,2048]{1,0:T(8,128)(2,1)S(1)} %copy.62.x0), channel_id=1, source_target_pairs={{0,1},{1,0},{2,3},{3,2},{4,5},{5,4},{6,7},{7,6},{8,9},{9,8},{10,11... | collective-permute-start | bytes 1572872 | tf_op jit(solution)/shard_map/ppermute | solution.py:1022
  110.9 36.4 %collective-permute-start.5 = (bf16[1024,768]{1,0:T(8,128)(2,1)S(1)}, bf16[1024,768]{1,0:T(8,128)(2,1)S(1)}, u32[]{:S(2)}, u32[]{:S(2)}) collective-permute-start(bf16[1024,768]{1,0:T(8,128)(2,1)S(1)} %slice.150), channel_id=1, source_target_pairs={{0,64},{64,0},{1,65},{65,1},{2,66},{66,2},{3,67},{67,3},{4,68},{68... | collective-permute-start | bytes 4718600 | tf_op jit(solution)/shard_map/ppermute | solution.py:1022
  153.3 7.8 %collective-permute-start.6 = (bf16[128,2048]{1,0:T(8,128)(2,1)}, bf16[128,2048]{1,0:T(8,128)(2,1)S(1)}, u32[]{:S(2)}, u32[]{:S(2)}) collective-permute-start(bf16[128,2048]{1,0:T(8,128)(2,1)} %get-tuple-element.116), channel_id=1, source_target_pairs={{0,1},{1,0},{2,3},{3,2},{4,5},{5,4},{6,7},{7,6},{8,9},{9,8},{10,11... | collective-permute-start | bytes 1572872 | tf_op jit(solution)/shard_map/ppermute | solution.py:1022
  156.7 16.0 %collective-permute-start.8 = (bf16[128,2048]{1,0:T(8,128)(2,1)S(1)}, bf16[128,2048]{1,0:T(8,128)(2,1)S(1)}, u32[]{:S(2)}, u32[]{:S(2)}) collective-permute-start(bf16[128,2048]{1,0:T(8,128)(2,1)S(1)} %add_convert_fusion.3), channel_id=1, source_target_pairs={{0,2},{2,0},{1,3},{3,1},{4,6},{6,4},{5,7},{7,5},{8,10},{10,8},{9,1... | collective-permute-start | bytes 1572872 | tf_op jit(solution)/shard_map/ppermute | solution.py:1022
  173.3 14.7 %collective-permute-start.10 = (bf16[128,2048]{1,0:T(8,128)(2,1)S(1)}, bf16[128,2048]{1,0:T(8,128)(2,1)S(1)}, u32[]{:S(2)}, u32[]{:S(2)}) collective-permute-start(bf16[128,2048]{1,0:T(8,128)(2,1)S(1)} %multiply_convert_fusion.x0), channel_id=1, source_target_pairs={{0,2},{2,0},{1,3},{3,1},{4,6},{6,4},{5,7},{7,5},{8,10},{10,8},{9,1... | collective-permute-start | bytes 1572872 | tf_op jit(solution)/shard_map/ppermute | solution.py:1022
  176.3 12.6 %collective-permute-start.9 = (bf16[128,2048]{1,0:T(8,128)(2,1)S(1)}, bf16[128,2048]{1,0:T(8,128)(2,1)S(1)}, u32[]{:S(2)}, u32[]{:S(2)}) collective-permute-start(bf16[128,2048]{1,0:T(8,128)(2,1)S(1)} %multiply_convert_fusion.x0), channel_id=1, source_target_pairs={{0,1},{1,0},{2,3},{3,2},{4,5},{5,4},{6,7},{7,6},{8,9},{9,8},{10,11... | collective-permute-start | bytes 1572872 | tf_op jit(solution)/shard_map/ppermute | solution.py:1022
  190.7 23.0 %collective-permute-start.13 = (bf16[1024,256]{1,0:T(8,128)(2,1)}, bf16[1024,256]{1,0:T(8,128)(2,1)S(1)}, u32[]{:S(2)}, u32[]{:S(2)}) collective-permute-start(bf16[1024,256]{1,0:T(8,128)(2,1)} %slice.151), channel_id=1, source_target_pairs={{0,64},{64,0},{1,65},{65,1},{2,66},{66,2},{3,67},{67,3},{4,68},{68... | collective-permute-start | bytes 1572872 | tf_op jit(solution)/shard_map/ppermute | solution.py:1022
  225.1 15.8 %collective-permute-start.16 = (bf16[128,2048]{1,0:T(8,128)(2,1)}, bf16[128,2048]{1,0:T(8,128)(2,1)}, u32[]{:S(2)}, u32[]{:S(2)}) collective-permute-start(bf16[128,2048]{1,0:T(8,128)(2,1)} %add_convert_fusion.2), channel_id=1, source_target_pairs={{0,2},{2,0},{1,3},{3,1},{4,6},{6,4},{5,7},{7,5},{8,10},{10,8},{9,1... | collective-permute-start | bytes 1572872 | tf_op jit(solution)/shard_map/ppermute | solution.py:1022
  233.1 7.9 %collective-permute-start.15 = (bf16[128,2048]{1,0:T(8,128)(2,1)}, bf16[128,2048]{1,0:T(8,128)(2,1)}, u32[]{:S(2)}, u32[]{:S(2)}) collective-permute-start(bf16[128,2048]{1,0:T(8,128)(2,1)} %get-tuple-element.132), channel_id=1, source_target_pairs={{0,1},{1,0},{2,3},{3,2},{4,5},{5,4},{6,7},{7,6},{8,9},{9,8},{10,11... | collective-permute-start | bytes 1572872 | tf_op jit(solution)/shard_map/ppermute | solution.py:1022
  243.0 15.8 %collective-permute-start.17 = (bf16[128,2048]{1,0:T(8,128)(2,1)S(1)}, bf16[128,2048]{1,0:T(8,128)(2,1)S(1)}, u32[]{:S(2)}, u32[]{:S(2)}) collective-permute-start(bf16[128,2048]{1,0:T(8,128)(2,1)S(1)} %get-tuple-element.220.x0), channel_id=1, source_target_pairs={{0,2},{2,0},{1,3},{3,1},{4,6},{6,4},{5,7},{7,5},{8,10},{10,8},{9,1... | collective-permute-start | bytes 1572872 | tf_op jit(solution)/shard_map/ppermute | solution.py:1022
  280.4 193.6 %reduce-scatter.3.cloned.1.call-start = ((), (), s32[]{:S(2)}) async-start(), calls=%async_computation.2 | async-start | bytes 14483456 | tf_op jit(solution)/shard_map/reduce_scatter | solution.py:1227
  291.9 15.5 %collective-permute-start.22 = (bf16[128,2048]{1,0:T(8,128)(2,1)S(1)}, bf16[128,2048]{1,0:T(8,128)(2,1)S(1)}, u32[]{:S(2)}, u32[]{:S(2)}) collective-permute-start(bf16[128,2048]{1,0:T(8,128)(2,1)S(1)} %add_convert_fusion.1), channel_id=1, source_target_pairs={{0,2},{2,0},{1,3},{3,1},{4,6},{6,4},{5,7},{7,5},{8,10},{10,8},{9,1... | collective-permute-start | bytes 1572872 | tf_op jit(solution)/shard_map/ppermute | solution.py:1022
  310.6 14.6 %collective-permute-start.24 = (bf16[128,2048]{1,0:T(8,128)(2,1)S(1)}, bf16[128,2048]{1,0:T(8,128)(2,1)S(1)}, u32[]{:S(2)}, u32[]{:S(2)}) collective-permute-start(bf16[128,2048]{1,0:T(8,128)(2,1)S(1)} %get-tuple-element.152.x0), channel_id=1, source_target_pairs={{0,2},{2,0},{1,3},{3,1},{4,6},{6,4},{5,7},{7,5},{8,10},{10,8},{9,1... | collective-permute-start | bytes 1572872 | tf_op jit(solution)/shard_map/ppermute | solution.py:1022
  313.6 16.7 %collective-permute-start.23 = (bf16[128,2048]{1,0:T(8,128)(2,1)S(1)}, bf16[128,2048]{1,0:T(8,128)(2,1)S(1)}, u32[]{:S(2)}, u32[]{:S(2)}) collective-permute-start(bf16[128,2048]{1,0:T(8,128)(2,1)S(1)} %get-tuple-element.152.x0), channel_id=1, source_target_pairs={{0,1},{1,0},{2,3},{3,2},{4,5},{5,4},{6,7},{7,6},{8,9},{9,8},{10,11... | collective-permute-start | bytes 1572872 | tf_op jit(solution)/shard_map/ppermute | solution.py:1022
  325.3 5.1 %collective-permute-start.25 = (bf16[128,2048]{1,0:T(8,128)(2,1)S(1)}, bf16[128,2048]{1,0:T(8,128)(2,1)S(1)}, u32[]{:S(2)}, u32[]{:S(2)}) collective-permute-start(bf16[128,2048]{1,0:T(8,128)(2,1)S(1)} %collective-permute-done.24.x2), channel_id=1, source_target_pairs={{0,1},{1,0},{2,3},{3,2},{4,5},{5,4},{6,7},{7,6},{8,9},{9,8},{10,11... | collective-permute-start | bytes 1572872 | tf_op jit(solution)/shard_map/ppermute | solution.py:1022
  330.4 27.2 %collective-permute-start.26 = (bf16[1024,512]{1,0:T(8,128)(2,1)}, bf16[1024,512]{1,0:T(8,128)(2,1)S(1)}, u32[]{:S(2)}, u32[]{:S(2)}) collective-permute-start(bf16[1024,512]{1,0:T(8,128)(2,1)} %get-tuple-element.171), channel_id=1, source_target_pairs={{0,64},{64,0},{1,65},{65,1},{2,66},{66,2},{3,67},{67,3},{4,68},{68... | collective-permute-start | bytes 3145736 | tf_op jit(solution)/shard_map/ppermute | solution.py:1022
  381.1 9.3 %collective-permute-start.27 = (bf16[128,2048]{1,0:T(8,128)(2,1)}, bf16[128,2048]{1,0:T(8,128)(2,1)}, u32[]{:S(2)}, u32[]{:S(2)}) collective-permute-start(bf16[128,2048]{1,0:T(8,128)(2,1)} %get-tuple-element.174), channel_id=1, source_target_pairs={{0,1},{1,0},{2,3},{3,2},{4,5},{5,4},{6,7},{7,6},{8,9},{9,8},{10,11... | collective-permute-start | bytes 1572872 | tf_op jit(solution)/shard_map/ppermute | solution.py:1022
  385.4 15.9 %collective-permute-start.29 = (bf16[128,2048]{1,0:T(8,128)(2,1)}, bf16[128,2048]{1,0:T(8,128)(2,1)}, u32[]{:S(2)}, u32[]{:S(2)}) collective-permute-start(bf16[128,2048]{1,0:T(8,128)(2,1)} %add_convert_fusion), channel_id=1, source_target_pairs={{0,2},{2,0},{1,3},{3,1},{4,6},{6,4},{5,7},{7,5},{8,10},{10,8},{9,1... | collective-permute-start | bytes 1572872 | tf_op jit(solution)/shard_map/ppermute | solution.py:1022
  407.9 5.9 %collective-permute-start.31 = (f32[72,128]{1,0:T(8,128)S(1)}, f32[72,128]{1,0:T(8,128)S(1)}, u32[]{:S(2)}, u32[]{:S(2)}) collective-permute-start(f32[72,128]{1,0:T(8,128)S(1)} %fusion.11), channel_id=1, source_target_pairs={{0,16},{16,0},{32,48},{48,32},{1,17},{17,1},{33,49},{49,33},{2,18}... | collective-permute-start | bytes 110600 | tf_op jit(solution)/shard_map/ppermute | solution.py:1080
  413.9 6.3 %collective-permute-start.32 = (f32[72,128]{1,0:T(8,128)S(1)}, f32[72,128]{1,0:T(8,128)S(1)}, u32[]{:S(2)}, u32[]{:S(2)}) collective-permute-start(f32[72,128]{1,0:T(8,128)S(1)} %fusion.17), channel_id=1, source_target_pairs={{0,32},{16,48},{32,0},{48,16},{1,33},{17,49},{33,1},{49,17},{2,34}... | collective-permute-start | bytes 110600 | tf_op jit(solution)/shard_map/ppermute | solution.py:1080
  420.2 5.0 %collective-permute-start.33 = (f32[72,128]{1,0:T(8,128)S(1)}, f32[72,128]{1,0:T(8,128)S(1)}, u32[]{:S(2)}, u32[]{:S(2)}) collective-permute-start(f32[72,128]{1,0:T(8,128)S(1)} %add.167), channel_id=1, source_target_pairs={{0,4},{4,0},{8,12},{12,8},{1,5},{5,1},{9,13},{13,9},{2,6},{6,2},{1... | collective-permute-start | bytes 110600 | tf_op jit(solution)/shard_map/ppermute | solution.py:1080
  425.2 6.1 %collective-permute-start.34 = (f32[72,128]{1,0:T(8,128)S(1)}, f32[72,128]{1,0:T(8,128)S(1)}, u32[]{:S(2)}, u32[]{:S(2)}) collective-permute-start(f32[72,128]{1,0:T(8,128)S(1)} %add.168), channel_id=1, source_target_pairs={{0,8},{4,12},{8,0},{12,4},{1,9},{5,13},{9,1},{13,5},{2,10},{6,14},... | collective-permute-start | bytes 110600 | tf_op jit(solution)/shard_map/ppermute | solution.py:1080
  431.3 5.4 %collective-permute-start.35 = (f32[34,128]{1,0:T(8,128)S(1)}, f32[34,128]{1,0:T(8,128)S(1)}, u32[]{:S(2)}, u32[]{:S(2)}) collective-permute-start(f32[34,128]{1,0:T(8,128)S(1)} %slice.160), channel_id=1, source_target_pairs={{0,2},{2,0},{1,3},{3,1},{4,6},{6,4},{5,7},{7,5},{8,10},{10,8},{9,1... | collective-permute-start | bytes 52232 | tf_op jit(solution)/shard_map/ppermute | solution.py:1080
  437.7 11.2 %collective-permute-start.38 = (bf16[64,2816]{1,0:T(8,128)(2,1)S(1)}, bf16[64,2816]{1,0:T(8,128)(2,1)S(1)}, u32[]{:S(2)}, u32[]{:S(2)}) collective-permute-start(bf16[64,2816]{1,0:T(8,128)(2,1)S(1)} %slice.170), channel_id=1, source_target_pairs={{0,64},{64,0},{1,65},{65,1},{2,66},{66,2},{3,67},{67,3},{4,68},{68... | collective-permute-start | bytes 1081352 | tf_op jit(solution)/shard_map/ppermute | solution.py:1022
  475.0 10.8 %collective-permute-start.37 = (bf16[64,3072]{1,0:T(8,128)(2,1)S(1)}, bf16[64,3072]{1,0:T(8,128)(2,1)S(1)}, u32[]{:S(2)}, u32[]{:S(2)}) collective-permute-start(bf16[64,3072]{1,0:T(8,128)(2,1)S(1)} %slice.161), channel_id=1, source_target_pairs={{0,64},{64,0},{1,65},{65,1},{2,66},{66,2},{3,67},{67,3},{4,68},{68... | collective-permute-start | bytes 1179656 | tf_op jit(solution)/shard_map/ppermute | solution.py:1022
  (67 other events, 687.7 us)
Sparse Core Ops, SparseCore 0:
  20.9 85.5 all-gather.4
  108.6 92.2 all-gather.6
  280.5 91.7 reduce-scatter.4
  376.0 97.8 reduce-scatter.2

commit v5 on v4

--- a/solution.py
+++ b/solution.py
@@ -1202,8 +1202,10 @@
         * jnp.mean(weighted_two * hidden, axis=-1, keepdims=True)
     )
     down_own, down_other = down_part(rows_near, rows_far, act_low)
-    blocks = gather_tokens(grad_hidden.astype(jnp.bfloat16))
-    down_other, *blocks = lax.optimization_barrier((down_other, *blocks))
+    hidden_low = grad_hidden.astype(jnp.bfloat16)
+    across = trade(hidden_low, "xh")
+    across, down_other = lax.optimization_barrier((across, down_other))
+    blocks = (hidden_low, trade(hidden_low, "c"), across, trade(across, "c"))
     down_across = trade(down_other, "xl")
     grad_mixed, gate_low, gain_grad, grad_turned = gated_back(
         places, blocks, mixer_full, raw, mixed, gain_mixer

time: 503 us -> 503 us (level)
    ppermute x32, waiting for transfers between devices: 117 us -> 111 us  [trade(): return lax.ppermute(values, axis, SWAP)]
  transfers between devices with their start and end apart: 43 -> 43, of which waited for: 27 -> 28; matrix products, arithmetic and copies ran while one was open for 9% -> 9% of each run, Pallas kernels for 26% -> 26%
where the time goes in v5:
time: 503 us; the launch traced here: 496 us
  waiting for transfers between devices  213 us (42%)
  Pallas kernels  158 us (31%)
  starting transfers between devices  51.3 us (10%)
  local copies, waits for them, and re-layouts  33.8 us (7%)
  other arithmetic  24.2 us (5%)
  between operations  15.8 us (3%)
    ppermute x32, waiting for transfers between devices, trade(): return lax.ppermute(values, axis, SWAP)  111 us
    all_gather x2, waiting for transfers between devices, gather_plane(): lax.all_gather(block, PLANE, axis=0, tiled=False)  63 us
    ppermute x32, starting transfers between devices, trade(): return lax.ppermute(values, axis, SWAP)  39 us
    reduce_scatter x1, waiting for transfers between devices, shards(): lax.psum_scatter(last_grad, PLANE, scatter_dimension=0, tiled=True)  26.4 us
    pallas_call x3, Pallas kernels, half_back(): pl.pallas_call(half_back_kernel, grid=(features // tile,), out_shape=[jax...  21 us
    pallas_call x1, Pallas kernels, mixer_backward(): pl.pallas_call(mixer_backward_kernel, out_shape=outs, in_specs=[SMEM] + v...  18.7 us
    pallas_call x2, Pallas kernels, act_back(): pl.pallas_call(act_back_kernel, grid=(count,), out_shape=[jax.ShapeDtypeS...  16.4 us
    pallas_call x1, Pallas kernels, last_grads(): pl.pallas_call(last_grads_kernel, grid=(features // STEP,), out_shape=jax...  13.9 us
  transfers between devices with their start and end apart: 43, of which 28 were waited for; matrix products, arithmetic and copies ran while one was open for 9% of the time, Pallas kernels for 26%

profile of v5, /device:TPU:0, one launch (start us, length us, event | category | flops | bytes accessed | tf_op | source)
XLA Modules:
  0.0 496.2 jit_solution(12507391422948579404)
XLA Ops:
  12.4 5.1 %collective-permute-done.1.refs_3_ = bf16[64,128]{1,0:T(8,128)(2,1)S(1)} collective-permute-done((bf16[64,128]{1,0:T(8,128)(2,1)S(1)}, bf16[64,128]{1,0:T(8,128)(2,1)S(1)}, u32[]{:S(2)}, u32[]{:S(2)}) %collective-permute-start.1) | collective-permute-done | bytes 16416 | tf_op jit(solution)/shard_map/ppermute | solution.py:1022
  23.6 8.6 %collective-permute-done.12.refs_1_ = bf16[64,3200]{1,0:T(8,128)(2,1)S(1)} collective-permute-done((bf16[64,3200]{1,0:T(8,128)(2,1)S(1)}, bf16[64,3200]{1,0:T(8,128)(2,1)S(1)}, u32[]{:S(2)}, u32[]{:S(2)}) %collective-permute-start.12) | collective-permute-done | bytes 409632 | tf_op jit(solution)/shard_map/ppermute | solution.py:1022
  41.5 8.6 %collective-permute-done.3.x2 = bf16[128,2048]{1,0:T(8,128)(2,1)S(1)} collective-permute-done((bf16[128,2048]{1,0:T(8,128)(2,1)S(1)}, bf16[128,2048]{1,0:T(8,128)(2,1)S(1)}, u32[]{:S(2)}, u32[]{:S(2)}) %collective-permute-start.3) | collective-permute-done | bytes 524320 | tf_op jit(solution)/shard_map/ppermute | solution.py:1022
  52.1 54.4 %all-gather.5.cloned.1.call-done.small.weights = bf16[2048,2688]{1,0:T(8,128)(2,1)} async-done(((bf16[128,2688]{1,0:T(8,128)(2,1)}), bf16[2048,2688]{1,0:T(8,128)(2,1)}) %all-gather.5.cloned.1.call-update) | async-done | bytes 11010064 | tf_op jit(solution)/shard_map/all_gather | solution.py:1046
  112.7 12.2 %project.1 = (f32[512,1664]{1,0:T(8,128)}, bf16[512,2048]{1,0:T(8,128)(2,1)}, f32[8,2048]{1,0:T(8,128)}) custom-call(s32[4]{0:T(128)} %pad_add_fusion.places, bf16[128,2048]{1,0:T(8,128)(2,1)} %copy-done.1, bf16[128,2048]{1,0:T(8,128)(2,1)} %copy-done.36, bf16[128,2048]{1,0:T(8,128)(2,1)} %copy-done.35, bf16[128,2048]{1,0:T(8,128)(2,1)} %copy-done.37, ...), custom_call_target="tpu_custom_call" | custom-call | flops 12000000000 | bytes 36000000 | tf_op jit(solution)/shard_map/project/pallas_call | solution.py:484
  124.9 12.4 %mixer_forward.1 = (bf16[512,512]{1,0:T(8,128)(2,1)}, f32[512,1024]{1,0:T(8,128)}, f32[8,128,128]{2,1,0:T(8,128)}, f32[8,128,128]{2,1,0:T(8,128)}, f32[8,128,128...) custom-call(s32[2]{0:T(128)} %bitcast.108, ...), custom_call_target="tpu_custom_call" | custom-call | flops 12499999744 | bytes 37500000 | tf_op jit(solution)/shard_map/mixer_forward/pallas_call | solution.py:406
  137.4 10.0 %collective-permute-done.5.early = bf16[1024,768]{1,0:T(8,128)(2,1)S(1)} collective-permute-done((bf16[1024,768]{1,0:T(8,128)(2,1)S(1)}, bf16[1024,768]{1,0:T(8,128)(2,1)S(1)}, u32[]{:S(2)}, u32[]{:S(2)}) %collective-permute-start.5) | collective-permute-done | bytes 1572896 | tf_op jit(solution)/shard_map/ppermute | solution.py:1022
  147.4 5.8 %mix_out.1 = (f32[128,2048]{1,0:T(8,128)}, bf16[128,2048]{1,0:T(8,128)(2,1)}, f32[128,2048]{1,0:T(8,128)}, bf16[128,2048]{1,0:T(8,128)(2,1)}, bf16[512,512]{1,0:T(8,128)(2,1)}) custom-call(s32[4]{0:T(128)} %pad_add_fusion.places, bf16[512,512]{1,0:T(8,128)(2,1)} %get-tuple-element.111.gated, bf16[2048,2688]{1,0:T(8,128)(2,1)} %all-gather.5.cloned.1.call-done.small.weights), custom_call_target="tpu_custom_call" | custom-call | flops 5000000000 | bytes 15000000 | tf_op jit(solution)/shard_map/mix_out/pallas_call | solution.py:533
  161.1 11.6 %collective-permute-done.8 = bf16[128,2048]{1,0:T(8,128)(2,1)S(1)} collective-permute-done((bf16[128,2048]{1,0:T(8,128)(2,1)S(1)}, bf16[128,2048]{1,0:T(8,128)(2,1)S(1)}, u32[]{:S(2)}, u32[]{:S(2)}) %collective-permute-start.8) | collective-permute-done | bytes 524320 | tf_op jit(solution)/shard_map/ppermute | solution.py:1022
  176.3 11.7 %collective-permute-done.10.x2 = bf16[128,2048]{1,0:T(8,128)(2,1)S(1)} collective-permute-done((bf16[128,2048]{1,0:T(8,128)(2,1)S(1)}, bf16[128,2048]{1,0:T(8,128)(2,1)S(1)}, u32[]{:S(2)}, u32[]{:S(2)}) %collective-permute-start.10) | collective-permute-done | bytes 524320 | tf_op jit(solution)/shard_map/ppermute | solution.py:1022
  192.3 8.6 %all-gather.7.cloned.1.call-done.weights.refs_0_.refs_1_.refs_2_ = bf16[2048,3200]{1,0:T(8,128)(2,1)} async-done(((bf16[128,3200]{1,0:T(8,128)(2,1)}), bf16[2048,3200]{1,0:T(8,128)(2,1)}) %all-gather.7.cloned.1.call-update) | async-done | bytes 13107216 | tf_op jit(solution)/shard_map/all_gather | solution.py:1046
  200.9 12.8 %gate_up.1 = (bf16[512,1408]{1,0:T(8,128)(2,1)}, f32[512,1408]{1,0:T(8,128)}, f32[512,1408]{1,0:T(8,128)}, bf16[512,2048]{1,0:T(8,128)(2,1)}) custom-call(bf16[128,2048]{1,0:T(8,128)(2,1)} %copy-done.18, bf16[128,2048]{1,0:T(8,128)(2,1)} %copy-done.40, bf16[128,2048]{1,0:T(8,128)(2,1)} %copy-done.39, bf16[128,2048]{1,0:T(8,128)(2,1)} %copy-done.43, ...), custom_call_target="tpu_custom_call" | custom-call | flops 12499999744 | bytes 37500000 | tf_op jit(solution)/shard_map/gate_up/pallas_call | solution.py:572
  214.6 6.3 %down_first.1 = (f32[128,2048]{1,0:T(8,128)}, bf16[128,2048]{1,0:T(8,128)(2,1)}, bf16[2048,1408]{1,0:T(8,128)(2,1)}) custom-call(bf16[512,1408]{1,0:T(8,128)(2,1)} %get-tuple-element.126.left.right_a.right_b.act, bf16[1024,1024]{1,0:T(8,128)(2,1)} %bitcast.66, bf16[1024,768]{1,0:T(8,128)(2,1)} %copy-done.10, bf16[1024,256]{1,0:T(8,128)(2,1)} %copy-done.13, ...), custom_call_target="tpu_custom_call" | custom-call | flops 6000000000 | bytes 18000000 | tf_op jit(solution)/shard_map/down_first/pallas_call | solution.py:647
  228.1 4.9 down_near.1
  234.9 6.1 %collective-permute-done.16 = bf16[128,2048]{1,0:T(8,128)(2,1)} collective-permute-done((bf16[128,2048]{1,0:T(8,128)(2,1)}, bf16[128,2048]{1,0:T(8,128)(2,1)}, u32[]{:S(2)}, u32[]{:S(2)}) %collective-permute-start.16) | collective-permute-done | bytes 524320 | tf_op jit(solution)/shard_map/ppermute | solution.py:1022
  246.9 8.2 %act_back.2 = (bf16[256,2816]{1,0:T(8,128)(2,1)}, bf16[256,2048]{1,0:T(8,128)(2,1)}) custom-call(bf16[128,2048]{1,0:T(8,128)(2,1)} %copy-done.15, bf16[128,2048]{1,0:T(8,128)(2,1)} %copy-done.45, bf16[2048,1408]{1,0:T(8,128)(2,1)} %get-tuple-element.127.weights, f32[512,1408]{1,0:T(8,128)} %get-tuple-element.132.gate, f32[512,1408]{1,0:T(8,128)} %get-tuple-element.133.up), custom_call_target="tpu_custom_call" | custom-call | flops 8000000000 | bytes 24000000 | tf_op jit(solution)/shard_map/act_back/pallas_call | solution.py:706
  261.7 8.2 %act_back.3 = (bf16[256,2816]{1,0:T(8,128)(2,1)}, bf16[256,2048]{1,0:T(8,128)(2,1)}) custom-call(bf16[128,2048]{1,0:T(8,128)(2,1)} %copy-done.42, bf16[128,2048]{1,0:T(8,128)(2,1)} %copy-done.46, bf16[2048,1408]{1,0:T(8,128)(2,1)} %get-tuple-element.127.weights, f32[512,1408]{1,0:T(8,128)} %get-tuple-element.132.gate, f32[512,1408]{1,0:T(8,128)} %get-tuple-element.133.up), custom_call_target="tpu_custom_call" | custom-call | flops 8000000000 | bytes 24000000 | tf_op jit(solution)/shard_map/act_back/pallas_call | solution.py:706
  269.9 10.5 %units_grads.1 = bf16[2048,2816]{1,0:T(8,128)(2,1)} custom-call(bf16[512,2048]{1,0:T(8,128)(2,1)} %get-tuple-element.131.refs_0_.refs_2_, bf16[256,2816]{1,0:T(8,128)(2,1)} %get-tuple-element.142.refs_1_.left, bf16[512,2048]{1,0:T(8,128)(2,1)} %get-tuple-element.131.refs_0_.refs_2_, bf16[256,2816]{1,0:T(8,128)(2,1)} %get-tuple-element.138.refs_3_.left), custom_call_target="tpu_custom_call" | custom-call | flops 10499999744 | bytes 31500000 | tf_op jit(solution)/shard_map/units_grads/pallas_call | solution.py:842
  280.4 8.0 %normed_far.1 = (f32[128,2048]{1,0:T(8,128)}, bf16[128,2048]{1,0:T(8,128)(2,1)}) custom-call(bf16[256,2816]{1,0:T(8,128)(2,1)} %get-tuple-element.138.refs_3_.left, bf16[2048,3200]{1,0:T(8,128)(2,1)} %all-gather.7.cloned.1.call-done.weights.refs_0_.refs_1_.refs_2_), custom_call_target="tpu_custom_call" | custom-call | flops 8000000000 | bytes 24000000 | tf_op jit(solution)/shard_map/normed_far/pallas_call | solution.py:606
  294.9 8.1 %normed_near.1 = (f32[128,2048]{1,0:T(8,128)}, bf16[128,2048]{1,0:T(8,128)(2,1)}) custom-call(bf16[256,2816]{1,0:T(8,128)(2,1)} %get-tuple-element.142.refs_1_.left, bf16[2048,3200]{1,0:T(8,128)(2,1)} %all-gather.7.cloned.1.call-done.weights.refs_0_.refs_1_.refs_2_), custom_call_target="tpu_custom_call" | custom-call | flops 8000000000 | bytes 24000000 | tf_op jit(solution)/shard_map/normed_near/pallas_call | solution.py:606
  303.0 4.4 collective-permute-done.22
  313.6 4.8 down_part.1
  318.5 6.7 %collective-permute-done.24.x2 = bf16[128,2048]{1,0:T(8,128)(2,1)S(1)} collective-permute-done((bf16[128,2048]{1,0:T(8,128)(2,1)S(1)}, bf16[128,2048]{1,0:T(8,128)(2,1)S(1)}, u32[]{:S(2)}, u32[]{:S(2)}) %collective-permute-start.24) | collective-permute-done | bytes 524320 | tf_op jit(solution)/shard_map/ppermute | solution.py:1022
  328.0 6.6 %gated_back.1 = (f32[512,512]{1,0:T(8,128)}, bf16[512,512]{1,0:T(8,128)(2,1)}, f32[8,256]{1,0:T(8,128)}, bf16[512,2048]{1,0:T(8,128)(2,1)}) custom-call(s32[4]{0:T(128)} %pad_add_fusion.places, bf16[128,2048]{1,0:T(8,128)(2,1)} %copy-done.14, bf16[128,2048]{1,0:T(8,128)(2,1)} %copy-done.41, bf16[128,2048]{1,0:T(8,128)(2,1)} %copy-done.38, ...), custom_call_target="tpu_custom_call" | custom-call | flops 6499999744 | bytes 19500000 | tf_op jit(solution)/shard_map/gated_back/pallas_call | solution.py:760
  334.5 18.7 %mixer_backward.1 = (bf16[512,1152]{1,0:T(8,128)(2,1)}, f32[8,1024]{1,0:T(8,128)}, f32[8,128]{1,0:T(8,128)}) custom-call(s32[2]{0:T(128)} %bitcast.109, f32[512,512]{1,0:T(8,128)} %get-tuple-element.155.grad_mixed, f32[512,1664]{1,0:T(8,128)} %get-tuple-element.108.raw.raw_gate, f32[4,1024]{1,0:T(4,128)} %maximum_convert_fusion.taps, ...), custom_call_target="tpu_custom_call" | custom-call | flops 18499999744 | bytes 55500000 | tf_op jit(solution)/shard_map/mixer_backward/pallas_call | solution.py:423
  354.2 13.9 %last_grads.1 = bf16[2048,3328]{1,0:T(8,128)(2,1)} custom-call(bf16[512,2048]{1,0:T(8,128)(2,1)} %get-tuple-element.152.turned, bf16[512,512]{1,0:T(8,128)(2,1)} %get-tuple-element.153.gated, bf16[512,2048]{1,0:T(8,128)(2,1)} %get-tuple-element.154.normed, bf16[512,512]{1,0:T(8,128)(2,1)} %get-tuple-element.151.gate, ...), custom_call_target="tpu_custom_call" | custom-call | flops 12999999488 | bytes 39000000 | tf_op jit(solution)/shard_map/last_grads/pallas_call | solution.py:958
  368.1 8.6 %input_back.1 = (f32[128,2048]{1,0:T(8,128)}, bf16[128,2048]{1,0:T(8,128)(2,1)}, f32[128,2048]{1,0:T(8,128)}, bf16[128,2048]{1,0:T(8,128)(2,1)}) custom-call(s32[4]{0:T(128)} %pad_add_fusion.places, bf16[512,512]{1,0:T(8,128)(2,1)} %get-tuple-element.151.gate, bf16[512,1152]{1,0:T(8,128)(2,1)} %get-tuple-element.166.conv, ...), custom_call_target="tpu_custom_call" | custom-call | flops 8499999744 | bytes 25500000 | tf_op jit(solution)/shard_map/input_back/pallas_call | solution.py:797
  386.6 10.5 %collective-permute-done.29 = bf16[128,2048]{1,0:T(8,128)(2,1)} collective-permute-done((bf16[128,2048]{1,0:T(8,128)(2,1)}, bf16[128,2048]{1,0:T(8,128)(2,1)}, u32[]{:S(2)}, u32[]{:S(2)}) %collective-permute-start.29) | collective-permute-done | bytes 524320 | tf_op jit(solution)/shard_map/ppermute | solution.py:1022
  416.8 3.8 collective-permute-done.33
  437.7 7.0 %collective-permute-done.38 = bf16[64,2816]{1,0:T(8,128)(2,1)S(1)} collective-permute-done((bf16[64,2816]{1,0:T(8,128)(2,1)S(1)}, bf16[64,2816]{1,0:T(8,128)(2,1)S(1)}, u32[]{:S(2)}, u32[]{:S(2)}) %collective-permute-start.38) | collective-permute-done | bytes 360480 | tf_op jit(solution)/shard_map/ppermute | solution.py:1022
  448.0 26.4 %reduce-scatter.3.cloned.1.call-done.both = bf16[128,3328]{1,0:T(8,128)(2,1)} async-done(((bf16[2048,3328]{1,0:T(8,128)(2,1)}), bf16[128,3328]{1,0:T(8,128)(2,1)}) %reduce-scatter.3.cloned.1.call-update) | async-done | bytes 851984 | tf_op jit(solution)/shard_map/reduce_scatter | solution.py:1229
  478.1 8.1 %collective-permute-done.37.arrived = bf16[64,3072]{1,0:T(8,128)(2,1)S(1)} collective-permute-done((bf16[64,3072]{1,0:T(8,128)(2,1)S(1)}, bf16[64,3072]{1,0:T(8,128)(2,1)S(1)}, u32[]{:S(2)}, u32[]{:S(2)}) %collective-permute-start.37) | collective-permute-done | bytes 393248 | tf_op jit(solution)/shard_map/ppermute | solution.py:1022
  (286 shorter events, 138.9 us)
Async XLA Ops:
  7.2 99.2 %all-gather.5.cloned.1.call-start = ((), (), s32[]{:S(2)}) async-start(), calls=%async_computation.4 | async-start | bytes 11698176 | tf_op jit(solution)/shard_map/all_gather | solution.py:1046
  9.0 8.4 %collective-permute-start = (bf16[64,2048]{1,0:T(8,128)(2,1)}, bf16[64,2048]{1,0:T(8,128)(2,1)S(1)}, u32[]{:S(2)}, u32[]{:S(2)}) collective-permute-start(bf16[64,2048]{1,0:T(8,128)(2,1)} %pack.1.refs_0_), channel_id=1, source_target_pairs={{0,64},{64,0},{1,65},{65,1},{2,66},{66,2},{3,67},{67,3},{4,68},{68... | collective-permute-start | bytes 786440 | tf_op jit(solution)/shard_map/ppermute | solution.py:1022
  11.2 6.3 %collective-permute-start.1 = (bf16[64,128]{1,0:T(8,128)(2,1)S(1)}, bf16[64,128]{1,0:T(8,128)(2,1)S(1)}, u32[]{:S(2)}, u32[]{:S(2)}) collective-permute-start(bf16[64,128]{1,0:T(8,128)(2,1)S(1)} %concatenate.29.refs_2_), channel_id=1, source_target_pairs={{0,64},{64,0},{1,65},{65,1},{2,66},{66,2},{3,67},{67,3},{4,68},{68... | collective-permute-start | bytes 49160 | tf_op jit(solution)/shard_map/ppermute | solution.py:1022
  20.7 180.2 %all-gather.7.cloned.1.call-start = ((), (), s32[]{:S(2)}) async-start(), calls=%async_computation.5 | async-start | bytes 13926400 | tf_op jit(solution)/shard_map/all_gather | solution.py:1046
  21.8 10.4 %collective-permute-start.12 = (bf16[64,3200]{1,0:T(8,128)(2,1)S(1)}, bf16[64,3200]{1,0:T(8,128)(2,1)S(1)}, u32[]{:S(2)}, u32[]{:S(2)}) collective-permute-start(bf16[64,3200]{1,0:T(8,128)(2,1)S(1)} %pad_maximum_fusion.5.refs_0_), channel_id=1, source_target_pairs={{0,64},{64,0},{1,65},{65,1},{2,66},{66,2},{3,67},{67,3},{4,68},{68... | collective-permute-start | bytes 1228808 | tf_op jit(solution)/shard_map/ppermute | solution.py:1022
  35.2 397.3 %reduce-scatter.5.cloned.1.call-start = ((), (), s32[]{:S(2)}) async-start(), calls=%async_computation.3 | async-start | bytes 12255232 | tf_op jit(solution)/shard_map/reduce_scatter | solution.py:1050
  36.7 13.4 %collective-permute-start.3 = (bf16[128,2048]{1,0:T(8,128)(2,1)S(1)}, bf16[128,2048]{1,0:T(8,128)(2,1)S(1)}, u32[]{:S(2)}, u32[]{:S(2)}) collective-permute-start(bf16[128,2048]{1,0:T(8,128)(2,1)S(1)} %copy.62.x0), channel_id=1, source_target_pairs={{0,2},{2,0},{1,3},{3,1},{4,6},{6,4},{5,7},{7,5},{8,10},{10,8},{9,1... | collective-permute-start | bytes 1572872 | tf_op jit(solution)/shard_map/ppermute | solution.py:1022
  40.0 12.0 %collective-permute-start.2 = (bf16[128,2048]{1,0:T(8,128)(2,1)S(1)}, bf16[128,2048]{1,0:T(8,128)(2,1)S(1)}, u32[]{:S(2)}, u32[]{:S(2)}) collective-permute-start(bf16[128,2048]{1,0:T(8,128)(2,1)S(1)} %copy.62.x0), channel_id=1, source_target_pairs={{0,1},{1,0},{2,3},{3,2},{4,5},{5,4},{6,7},{7,6},{8,9},{9,8},{10,11... | collective-permute-start | bytes 1572872 | tf_op jit(solution)/shard_map/ppermute | solution.py:1022
  110.9 36.4 %collective-permute-start.5 = (bf16[1024,768]{1,0:T(8,128)(2,1)S(1)}, bf16[1024,768]{1,0:T(8,128)(2,1)S(1)}, u32[]{:S(2)}, u32[]{:S(2)}) collective-permute-start(bf16[1024,768]{1,0:T(8,128)(2,1)S(1)} %slice.150), channel_id=1, source_target_pairs={{0,64},{64,0},{1,65},{65,1},{2,66},{66,2},{3,67},{67,3},{4,68},{68... | collective-permute-start | bytes 4718600 | tf_op jit(solution)/shard_map/ppermute | solution.py:1022
  153.3 7.8 %collective-permute-start.6 = (bf16[128,2048]{1,0:T(8,128)(2,1)}, bf16[128,2048]{1,0:T(8,128)(2,1)S(1)}, u32[]{:S(2)}, u32[]{:S(2)}) collective-permute-start(bf16[128,2048]{1,0:T(8,128)(2,1)} %get-tuple-element.113), channel_id=1, source_target_pairs={{0,1},{1,0},{2,3},{3,2},{4,5},{5,4},{6,7},{7,6},{8,9},{9,8},{10,11... | collective-permute-start | bytes 1572872 | tf_op jit(solution)/shard_map/ppermute | solution.py:1022
  156.7 16.0 %collective-permute-start.8 = (bf16[128,2048]{1,0:T(8,128)(2,1)S(1)}, bf16[128,2048]{1,0:T(8,128)(2,1)S(1)}, u32[]{:S(2)}, u32[]{:S(2)}) collective-permute-start(bf16[128,2048]{1,0:T(8,128)(2,1)S(1)} %add_convert_fusion.3), channel_id=1, source_target_pairs={{0,2},{2,0},{1,3},{3,1},{4,6},{6,4},{5,7},{7,5},{8,10},{10,8},{9,1... | collective-permute-start | bytes 1572872 | tf_op jit(solution)/shard_map/ppermute | solution.py:1022
  173.3 14.7 %collective-permute-start.10 = (bf16[128,2048]{1,0:T(8,128)(2,1)S(1)}, bf16[128,2048]{1,0:T(8,128)(2,1)S(1)}, u32[]{:S(2)}, u32[]{:S(2)}) collective-permute-start(bf16[128,2048]{1,0:T(8,128)(2,1)S(1)} %multiply_convert_fusion.x0), channel_id=1, source_target_pairs={{0,2},{2,0},{1,3},{3,1},{4,6},{6,4},{5,7},{7,5},{8,10},{10,8},{9,1... | collective-permute-start | bytes 1572872 | tf_op jit(solution)/shard_map/ppermute | solution.py:1022
  176.3 12.6 %collective-permute-start.9 = (bf16[128,2048]{1,0:T(8,128)(2,1)S(1)}, bf16[128,2048]{1,0:T(8,128)(2,1)S(1)}, u32[]{:S(2)}, u32[]{:S(2)}) collective-permute-start(bf16[128,2048]{1,0:T(8,128)(2,1)S(1)} %multiply_convert_fusion.x0), channel_id=1, source_target_pairs={{0,1},{1,0},{2,3},{3,2},{4,5},{5,4},{6,7},{7,6},{8,9},{9,8},{10,11... | collective-permute-start | bytes 1572872 | tf_op jit(solution)/shard_map/ppermute | solution.py:1022
  190.7 23.0 %collective-permute-start.13 = (bf16[1024,256]{1,0:T(8,128)(2,1)}, bf16[1024,256]{1,0:T(8,128)(2,1)S(1)}, u32[]{:S(2)}, u32[]{:S(2)}) collective-permute-start(bf16[1024,256]{1,0:T(8,128)(2,1)} %slice.151), channel_id=1, source_target_pairs={{0,64},{64,0},{1,65},{65,1},{2,66},{66,2},{3,67},{67,3},{4,68},{68... | collective-permute-start | bytes 1572872 | tf_op jit(solution)/shard_map/ppermute | solution.py:1022
  225.1 15.8 %collective-permute-start.16 = (bf16[128,2048]{1,0:T(8,128)(2,1)}, bf16[128,2048]{1,0:T(8,128)(2,1)}, u32[]{:S(2)}, u32[]{:S(2)}) collective-permute-start(bf16[128,2048]{1,0:T(8,128)(2,1)} %add_convert_fusion.2), channel_id=1, source_target_pairs={{0,2},{2,0},{1,3},{3,1},{4,6},{6,4},{5,7},{7,5},{8,10},{10,8},{9,1... | collective-permute-start | bytes 1572872 | tf_op jit(solution)/shard_map/ppermute | solution.py:1022
  233.1 7.9 %collective-permute-start.15 = (bf16[128,2048]{1,0:T(8,128)(2,1)}, bf16[128,2048]{1,0:T(8,128)(2,1)}, u32[]{:S(2)}, u32[]{:S(2)}) collective-permute-start(bf16[128,2048]{1,0:T(8,128)(2,1)} %get-tuple-element.129), channel_id=1, source_target_pairs={{0,1},{1,0},{2,3},{3,2},{4,5},{5,4},{6,7},{7,6},{8,9},{9,8},{10,11... | collective-permute-start | bytes 1572872 | tf_op jit(solution)/shard_map/ppermute | solution.py:1022
  243.0 15.8 %collective-permute-start.17 = (bf16[128,2048]{1,0:T(8,128)(2,1)S(1)}, bf16[128,2048]{1,0:T(8,128)(2,1)S(1)}, u32[]{:S(2)}, u32[]{:S(2)}) collective-permute-start(bf16[128,2048]{1,0:T(8,128)(2,1)S(1)} %get-tuple-element.214.x0), channel_id=1, source_target_pairs={{0,2},{2,0},{1,3},{3,1},{4,6},{6,4},{5,7},{7,5},{8,10},{10,8},{9,1... | collective-permute-start | bytes 1572872 | tf_op jit(solution)/shard_map/ppermute | solution.py:1022
  280.4 194.1 %reduce-scatter.3.cloned.1.call-start = ((), (), s32[]{:S(2)}) async-start(), calls=%async_computation.2 | async-start | bytes 14483456 | tf_op jit(solution)/shard_map/reduce_scatter | solution.py:1229
  291.9 15.5 %collective-permute-start.22 = (bf16[128,2048]{1,0:T(8,128)(2,1)S(1)}, bf16[128,2048]{1,0:T(8,128)(2,1)S(1)}, u32[]{:S(2)}, u32[]{:S(2)}) collective-permute-start(bf16[128,2048]{1,0:T(8,128)(2,1)S(1)} %add_convert_fusion.1), channel_id=1, source_target_pairs={{0,2},{2,0},{1,3},{3,1},{4,6},{6,4},{5,7},{7,5},{8,10},{10,8},{9,1... | collective-permute-start | bytes 1572872 | tf_op jit(solution)/shard_map/ppermute | solution.py:1022
  303.0 4.4 collective-permute-start.21
  310.6 14.6 %collective-permute-start.24 = (bf16[128,2048]{1,0:T(8,128)(2,1)S(1)}, bf16[128,2048]{1,0:T(8,128)(2,1)S(1)}, u32[]{:S(2)}, u32[]{:S(2)}) collective-permute-start(bf16[128,2048]{1,0:T(8,128)(2,1)S(1)} %get-tuple-element.212.x0), channel_id=1, source_target_pairs={{0,2},{2,0},{1,3},{3,1},{4,6},{6,4},{5,7},{7,5},{8,10},{10,8},{9,1... | collective-permute-start | bytes 1572872 | tf_op jit(solution)/shard_map/ppermute | solution.py:1022
  318.5 8.5 %collective-permute-start.23 = (bf16[128,2048]{1,0:T(8,128)(2,1)S(1)}, bf16[128,2048]{1,0:T(8,128)(2,1)S(1)}, u32[]{:S(2)}, u32[]{:S(2)}) collective-permute-start(bf16[128,2048]{1,0:T(8,128)(2,1)S(1)} %get-tuple-element.212.x0), channel_id=1, source_target_pairs={{0,1},{1,0},{2,3},{3,2},{4,5},{5,4},{6,7},{7,6},{8,9},{9,8},{10,11... | collective-permute-start | bytes 1572872 | tf_op jit(solution)/shard_map/ppermute | solution.py:1022
  325.3 27.9 %collective-permute-start.26 = (bf16[1024,512]{1,0:T(8,128)(2,1)}, bf16[1024,512]{1,0:T(8,128)(2,1)S(1)}, u32[]{:S(2)}, u32[]{:S(2)}) collective-permute-start(bf16[1024,512]{1,0:T(8,128)(2,1)} %get-tuple-element.165), channel_id=1, source_target_pairs={{0,64},{64,0},{1,65},{65,1},{2,66},{66,2},{3,67},{67,3},{4,68},{68... | collective-permute-start | bytes 3145736 | tf_op jit(solution)/shard_map/ppermute | solution.py:1022
  377.1 9.5 %collective-permute-start.27 = (bf16[128,2048]{1,0:T(8,128)(2,1)}, bf16[128,2048]{1,0:T(8,128)(2,1)}, u32[]{:S(2)}, u32[]{:S(2)}) collective-permute-start(bf16[128,2048]{1,0:T(8,128)(2,1)} %get-tuple-element.168), channel_id=1, source_target_pairs={{0,1},{1,0},{2,3},{3,2},{4,5},{5,4},{6,7},{7,6},{8,9},{9,8},{10,11... | collective-permute-start | bytes 1572872 | tf_op jit(solution)/shard_map/ppermute | solution.py:1022
  381.1 15.9 %collective-permute-start.29 = (bf16[128,2048]{1,0:T(8,128)(2,1)}, bf16[128,2048]{1,0:T(8,128)(2,1)}, u32[]{:S(2)}, u32[]{:S(2)}) collective-permute-start(bf16[128,2048]{1,0:T(8,128)(2,1)} %add_convert_fusion), channel_id=1, source_target_pairs={{0,2},{2,0},{1,3},{3,1},{4,6},{6,4},{5,7},{7,5},{8,10},{10,8},{9,1... | collective-permute-start | bytes 1572872 | tf_op jit(solution)/shard_map/ppermute | solution.py:1022
  403.5 6.2 %collective-permute-start.31 = (f32[72,128]{1,0:T(8,128)S(1)}, f32[72,128]{1,0:T(8,128)S(1)}, u32[]{:S(2)}, u32[]{:S(2)}) collective-permute-start(f32[72,128]{1,0:T(8,128)S(1)} %fusion.11), channel_id=1, source_target_pairs={{0,16},{16,0},{32,48},{48,32},{1,17},{17,1},{33,49},{49,33},{2,18}... | collective-permute-start | bytes 110600 | tf_op jit(solution)/shard_map/ppermute | solution.py:1080
  409.7 6.5 %collective-permute-start.32 = (f32[72,128]{1,0:T(8,128)S(1)}, f32[72,128]{1,0:T(8,128)S(1)}, u32[]{:S(2)}, u32[]{:S(2)}) collective-permute-start(f32[72,128]{1,0:T(8,128)S(1)} %fusion.17), channel_id=1, source_target_pairs={{0,32},{16,48},{32,0},{48,16},{1,33},{17,49},{33,1},{49,17},{2,34}... | collective-permute-start | bytes 110600 | tf_op jit(solution)/shard_map/ppermute | solution.py:1080
  416.2 4.4 collective-permute-start.33
  420.6 6.4 %collective-permute-start.34 = (f32[72,128]{1,0:T(8,128)S(1)}, f32[72,128]{1,0:T(8,128)S(1)}, u32[]{:S(2)}, u32[]{:S(2)}) collective-permute-start(f32[72,128]{1,0:T(8,128)S(1)} %add.168), channel_id=1, source_target_pairs={{0,8},{4,12},{8,0},{12,4},{1,9},{5,13},{9,1},{13,5},{2,10},{6,14},... | collective-permute-start | bytes 110600 | tf_op jit(solution)/shard_map/ppermute | solution.py:1080
  427.1 5.4 %collective-permute-start.35 = (f32[34,128]{1,0:T(8,128)S(1)}, f32[34,128]{1,0:T(8,128)S(1)}, u32[]{:S(2)}, u32[]{:S(2)}) collective-permute-start(f32[34,128]{1,0:T(8,128)S(1)} %slice.160), channel_id=1, source_target_pairs={{0,2},{2,0},{1,3},{3,1},{4,6},{6,4},{5,7},{7,5},{8,10},{10,8},{9,1... | collective-permute-start | bytes 52232 | tf_op jit(solution)/shard_map/ppermute | solution.py:1080
  433.6 11.1 %collective-permute-start.38 = (bf16[64,2816]{1,0:T(8,128)(2,1)S(1)}, bf16[64,2816]{1,0:T(8,128)(2,1)S(1)}, u32[]{:S(2)}, u32[]{:S(2)}) collective-permute-start(bf16[64,2816]{1,0:T(8,128)(2,1)S(1)} %slice.170), channel_id=1, source_target_pairs={{0,64},{64,0},{1,65},{65,1},{2,66},{66,2},{3,67},{67,3},{4,68},{68... | collective-permute-start | bytes 1081352 | tf_op jit(solution)/shard_map/ppermute | solution.py:1022
  475.5 10.8 %collective-permute-start.37 = (bf16[64,3072]{1,0:T(8,128)(2,1)S(1)}, bf16[64,3072]{1,0:T(8,128)(2,1)S(1)}, u32[]{:S(2)}, u32[]{:S(2)}) collective-permute-start(bf16[64,3072]{1,0:T(8,128)(2,1)S(1)} %slice.161), channel_id=1, source_target_pairs={{0,64},{64,0},{1,65},{65,1},{2,66},{66,2},{3,67},{67,3},{4,68},{68... | collective-permute-start | bytes 1179656 | tf_op jit(solution)/shard_map/ppermute | solution.py:1022
  (67 other events, 670.1 us)
Sparse Core Ops, SparseCore 0:
  20.9 85.5 all-gather.4
  108.6 92.2 all-gather.6
  280.5 91.6 reduce-scatter.4
  375.9 98.5 reduce-scatter.2
